TPU v7x, 32 devices: a whole 2x2x4 slice. The times are simulated.
32 devices in a mesh: pool: 8 (over z, x), tp: 4 (over y, core).
Axes of the slice: x: 2, y: 2, z: 4, core: 2. Of those that a mesh axis runs over, the one named last changes fastest.
Arguments:
- activations: bfloat16 [2, 256, 8192], P(None, None, 'tp'), may hold values from -6 to 6
- gate_matrix: bfloat16 [8192, 28672], P('tp', 'pool'), may hold values from -0.0625 to 0.0625
- up_weight: bfloat16 [8192, 28672], P('tp', 'pool'), may hold values from -0.0625 to 0.0625
- down_matrix: bfloat16 [28672, 8192], P('pool', 'tp'), may hold values from -0.03125 to 0.03125
- shrink_pages: bfloat16 [32, 64, 8192], P('pool', None, 'tp'), may hold values from -0.0625 to 0.0625
- expand_pages: bfloat16 [32, 64, 28672], P('pool', 'tp'), may hold values from -0.75 to 0.75
- row_adapter: int32 [2, 256], replicated, may hold values from 0 to 31, as said below
- page_table: int32 [32], replicated, may hold values from 0 to 31, as said below
Outputs:
- layer_out: bfloat16 [2, 256, 8192], P(None, None, 'tp')
Inputs may be any that keep to these rules, and one draw needn't show every extreme that they name: `row_adapter`: in each micro-batch, the rows use at most 1 distinct adapter among those whose pages have the same owner, the owner of page g being g // 4 (so a micro-batch may use up to 8 adapters, one per owner). A permutation: adapter a is stored at page page_table[a].
All inputs are finite; a program needn't handle non-finite values.
Results may differ from a plain program's by a relative error of at most 0.0057.
Values may be sent and summed in bfloat16 or wider, within the bound.
No kernel may reach another device: no remote copies, remote signals or barrier semaphores. Data moves between devices by JAX's collectives and lax.ppermute only.
A program may use at most 128 MiB of HBM per device.

v0:
```python
import jax
import jax.numpy as jnp
from jax import lax
from jax.sharding import PartitionSpec as P

CAP = 1


adapter_scale = 2.0


def on_device(
    activations,
    gate_matrix,
    up_weight,
    down_matrix,
    shrink_pages,
    expand_pages,
    row_adapter,
    page_table,
):
    pool_count = lax.axis_size("pool")
    pool_index = lax.axis_index("pool")
    tp_index = lax.axis_index("tp")
    batches, row_count, local_width = activations.shape
    page_count = shrink_pages.shape[0]
    rank_local = expand_pages.shape[1]
    hidden_local = gate_matrix.shape[1]
    adapter_total = page_table.shape[0]
    catalog = jnp.arange(adapter_total, dtype=jnp.int32)
    page_of_row = jnp.sum(jnp.where(row_adapter[:, :, None] == catalog, page_table, 0), axis=2)
    contract_first = (((0,), (0,)), ((), ()))
    contract_cross = (((0,), (1,)), ((), ()))
    groups = [(batch_index, batch_index + 1) for batch_index in range(batches)]
    outputs = []
    for group_start, group_stop in groups:
        group_size = group_stop - group_start
        rows_in = activations[group_start:group_stop].reshape(group_size * row_count, local_width)
        pages_in = page_of_row[group_start:group_stop]
        row_pages = pages_in.reshape(-1)
        row_owner = row_pages // page_count
        row_local = row_pages % page_count
        row_total = group_size * row_count
        projected = jnp.einsum(
            "nd,prd->npr", rows_in, shrink_pages, preferred_element_type=jnp.float32
        )
        owned_here = (row_owner == pool_index)[:, None] & (
            row_local[:, None] == jnp.arange(page_count, dtype=jnp.int32)
        )
        shrink_part = jnp.sum(jnp.where(owned_here[:, :, None], projected, 0.0), axis=1)
        shrink_full = lax.psum(shrink_part, ("pool", "tp"))
        shrink_mine = lax.dynamic_slice_in_dim(
            shrink_full.astype(jnp.bfloat16), tp_index * rank_local, rank_local, 1
        )
        page_used = jnp.any(pages_in[:, :, None] == catalog, axis=1)
        page_order = jnp.cumsum(page_used.astype(jnp.int32), axis=1) - 1
        owner_order = (
            page_order.reshape(group_size, pool_count, page_count)
            - lax.dynamic_index_in_dim(page_order.reshape(group_size, pool_count, page_count), 0, 2)
            + page_used.reshape(group_size, pool_count, page_count)[:, :, :1].astype(jnp.int32)
            - 1
        )
        owned_used = lax.dynamic_index_in_dim(
            page_used.reshape(group_size, pool_count, page_count), pool_index, 1, keepdims=False
        )
        owned_order = lax.dynamic_index_in_dim(owner_order, pool_index, 1, keepdims=False)
        hit_table = owned_used[:, :, None] & (
            owned_order[:, :, None] == jnp.arange(CAP, dtype=jnp.int32)
        )
        chosen = jnp.sum(
            jnp.where(hit_table, jnp.arange(page_count, dtype=jnp.int32)[None, :, None], 0), axis=1
        )
        outgoing = jnp.take(expand_pages, chosen.reshape(-1), axis=0)
        outgoing = outgoing.reshape(group_size * CAP, rank_local, pool_count, hidden_local)
        received = lax.all_to_all(outgoing, "pool", split_axis=2, concat_axis=0, tiled=True)
        blocks_mat = received.reshape(pool_count * group_size * CAP * rank_local, hidden_local)
        slot_total = pool_count * group_size * CAP
        flat_order = owner_order.reshape(group_size, adapter_total)
        row_order = jnp.sum(
            jnp.where(pages_in[:, :, None] == catalog, flat_order[:, None, :], 0), axis=2
        )
        batch_of_row = lax.broadcasted_iota(jnp.int32, (group_size, row_count), 0)
        slot_of_row = (
            (pages_in // page_count * group_size + batch_of_row) * CAP + row_order
        ).reshape(-1)
        onehot = slot_of_row[:, None] == jnp.arange(slot_total, dtype=jnp.int32)
        wide_rows = jnp.where(
            onehot[:, :, None], shrink_mine[:, None, :], jnp.zeros((), jnp.bfloat16)
        )
        wide_rows = wide_rows.reshape(row_total, slot_total * rank_local)
        gate_term = lax.dot_general(
            gate_matrix, rows_in, contract_cross, preferred_element_type=jnp.float32
        )
        up_product = lax.dot_general(
            up_weight, rows_in, contract_cross, preferred_element_type=jnp.float32
        )
        up_product = up_product + adapter_scale * lax.dot_general(
            blocks_mat, wide_rows, contract_cross, preferred_element_type=jnp.float32
        )
        summed = lax.psum_scatter(
            jnp.concatenate([gate_term, up_product], axis=1), "tp", scatter_dimension=0, tiled=True
        )
        hidden_cols = (jax.nn.silu(summed[:, :row_total]) * summed[:, row_total:]).astype(
            jnp.bfloat16
        )
        partial_out = lax.dot_general(
            lax.all_gather(hidden_cols, "tp", axis=0, tiled=True),
            down_matrix,
            contract_first,
            preferred_element_type=jnp.float32,
        )
        out_total = lax.psum(partial_out, "pool")
        outputs.append(out_total.astype(jnp.bfloat16).reshape(group_size, row_count, local_width))
    return jnp.concatenate(outputs, axis=0)


def solution(mesh):
    in_specs = (
        P(None, None, "tp"),
        P("tp", "pool"),
        P("tp", "pool"),
        P("pool", "tp"),
        P("pool", None, "tp"),
        P("pool", "tp", None),
        P(),
        P(),
    )
    out_specs = P(None, None, "tp")
    return jax.shard_map(
        on_device, mesh=mesh, in_specs=in_specs, out_specs=out_specs, check_vma=False
    )
```

profile of v0, /device:TPU:0, one launch (start us, length us, event | category | flops | bytes accessed | tf_op | source)
XLA Modules:
  0.0 464.7 jit_solution(6961429156016451727)
XLA Ops:
  6.5 0.9 select_reduce_fusion
  7.4 0.1 fusion.22
  7.5 0.1 reshape.817
  7.6 0.1 fusion.23
  7.8 0.1 reshape.811
  7.8 0.2 reduce_window_sum.18
  8.2 0.1 slice_reduce_fusion
  8.3 0.1 convert_reduce_fusion
  8.4 0.2 reduce_window_sum.17
  8.7 0.1 slice_reduce_fusion.1
  8.8 0.1 convert_reduce_fusion.1
  9.1 0.6 fusion.40
  13.4 1.6 dynamic-slice_select_fusion.1
  15.0 1.0 copy.20
  16.0 7.3 %all-to-all-start = ((bf16[1,16,8,3584]{3,1,0,2:T(8,128)(2,1)}), bf16[1,16,8,3584]{3,1,0,2:T(8,128)(2,1)S(1)}, u32[]{:S(2)}, u32[]{:S(2)}) async-start(bf16[1,16,8,3584]{3,1,0,2:T(8,128)(2,1)} %bitcast.103), calls=%async_computation | async-start | bytes 1835008 | tf_op jit(solution)/shard_map/all_to_all | solution.py:75
  23.4 1.8 fusion.2
  25.2 0.5 fusion.3
  25.8 0.1 sub.109
  25.9 0.1 add.213
  26.0 0.1 select_reduce_fusion.2
  26.2 0.1 sub.122
  26.3 0.1 add.225
  26.4 0.1 select_reduce_fusion.1
  26.5 11.3 %fusion.12 = f32[3584,256]{0,1:T(8,128)} fusion(bf16[2048,3584]{1,0:T(8,128)(2,1)} %param.12, bf16[2,256,2048]{2,1,0:T(8,128)(2,1)} %param.10), kind=kOutput, calls=%fused_computation.19 | convolution fusion | flops 3758096384 | bytes 19398656 | tf_op jit(solution)/shard_map/dot_general | solution.py:94
  37.8 41.6 %all-reduce.4 = (bf16[256,64]{0,1:T(8,128)(2,1)S(1)}, bf16[256,64]{0,1:T(8,128)(2,1)S(1)}) all-reduce(f32[256,64]{0,1:T(8,128)S(1)} %fusion.3, f32[256,64]{0,1:T(8,128)S(1)} %fusion.2), channel_id=1, replica_groups=mesh['pool'=8,'tp'=4] {'pool','tp'}, use_global_device_ids=true, to_apply=%region_14.16 | all-reduce | flops 32768 | bytes 196608 | tf_op jit(solution)/shard_map/psum | solution.py:51
  79.5 11.3 %fusion.10 = f32[3584,256]{0,1:T(8,128)} fusion(bf16[2048,3584]{1,0:T(8,128)(2,1)} %param.11, bf16[2,256,2048]{2,1,0:T(8,128)(2,1)} %param.10), kind=kOutput, calls=%fused_computation.17 | convolution fusion | flops 3758096384 | bytes 19398656 | tf_op jit(solution)/shard_map/dot_general | solution.py:91
  90.8 2.9 fusion.1
  93.7 0.3 copy-done.2
  94.0 3.4 pad_maximum_fusion
  97.4 1.0 copy.19
  98.4 5.4 %all-to-all-start.1 = ((bf16[1,16,8,3584]{3,1,0,2:T(8,128)(2,1)}), bf16[1,16,8,3584]{3,1,0,2:T(8,128)(2,1)S(1)}, u32[]{:S(2)}, u32[]{:S(2)}) async-start(bf16[1,16,8,3584]{3,1,0,2:T(8,128)(2,1)} %bitcast.102), calls=%async_computation.2 | async-start | bytes 1835008 | tf_op jit(solution)/shard_map/all_to_all | solution.py:75
  103.8 0.2 reduce-scatter.5.cloned.1.call-start
  104.1 13.7 %fusion.7 = f32[3584,256]{0,1:T(8,128)} fusion(bf16[2048,3584]{1,0:T(8,128)(2,1)} %param.12, bf16[2,256,2048]{2,1,0:T(8,128)(2,1)} %param.10), kind=kOutput, calls=%fused_computation.14 | convolution fusion | flops 3758096384 | bytes 19398656 | tf_op jit(solution)/shard_map/dot_general | solution.py:94
  117.9 5.9 %fusion.5 = f32[3584,256]{0,1:T(8,128)} fusion(bf16[2048,3584]{1,0:T(8,128)(2,1)S(1)} %bitcast.125, bf16[2,256,2048]{2,1,0:T(8,128)(2,1)S(1)} %copy-done.5), kind=kOutput, calls=%fused_computation.12 | convolution fusion | flops 3758096384 | bytes 19398656 | tf_op jit(solution)/shard_map/dot_general | solution.py:91
  123.8 1.4 all-to-all-done.1
  125.2 2.9 fusion
  128.1 0.3 copy-done.3
  128.4 3.5 pad_maximum_fusion.1
  131.9 30.9 %reduce-scatter.3.cloned.1.call-done = f32[896,512]{0,1:T(8,128)} async-done(((f32[3584,512]{0,1:T(8,128)}), f32[896,512]{0,1:T(8,128)}) %reduce-scatter.3.cloned.1.call-update) | async-done | bytes 1835024 | tf_op jit(solution)/shard_map/reduce_scatter | solution.py:100
  162.9 2.5 fusion.15
  165.4 65.6 %reduce-scatter.5.cloned.1.call-done = f32[896,512]{0,1:T(8,128)} async-done(((f32[3584,512]{0,1:T(8,128)}), f32[896,512]{0,1:T(8,128)}) %reduce-scatter.5.cloned.1.call-update) | async-done | bytes 1835024 | tf_op jit(solution)/shard_map/reduce_scatter | solution.py:100
  231.0 2.5 fusion.14
  233.6 20.2 %all-gather.3.cloned.1.call-done = bf16[3584,256]{0,1:T(8,128)(2,1)} async-done(((bf16[896,256]{0,1:T(8,128)(2,1)}), bf16[3584,256]{0,1:T(8,128)(2,1)}) %all-gather.3.cloned.1.call-update) | async-done | bytes 1835024 | tf_op jit(solution)/shard_map/all_gather | solution.py:107
  253.8 7.8 %fusion.43 = f32[256,2048]{1,0:T(8,128)S(1)} fusion(bf16[3584,256]{0,1:T(8,128)(2,1)} %all-gather.3.cloned.1.call-done, bf16[3584,2048]{1,0:T(8,128)(2,1)} %param.13), kind=kOutput, calls=%fused_computation.110 | convolution fusion | flops 3758096384 | bytes 18612224 | tf_op jit(solution)/shard_map/dot_general | solution.py:106
  261.6 14.8 %all-gather.5.cloned.1.call-done = bf16[3584,256]{0,1:T(8,128)(2,1)} async-done(((bf16[896,256]{0,1:T(8,128)(2,1)}), bf16[3584,256]{0,1:T(8,128)(2,1)}) %all-gather.5.cloned.1.call-update) | async-done | bytes 1835024 | tf_op jit(solution)/shard_map/all_gather | solution.py:107
  276.4 11.1 %fusion.44 = f32[256,2048]{1,0:T(8,128)} fusion(bf16[3584,256]{0,1:T(8,128)(2,1)} %all-gather.5.cloned.1.call-done, bf16[3584,2048]{1,0:T(8,128)(2,1)} %param.13), kind=kOutput, calls=%fused_computation.111 | convolution fusion | flops 3758096384 | bytes 18612224 | tf_op jit(solution)/shard_map/dot_general | solution.py:106
  287.4 167.7 %all-reduce.5 = (bf16[256,2048]{1,0:T(8,128)(2,1)}, bf16[256,2048]{1,0:T(8,128)(2,1)}) all-reduce(f32[256,2048]{1,0:T(8,128)} %fusion.44, f32[256,2048]{1,0:T(8,128)S(1)} %fusion.43), channel_id=1, replica_groups=mesh['pool'=8,'tp'=4] {'pool'}, use_global_device_ids=true, to_apply=%region_16.18 | all-reduce | flops 1048576 | bytes 6291456 | tf_op jit(solution)/shard_map/psum | solution.py:112
  455.1 3.1 pad_maximum_fusion.2
  (53 shorter events, 1.0 us)
Async XLA Ops:
  6.5 16.8 %copy-start = (bf16[4,64,2048]{2,1,0:T(8,128)(2,1)S(1)}, bf16[4,64,2048]{2,1,0:T(8,128)(2,1)}, u32[]{:S(2)}) copy-start(bf16[4,64,2048]{2,1,0:T(8,128)(2,1)} %param.14) | copy-start | bytes 3145732
  16.0 74.8 %all-to-all-start = ((bf16[1,16,8,3584]{3,1,0,2:T(8,128)(2,1)}), bf16[1,16,8,3584]{3,1,0,2:T(8,128)(2,1)S(1)}, u32[]{:S(2)}, u32[]{:S(2)}) async-start(bf16[1,16,8,3584]{3,1,0,2:T(8,128)(2,1)} %bitcast.103), calls=%async_computation | async-start | bytes 1835008 | tf_op jit(solution)/shard_map/all_to_all | solution.py:75
  23.2 139.6 %reduce-scatter.3.cloned.1.call-start = ((), (), s32[]{:S(2)}) async-start(), calls=%async_computation.4 | async-start | bytes 9175040 | tf_op jit(solution)/shard_map/reduce_scatter | solution.py:100
  23.3 1.9 copy-start.4
  90.8 3.1 copy-start.2
  98.4 19.5 %slice-start = ((s8[14680064]{0:T(1024)(128)(4,1)}), s8[2097152]{0:T(1024)(128)(4,1)S(1)}, s32[]{:S(2)}) async-start(s8[14680064]{0:T(1024)(128)(4,1)} %bitcast.124), calls=%async_computation.8 | async-start | bytes 4194304
  98.4 26.8 %all-to-all-start.1 = ((bf16[1,16,8,3584]{3,1,0,2:T(8,128)(2,1)}), bf16[1,16,8,3584]{3,1,0,2:T(8,128)(2,1)S(1)}, u32[]{:S(2)}, u32[]{:S(2)}) async-start(bf16[1,16,8,3584]{3,1,0,2:T(8,128)(2,1)} %bitcast.102), calls=%async_computation.2 | async-start | bytes 1835008 | tf_op jit(solution)/shard_map/all_to_all | solution.py:75
  103.8 127.2 %reduce-scatter.5.cloned.1.call-start = ((), (), s32[]{:S(2)}) async-start(), calls=%async_computation.6 | async-start | bytes 9175040 | tf_op jit(solution)/shard_map/reduce_scatter | solution.py:100
  104.1 13.8 %slice-start.1 = ((s8[14680064]{0:T(1024)(128)(4,1)}), s8[4194304]{0:T(1024)(128)(4,1)S(1)}, s32[]{:S(2)}) async-start(s8[14680064]{0:T(1024)(128)(4,1)} %bitcast.124), calls=%async_computation.9 | async-start | bytes 8388608
  104.1 13.8 %slice-start.2 = ((s8[14680064]{0:T(1024)(128)(4,1)}), s8[4194304]{0:T(1024)(128)(4,1)S(1)}, s32[]{:S(2)}) async-start(s8[14680064]{0:T(1024)(128)(4,1)} %bitcast.124), calls=%async_computation.10 | async-start | bytes 8388608
  104.1 13.8 %slice-start.3 = ((s8[14680064]{0:T(1024)(128)(4,1)}), s8[4194304]{0:T(1024)(128)(4,1)S(1)}, s32[]{:S(2)}) async-start(s8[14680064]{0:T(1024)(128)(4,1)} %bitcast.124), calls=%async_computation.11 | async-start | bytes 8388608
  104.1 13.8 %copy-start.5 = (bf16[2,256,2048]{2,1,0:T(8,128)(2,1)S(1)}, bf16[2,256,2048]{2,1,0:T(8,128)(2,1)}, u32[]{:S(2)}) copy-start(bf16[2,256,2048]{2,1,0:T(8,128)(2,1)} %param.10) | copy-start | bytes 6291460
  125.2 3.1 copy-start.3
  131.9 121.9 %all-gather.3.cloned.1.call-start = ((), (), s32[]{:S(2)}) async-start(), calls=%async_computation.5 | async-start | bytes 2293760 | tf_op jit(solution)/shard_map/all_gather | solution.py:107
  165.4 111.0 %all-gather.5.cloned.1.call-start = ((), (), s32[]{:S(2)}) async-start(), calls=%async_computation.7 | async-start | bytes 2293760 | tf_op jit(solution)/shard_map/all_gather | solution.py:107
  276.4 181.8 %copy-start.1 = (bf16[4,64,2048]{2,1,0:T(8,128)(2,1)S(1)}, bf16[4,64,2048]{2,1,0:T(8,128)(2,1)}, u32[]{:S(2)}) copy-start(bf16[4,64,2048]{2,1,0:T(8,128)(2,1)} %param.14) | copy-start | bytes 3145732
Sparse Core Ops, SparseCore 0:
  97.5 65.2 reduce-scatter.2
  165.6 65.4 reduce-scatter.4
  232.6 21.1 all-gather.2
  255.2 21.1 all-gather.4
where the time goes:
time: 465 us
  blocking collectives  209 us (45%)
  waiting for transfers between devices  133 us (29%)
  matrix products  69 us (15%)
  other arithmetic  19.5 us (4%)
  between operations  17.1 us (4%)
  starting transfers between devices  13 us (3%)
    psum x1, blocking collectives, on_device(): out_total = lax.psum(partial_out, 'pool')  168 us
    reduce_scatter x2, waiting for transfers between devices, on_device(): lax.psum_scatter(jnp.concatenate([gate_term, up_product], axis=1), 'tp',...  96.5 us
    psum x1, blocking collectives, on_device(): shrink_full = lax.psum(shrink_part, ('pool', 'tp'))  41.6 us
    all_gather x2, waiting for transfers between devices, on_device(): lax.all_gather(hidden_cols, 'tp', axis=0, tiled=True)  35 us
    dot_general x2, matrix products, on_device(): lax.dot_general(up_weight, rows_in, contract_cross, preferred_element_typ...  25 us
    dot_general x2, matrix products, on_device(): lax.dot_general(lax.all_gather(hidden_cols, 'tp', axis=0, tiled=True), do...  18.8 us
    dot_general x2, matrix products, on_device(): lax.dot_general(gate_matrix, rows_in, contract_cross, preferred_element_t...  17.2 us
    all_to_all x2, starting transfers between devices, on_device(): lax.all_to_all(outgoing, 'pool', split_axis=2, concat_axis=0, tiled=True)  12.7 us
  transfers between devices with their start and end apart: 6, of which 5 were waited for; matrix products, arithmetic and copies ran while one was open for 14% of the time, Pallas kernels for 0%

commit v1 on v0

v1 whole, which is shorter than its diff:
```python
import functools

import jax
import jax.numpy as jnp
from jax import lax
from jax.experimental import pallas as pl
from jax.experimental.pallas import tpu as pltpu
from jax.sharding import PartitionSpec as P

ADAPTER_SCALE = 2.0
VMEM_LIMIT = 48 * 1024 * 1024
BF16 = jnp.bfloat16
F32 = jnp.float32


def tile_of(size, choices):
    return next((c for c in choices if size % c == 0), size)


def exchange(x, axis, bit):
    return lax.ppermute(x, axis, [(i, i ^ bit) for i in range(lax.axis_size(axis))])


def params():
    return pltpu.CompilerParams(vmem_limit_bytes=VMEM_LIMIT)


def pick_pages(expand_pages, chosen, pool_count):
    _, ranks, hidden = expand_pages.shape
    width = hidden // pool_count

    def body(chosen_ref, page_ref, out_ref):
        out_ref[...] = page_ref[...]

    return pl.pallas_call(
        body,
        grid_spec=pltpu.PrefetchScalarGridSpec(
            num_scalar_prefetch=1,
            grid=(pool_count,),
            in_specs=[pl.BlockSpec((None, ranks, width), lambda i, c: (c[0], 0, i))],
            out_specs=pl.BlockSpec((None, ranks, width), lambda i, c: (i, 0, 0)),
        ),
        out_shape=jax.ShapeDtypeStruct((pool_count, ranks, width), BF16),
        compiler_params=params(),
        name="pick_pages",
    )(chosen, expand_pages)


def project(tp_index, activations, batch, start, rows, weight, wide=None, factors=None):
    tp = lax.axis_size("tp")
    block = rows // tp
    depth, hidden = weight.shape
    tile = tile_of(hidden, (512, 256, 128))
    order = [*range(0, tp, 2), *range(1, tp, 2)]
    half = tp // 2

    def body(t_ref, *refs):
        x_refs, refs = refs[:tp], refs[tp:]
        w_ref, refs = refs[0], refs[1:]
        if wide is not None:
            wide_refs, e_ref, refs = refs[:tp], refs[tp], refs[tp + 1 :]
        keep_ref, send_ref, xs = refs[:3]

        @pl.when(pl.program_id(0) == 0)
        def _():
            for k, x_ref in enumerate(x_refs):
                xs[k * block : (k + 1) * block, :] = x_ref[...]
            if wide is not None:
                for k, r_ref in enumerate(wide_refs):
                    refs[3][k * block : (k + 1) * block, :] = r_ref[...]

        acc = jnp.dot(xs[...], w_ref[...], preferred_element_type=F32)
        if wide is not None:
            acc += jnp.dot(refs[3][...], e_ref[...], preferred_element_type=F32)
        acc = acc.reshape(2, half, block, tile)
        keep_ref[...] = acc[0]
        send_ref[...] = acc[1].astype(BF16)

    first = start // block

    def x_spec(r, width):
        return pl.BlockSpec((None, block, width), lambda i, t: (batch, first + (t[0] ^ r), 0))

    in_specs = [x_spec(r, depth) for r in order] + [pl.BlockSpec((depth, tile), lambda i, t: (0, i))]
    operands = [activations] * tp + [weight]
    scratch = [pltpu.VMEM((rows, depth), BF16)]
    if wide is not None:
        slots = factors.shape[0]
        in_specs += [x_spec(r, slots) for r in order]
        in_specs += [pl.BlockSpec((slots, tile), lambda i, t: (0, i))]
        operands += [wide] * tp + [factors]
        scratch += [pltpu.VMEM((rows, slots), BF16)]
    out_spec = pl.BlockSpec((half, block, tile), lambda i, t: (0, 0, i))
    return pl.pallas_call(
        body,
        grid_spec=pltpu.PrefetchScalarGridSpec(
            num_scalar_prefetch=1,
            grid=(hidden // tile,),
            in_specs=in_specs,
            out_specs=[out_spec, out_spec],
            scratch_shapes=scratch,
        ),
        out_shape=[
            jax.ShapeDtypeStruct((half, block, hidden), F32),
            jax.ShapeDtypeStruct((half, block, hidden), BF16),
        ],
        compiler_params=params(),
        cost_estimate=pl.CostEstimate(
            flops=2 * rows * depth * hidden, bytes_accessed=2 * depth * hidden, transcendentals=0
        ),
        name="gate" if wide is None else "up",
    )(tp_index, *operands)


def scatter_sum(keep, send):
    bit = 1
    while True:
        got = exchange(send, "tp", bit)
        if keep.shape[0] == 1:
            return [keep[0], got[0]]
        total = keep[1::2] + got[1::2].astype(F32)
        keep = keep[0::2] + got[0::2].astype(F32)
        send = total.astype(BF16)
        bit *= 2


def gather_rows(block):
    tp = lax.axis_size("tp")
    blocks = [block]
    bit = tp // 2
    found = {0: block}
    while bit:
        for r in list(found):
            found[r ^ bit] = exchange(found[r], "tp", bit)
        bit //= 2
    return [found[r] for r in range(tp)]


def down_project(pool_index, blocks, weight, width):
    pool = lax.axis_size("pool")
    tp = len(blocks)
    block, depth = blocks[0].shape
    rows = tp * block
    half = pool // 2

    def body(p_ref, *refs):
        h_refs, w_ref, keep_ref, send_ref, hs = refs[:tp], *refs[tp:]
        step = pl.program_id(0)

        @pl.when(step == 0)
        def _():
            for k, h_ref in enumerate(h_refs):
                hs[k * block : (k + 1) * block, :] = h_ref[...]

        acc = jnp.dot(hs[...], w_ref[...], preferred_element_type=F32)

        @pl.when(step < half)
        def _():
            send_ref[...] = acc.astype(BF16)

        @pl.when(step >= half)
        def _():
            keep_ref[...] = acc

    def column(i, p):
        q = jnp.where(i < half, 2 * i + 1, 2 * (i - half))
        return (0, p[0] ^ q)

    return pl.pallas_call(
        body,
        grid_spec=pltpu.PrefetchScalarGridSpec(
            num_scalar_prefetch=1,
            grid=(pool,),
            in_specs=[pl.BlockSpec((block, depth), lambda i, p: (0, 0))] * tp
            + [pl.BlockSpec((depth, width), column)],
            out_specs=[
                pl.BlockSpec((None, rows, width), lambda i, p: (jnp.maximum(i - half, 0), 0, 0)),
                pl.BlockSpec((None, rows, width), lambda i, p: (jnp.minimum(i, half - 1), 0, 0)),
            ],
            scratch_shapes=[pltpu.VMEM((rows, depth), BF16)],
        ),
        out_shape=[
            jax.ShapeDtypeStruct((half, rows, width), F32),
            jax.ShapeDtypeStruct((half, rows, width), BF16),
        ],
        compiler_params=params(),
        cost_estimate=pl.CostEstimate(
            flops=2 * rows * depth * width * pool,
            bytes_accessed=2 * depth * width * pool,
            transcendentals=0,
        ),
        name="down",
    )(pool_index, *blocks, weight)


def pool_sum(keep, send):
    pool = lax.axis_size("pool")
    bit = 1
    while True:
        got = exchange(send, "pool", bit)
        if keep.shape[0] == 1:
            break
        send = (keep[1::2] + got[1::2].astype(F32)).astype(BF16)
        keep = keep[0::2] + got[0::2].astype(F32)
        bit *= 2
    held = (keep + got.astype(F32)).astype(BF16)
    parts = [(held, [0])]
    while bit:
        have = jnp.concatenate([a for a, _ in parts]) if len(parts) > 1 else parts[0][0]
        index = [q for _, qs in parts for q in qs]
        parts.append((exchange(have, "pool", bit), [q ^ bit for q in index]))
        bit //= 2
    return parts


def assemble(tp_index, pool_index, parts, tp):
    pool = lax.axis_size("pool")
    _, rows, width = parts[0][0].shape
    block = rows // tp
    order = [(k, j, q) for k, (_, qs) in enumerate(parts) for j, q in enumerate(qs)]
    begins = [next(s for s, o in enumerate(order) if o[0] == k) for k in range(len(parts))]

    def body(t_ref, p_ref, *refs):
        out_ref = refs[-1]
        step = pl.program_id(0)
        for k, (_, qs) in enumerate(parts):

            @pl.when((step >= begins[k]) & (step < begins[k] + len(qs)))
            def _(k=k):
                for r in range(tp):
                    at = pl.multiple_of((t_ref[0] ^ r) * block, block)
                    out_ref[pl.ds(at, block), :] = refs[k][r * block : (r + 1) * block, :]

    def out_column(i, t, p):
        q = sum(jnp.where(i == s, o[2], 0) for s, o in enumerate(order))
        return (0, p[0] ^ q)

    def in_block(begin, count):
        return lambda i, t, p: (jnp.clip(i - begin, 0, count - 1), 0, 0)

    return pl.pallas_call(
        body,
        grid_spec=pltpu.PrefetchScalarGridSpec(
            num_scalar_prefetch=2,
            grid=(pool,),
            in_specs=[
                pl.BlockSpec((None, rows, width), in_block(begins[k], len(qs)))
                for k, (_, qs) in enumerate(parts)
            ],
            out_specs=pl.BlockSpec((rows, width), out_column),
        ),
        out_shape=jax.ShapeDtypeStruct((rows, width * pool), BF16),
        compiler_params=params(),
        name="assemble",
    )(tp_index, pool_index, *[a for a, _ in parts])


def on_device(
    activations,
    gate_matrix,
    up_weight,
    down_matrix,
    shrink_pages,
    expand_pages,
    row_adapter,
    page_table,
):
    pool = lax.axis_size("pool")
    tp = lax.axis_size("tp")
    pool_index = lax.axis_index("pool")
    tp_index = lax.axis_index("tp")
    p_scalar = pool_index.astype(jnp.int32).reshape(1)
    t_scalar = tp_index.astype(jnp.int32).reshape(1)
    batches, row_count, _ = activations.shape
    page_count, ranks, _ = shrink_pages.shape
    rank_local = expand_pages.shape[1]
    columns = down_matrix.shape[1]

    catalog = jnp.arange(page_table.shape[0], dtype=jnp.int32)
    page_of_row = jnp.sum(jnp.where(row_adapter[:, :, None] == catalog, page_table, 0), axis=2)
    owned = page_of_row // page_count == pool_index
    chosen = jnp.max(jnp.where(owned, page_of_row % page_count, 0), axis=1)

    factors = []
    for m in range(batches):
        outgoing = pick_pages(expand_pages, chosen[m : m + 1], pool)
        received = lax.all_to_all(outgoing, "pool", split_axis=0, concat_axis=0, tiled=True)
        factors.append(received.reshape(pool * rank_local, -1))

    low = []
    for m in range(batches):
        page = lax.dynamic_index_in_dim(shrink_pages, chosen[m], 0, keepdims=False)
        part = lax.dot_general(
            page, activations[m], (((1,), (1,)), ((), ())), preferred_element_type=F32
        )
        low.append(jnp.where(owned[m][None, :], part, 0.0))
    low = jnp.stack(low, axis=1).reshape(tp, rank_local, batches * row_count)
    low = jnp.sum(lax.all_to_all(low, "tp", split_axis=0, concat_axis=0, tiled=True), axis=0)
    low = ADAPTER_SCALE * low.astype(BF16)
    low = lax.all_to_all(
        jnp.broadcast_to(low[None], (pool, *low.shape)), "pool", split_axis=0, concat_axis=0, tiled=True
    )
    wide = low.reshape(pool * rank_local, batches * row_count).T.reshape(
        batches, row_count, pool * rank_local
    )

    chunks = [(m, 0, row_count) for m in range(batches)]
    gates = []
    for m, start, rows in chunks:
        gates.append(scatter_sum(*project(t_scalar, activations, m, start, rows, gate_matrix)))
    outputs = []
    for (m, start, rows), gate in zip(chunks, gates):
        up = scatter_sum(
            *project(t_scalar, activations, m, start, rows, up_weight, wide, factors[m])
        )
        gate_value = gate[0] + gate[1].astype(F32)
        up_value = up[0] + up[1].astype(F32)
        hidden = (jax.nn.silu(gate_value) * up_value).astype(BF16)
        blocks = gather_rows(hidden)
        width = columns // pool
        if width % 128 == 0:
            parts = pool_sum(*down_project(p_scalar, blocks, down_matrix, width))
            outputs.append(assemble(t_scalar, p_scalar, parts, tp))
        else:
            here = jnp.stack(blocks)
            for bit in range(tp.bit_length() - 1):
                pairs = here.reshape(-1, 2, 1 << bit, *here.shape[1:])
                here = jnp.where((tp_index >> bit) & 1, pairs[:, ::-1], pairs).reshape(here.shape)
            partial = jnp.dot(
                here.reshape(rows, -1), down_matrix, preferred_element_type=F32
            )
            outputs.append(lax.psum(partial, "pool").astype(BF16))
    return jnp.concatenate(outputs, axis=0).reshape(batches, row_count, columns)


def solution(mesh):
    in_specs = (
        P(None, None, "tp"),
        P("tp", "pool"),
        P("tp", "pool"),
        P("pool", "tp"),
        P("pool", None, "tp"),
        P("pool", "tp", None),
        P(),
        P(),
    )
    return jax.shard_map(
        on_device, mesh=mesh, in_specs=in_specs, out_specs=P(None, None, "tp"), check_vma=False
    )
```

time: 465 us -> 241 us (0.52)
  blocking collectives: 209 us -> 8.67 us
  Pallas kernels: 0 us -> 69 us
  matrix products: 69 us -> 3.35 us
  waiting for transfers between devices: 133 us -> 106 us
  starting transfers between devices: 13 us -> 31.6 us
  between operations: 17.1 us -> 3.91 us
  other arithmetic: 19.5 us -> 12.3 us
    psum x2 -> x0, blocking collectives: 209 us -> none  [the longest x1 168 us: on_device(): out_total = lax.psum(partial_out, 'pool')]
    ppermute x0 -> x26, waiting for transfers between devices: none -> 98.2 us  [exchange(): lax.ppermute(x, axis, [(i, i ^ bit) for i in range(lax.axis_size(axis))])]
    reduce_scatter x2 -> x0, waiting for transfers between devices: 96.5 us -> none  [on_device(): lax.psum_scatter(jnp.concatenate([gate_term, up_product], axis=1), 'tp',...]
    pallas_call x0 -> x10, Pallas kernels: none -> 69 us  [the longest x4 41.2 us: project(): pl.pallas_call(body, grid_spec=pltpu.PrefetchScalarGridSpec(num_scalar_pr...]
    dot_general x10 -> x2, matrix products: 69 us -> 3.35 us  [on_device(): lax.dot_general(page, activations[m], (((1,), (1,)), ((), ())), preferred...]
    all_gather x2 -> x0, waiting for transfers between devices: 35 us -> none  [on_device(): lax.all_gather(hidden_cols, 'tp', axis=0, tiled=True)]
    ppermute x0 -> x26, starting transfers between devices: none -> 15.6 us  [exchange(): lax.ppermute(x, axis, [(i, i ^ bit) for i in range(lax.axis_size(axis))])]
    all_to_all x0 -> x1, blocking collectives: none -> 8.67 us  [on_device(): lax.all_to_all(low, 'tp', split_axis=0, concat_axis=0, tiled=True)]
  transfers between devices with their start and end apart: 6 -> 29, of which waited for: 5 -> 17; matrix products, arithmetic and copies ran while one was open for 14% -> 4% of each run, Pallas kernels for 0% -> 28%
where the time goes in v1:
time: 241 us; the launch traced here: 240 us
  waiting for transfers between devices  106 us (44%)
  Pallas kernels  69 us (29%)
  starting transfers between devices  31.6 us (13%)
  other arithmetic  12.3 us (5%)
  blocking collectives  8.67 us (4%)
  local copies, waits for them, and re-layouts  4.89 us (2%)
  between operations  3.91 us (2%)
  matrix products  3.35 us (1%)
    ppermute x26, waiting for transfers between devices, exchange(): lax.ppermute(x, axis, [(i, i ^ bit) for i in range(lax.axis_size(axis))])  98.2 us
    pallas_call x4, Pallas kernels, project(): pl.pallas_call(body, grid_spec=pltpu.PrefetchScalarGridSpec(num_scalar_pr...  41.2 us
    pallas_call x2, Pallas kernels, down_project(): pl.pallas_call(body, grid_spec=pltpu.PrefetchScalarGridSpec(num_scalar_pr...  19.8 us
    ppermute x26, starting transfers between devices, exchange(): lax.ppermute(x, axis, [(i, i ^ bit) for i in range(lax.axis_size(axis))])  15.6 us
    all_to_all x2, starting transfers between devices, on_device(): lax.all_to_all(outgoing, 'pool', split_axis=0, concat_axis=0, tiled=True)  10.1 us
    all_to_all x1, blocking collectives, on_device(): lax.all_to_all(low, 'tp', split_axis=0, concat_axis=0, tiled=True)  8.67 us
    pallas_call x2, Pallas kernels, pick_pages(): pl.pallas_call(body, grid_spec=pltpu.PrefetchScalarGridSpec(num_scalar_pr...  6.8 us
    all_to_all x2, waiting for transfers between devices, on_device(): lax.all_to_all(outgoing, 'pool', split_axis=0, concat_axis=0, tiled=True)  6.15 us
  transfers between devices with their start and end apart: 29, of which 17 were waited for; matrix products, arithmetic and copies ran while one was open for 4% of the time, Pallas kernels for 28%

profile of v1, /device:TPU:0, one launch (start us, length us, event | category | flops | bytes accessed | tf_op | source)
XLA Modules:
  0.0 239.9 jit_solution(15985726431406282966)
XLA Ops:
  0.0 0.9 select_reduce_fusion
  5.2 1.7 fusion
  6.9 1.7 fusion.1
  8.8 8.7 %all_to_all.20 = f32[4,16,512]{2,1,0:T(8,128)S(1)} all-to-all(f32[4,16,512]{2,1,0:T(8,128)S(1)} %reshape.39), channel_id=1, replica_groups=mesh['pool'=8,'tp'=4] {'tp'}, dimensions={0} | all-to-all | bytes 262144 | tf_op jit(solution)/shard_map/all_to_all | solution.py:298
  18.2 5.8 %all-to-all-start.1 = ((bf16[8,16,512]{2,1,0:T(8,128)(2,1)}), bf16[8,16,512]{2,1,0:T(8,128)(2,1)S(1)}, u32[]{:S(2)}, u32[]{:S(2)}) async-start(bf16[8,16,512]{2,1,0:T(8,128)(2,1)} %broadcast_in_dim.47), calls=%async_computation.1 | async-start | bytes 262144 | tf_op jit(solution)/shard_map/all_to_all | solution.py:300
  24.0 2.0 copy-done.3
  26.0 3.4 %pick_pages.3 = bf16[8,16,3584]{2,1,0:T(8,128)(2,1)} custom-call(s32[1]{0:T(128)} %get-tuple-element.38.chosen_ref, bf16[4,16,28672]{2,1,0:T(8,128)(2,1)S(1)} %copy-done.3), custom_call_target="tpu_custom_call" | custom-call | tf_op jit(solution)/shard_map/pick_pages/pallas_call | solution.py:35
  29.5 1.9 all-to-all-done.1
  31.3 4.1 %all-to-all-start.3 = ((bf16[8,16,3584]{2,1,0:T(8,128)(2,1)}), bf16[8,16,3584]{2,1,0:T(8,128)(2,1)S(1)}, u32[]{:S(2)}, u32[]{:S(2)}) async-start(bf16[8,16,3584]{2,1,0:T(8,128)(2,1)} %pick_pages.3), calls=%async_computation.3 | async-start | bytes 1835008 | tf_op jit(solution)/shard_map/all_to_all | solution.py:287
  35.5 10.3 %gate.3 = (f32[2,64,3584]{2,1,0:T(8,128)S(1)}, bf16[2,64,3584]{2,1,0:T(8,128)(2,1)}) custom-call(s32[1]{0:T(128)} %bitcast.t_ref, bf16[2,256,2048]{2,1,0:T(8,128)(2,1)S(1)} %copy-done.2, bf16[2,256,2048]{2,1,0:T(8,128)(2,1)S(1)} %copy-done.2, bf16[2,256,2048]{2,1,0:T(8,128)(2,1)S(1)} %copy-done.2, bf16[2,256,2048]{2,1,0:T(8,128)(2,1)S(1)} %copy-done.2, ...), custom_call_target="tpu_custom_call" | custom-call | flops 3758096384 | bytes 14680064 | tf_op jit(solution)/shard_map/gate/pallas_call | solution.py:94
  45.7 1.2 copy-done.8
  47.0 10.4 %gate.2 = (f32[2,64,3584]{2,1,0:T(8,128)S(1)}, bf16[2,64,3584]{2,1,0:T(8,128)(2,1)}) custom-call(s32[1]{0:T(128)} %bitcast.t_ref, bf16[2,256,2048]{2,1,0:T(8,128)(2,1)S(1)} %copy-done.2, bf16[2,256,2048]{2,1,0:T(8,128)(2,1)S(1)} %copy-done.2, bf16[2,256,2048]{2,1,0:T(8,128)(2,1)S(1)} %copy-done.2, bf16[2,256,2048]{2,1,0:T(8,128)(2,1)S(1)} %copy-done.2, ...), custom_call_target="tpu_custom_call" | custom-call | flops 3758096384 | bytes 14680064 | tf_op jit(solution)/shard_map/gate/pallas_call | solution.py:94
  57.9 3.4 %pick_pages.2 = bf16[8,16,3584]{2,1,0:T(8,128)(2,1)} custom-call(s32[1]{0:T(128)} %get-tuple-element.37.chosen_ref, bf16[4,16,28672]{2,1,0:T(8,128)(2,1)S(1)} %copy-done.4), custom_call_target="tpu_custom_call" | custom-call | tf_op jit(solution)/shard_map/pick_pages/pallas_call | solution.py:35
  61.4 6.0 %all-to-all-start.2 = ((bf16[8,16,3584]{2,1,0:T(8,128)(2,1)}), bf16[8,16,3584]{2,1,0:T(8,128)(2,1)}, u32[]{:S(2)}, u32[]{:S(2)}) async-start(bf16[8,16,3584]{2,1,0:T(8,128)(2,1)} %pick_pages.2), calls=%async_computation.2 | async-start | bytes 1835008 | tf_op jit(solution)/shard_map/all_to_all | solution.py:287
  67.4 2.1 add_convert_fusion.1
  69.9 10.6 %up.3 = (f32[2,64,3584]{2,1,0:T(8,128)S(1)}, bf16[2,64,3584]{2,1,0:T(8,128)(2,1)}) custom-call(s32[1]{0:T(128)} %bitcast.t_ref, bf16[2,256,2048]{2,1,0:T(8,128)(2,1)S(1)} %copy-done.2, bf16[2,256,2048]{2,1,0:T(8,128)(2,1)S(1)} %copy-done.2, bf16[2,256,2048]{2,1,0:T(8,128)(2,1)S(1)} %copy-done.2, bf16[2,256,2048]{2,1,0:T(8,128)(2,1)S(1)} %copy-done.2, ...), custom_call_target="tpu_custom_call" | custom-call | flops 3758096384 | bytes 14680064 | tf_op jit(solution)/shard_map/up/pallas_call | solution.py:94
  80.5 2.3 add_convert_fusion.3
  82.8 1.7 collective-permute-start.1
  84.4 6.2 %all-to-all-done.2 = bf16[8,16,3584]{2,1,0:T(8,128)(2,1)} async-done(((bf16[8,16,3584]{2,1,0:T(8,128)(2,1)}), bf16[8,16,3584]{2,1,0:T(8,128)(2,1)}, u32[]{:S(2)}, u32[]{:S(2)}) %all-to-all-start.2) | async-done | bytes 917536 | tf_op jit(solution)/shard_map/all_to_all | solution.py:287
  90.6 9.9 %up.2 = (f32[2,64,3584]{2,1,0:T(8,128)S(1)}, bf16[2,64,3584]{2,1,0:T(8,128)(2,1)S(1)}) custom-call(s32[1]{0:T(128)} %bitcast.t_ref, bf16[2,256,2048]{2,1,0:T(8,128)(2,1)S(1)} %copy-done.2, bf16[2,256,2048]{2,1,0:T(8,128)(2,1)S(1)} %copy-done.2, bf16[2,256,2048]{2,1,0:T(8,128)(2,1)S(1)} %copy-done.2, bf16[2,256,2048]{2,1,0:T(8,128)(2,1)S(1)} %copy-done.2, ...), custom_call_target="tpu_custom_call" | custom-call | flops 3758096384 | bytes 14680064 | tf_op jit(solution)/shard_map/up/pallas_call | solution.py:94
  100.6 1.2 add_convert_fusion
  102.3 0.8 collective-permute-done.2
  103.1 1.0 collective-permute-start.3
  104.1 11.1 %collective-permute-done.16 = bf16[1,64,3584]{2,1,0:T(8,128)(2,1)S(1)} collective-permute-done((bf16[1,64,3584]{2,1,0:T(8,128)(2,1)S(1)}, bf16[1,64,3584]{2,1,0:T(8,128)(2,1)S(1)}, u32[]{:S(2)}, u32[]{:S(2)}) %collective-permute-start.16) | collective-permute-done | bytes 458784 | tf_op jit(solution)/shard_map/ppermute | solution.py:21
  115.3 1.8 fusion.6.refs_0_
  117.5 7.6 %collective-permute-done.3 = bf16[1,64,3584]{2,1,0:T(8,128)(2,1)S(1)} collective-permute-done((bf16[1,64,3584]{2,1,0:T(8,128)(2,1)S(1)}, bf16[1,64,3584]{2,1,0:T(8,128)(2,1)S(1)}, u32[]{:S(2)}, u32[]{:S(2)}) %collective-permute-start.3) | collective-permute-done | bytes 458784 | tf_op jit(solution)/shard_map/ppermute | solution.py:21
  125.1 1.6 fusion.10.refs_0_
  127.2 7.8 %collective-permute-done.18.refs_2_ = bf16[64,3584]{1,0:T(8,128)(2,1)S(1)} collective-permute-done((bf16[64,3584]{1,0:T(8,128)(2,1)S(1)}, bf16[64,3584]{1,0:T(8,128)(2,1)S(1)}, u32[]{:S(2)}, u32[]{:S(2)}) %collective-permute-start.18) | collective-permute-done | bytes 458784 | tf_op jit(solution)/shard_map/ppermute | solution.py:21
  135.4 8.8 %collective-permute-done.5.refs_2_ = bf16[64,3584]{1,0:T(8,128)(2,1)S(1)} collective-permute-done((bf16[64,3584]{1,0:T(8,128)(2,1)S(1)}, bf16[64,3584]{1,0:T(8,128)(2,1)S(1)}, u32[]{:S(2)}, u32[]{:S(2)}) %collective-permute-start.5) | collective-permute-done | bytes 458784 | tf_op jit(solution)/shard_map/ppermute | solution.py:21
  144.2 9.9 %down.3 = (f32[4,256,256]{2,1,0:T(8,128)S(1)}, bf16[4,256,256]{2,1,0:T(8,128)(2,1)S(1)}) custom-call(s32[1]{0:T(128)} %bitcast.1.p_ref, bf16[64,3584]{1,0:T(8,128)(2,1)S(1)} %fusion.6.refs_0_, bf16[64,3584]{1,0:T(8,128)(2,1)S(1)} %collective-permute-done.17.refs_1_, bf16[64,3584]{1,0:T(8,128)(2,1)S(1)} %collective-permute-done.18.refs_2_, ...), custom_call_target="tpu_custom_call" | custom-call | flops 3758096384 | bytes 14680064 | tf_op jit(solution)/shard_map/down/pallas_call | solution.py:169
  154.1 1.5 collective-permute-start.20
  155.6 9.9 %down.2 = (f32[4,256,256]{2,1,0:T(8,128)S(1)}, bf16[4,256,256]{2,1,0:T(8,128)(2,1)S(1)}) custom-call(s32[1]{0:T(128)} %bitcast.1.p_ref, bf16[64,3584]{1,0:T(8,128)(2,1)S(1)} %fusion.10.refs_0_, bf16[64,3584]{1,0:T(8,128)(2,1)S(1)} %collective-permute-done.4.refs_1_, bf16[64,3584]{1,0:T(8,128)(2,1)S(1)} %collective-permute-done.5.refs_2_, ...), custom_call_target="tpu_custom_call" | custom-call | flops 3758096384 | bytes 14680064 | tf_op jit(solution)/shard_map/down/pallas_call | solution.py:169
  165.5 0.7 collective-permute-start.7
  166.2 2.4 %collective-permute-done.20 = bf16[4,256,256]{2,1,0:T(8,128)(2,1)S(1)} collective-permute-done((bf16[4,256,256]{2,1,0:T(8,128)(2,1)S(1)}, bf16[4,256,256]{2,1,0:T(8,128)(2,1)S(1)}, u32[]{:S(2)}, u32[]{:S(2)}) %collective-permute-start.20) | collective-permute-done | bytes 524320 | tf_op jit(solution)/shard_map/ppermute | solution.py:21
  169.1 10.7 %collective-permute-done.7 = bf16[4,256,256]{2,1,0:T(8,128)(2,1)S(1)} collective-permute-done((bf16[4,256,256]{2,1,0:T(8,128)(2,1)S(1)}, bf16[4,256,256]{2,1,0:T(8,128)(2,1)S(1)}, u32[]{:S(2)}, u32[]{:S(2)}) %collective-permute-start.7) | collective-permute-done | bytes 524320 | tf_op jit(solution)/shard_map/ppermute | solution.py:21
  180.0 1.9 collective-permute-start.22
  181.9 8.6 %collective-permute-done.8 = bf16[2,256,256]{2,1,0:T(8,128)(2,1)S(1)} collective-permute-done((bf16[2,256,256]{2,1,0:T(8,128)(2,1)S(1)}, bf16[2,256,256]{2,1,0:T(8,128)(2,1)S(1)}, u32[]{:S(2)}, u32[]{:S(2)}) %collective-permute-start.8) | collective-permute-done | bytes 262176 | tf_op jit(solution)/shard_map/ppermute | solution.py:21
  190.6 3.0 %collective-permute-start.23 = (bf16[1,256,256]{2,1,0:T(8,128)(2,1)S(1)}, bf16[1,256,256]{2,1,0:T(8,128)(2,1)S(1)}, u32[]{:S(2)}, u32[]{:S(2)}) collective-permute-start(bf16[1,256,256]{2,1,0:T(8,128)(2,1)S(1)} %fusion.16.refs_0_), channel_id=1, source_target_pairs={{0,16},{4,20},{8,24},{12,28},{16,0},{20,4},{24,8},{28,12},{1,17},{... | collective-permute-start | bytes 393224 | tf_op jit(solution)/shard_map/ppermute | solution.py:21
  193.6 7.2 %collective-permute-done.9 = bf16[1,256,256]{2,1,0:T(8,128)(2,1)S(1)} collective-permute-done((bf16[1,256,256]{2,1,0:T(8,128)(2,1)S(1)}, bf16[1,256,256]{2,1,0:T(8,128)(2,1)S(1)}, u32[]{:S(2)}, u32[]{:S(2)}) %collective-permute-start.9) | collective-permute-done | bytes 131104 | tf_op jit(solution)/shard_map/ppermute | solution.py:21
  201.0 5.0 %collective-permute-done.23.refs_1_ = bf16[1,256,256]{2,1,0:T(8,128)(2,1)S(1)} collective-permute-done((bf16[1,256,256]{2,1,0:T(8,128)(2,1)S(1)}, bf16[1,256,256]{2,1,0:T(8,128)(2,1)S(1)}, u32[]{:S(2)}, u32[]{:S(2)}) %collective-permute-start.23) | collective-permute-done | bytes 131104 | tf_op jit(solution)/shard_map/ppermute | solution.py:21
  206.1 2.8 %collective-permute-done.10.refs_1_ = bf16[1,256,256]{2,1,0:T(8,128)(2,1)S(1)} collective-permute-done((bf16[1,256,256]{2,1,0:T(8,128)(2,1)S(1)}, bf16[1,256,256]{2,1,0:T(8,128)(2,1)S(1)}, u32[]{:S(2)}, u32[]{:S(2)}) %collective-permute-start.10) | collective-permute-done | bytes 131104 | tf_op jit(solution)/shard_map/ppermute | solution.py:21
  209.0 6.3 %collective-permute-done.24.refs_2_ = bf16[2,256,256]{2,1,0:T(8,128)(2,1)S(1)} collective-permute-done((bf16[2,256,256]{2,1,0:T(8,128)(2,1)S(1)}, bf16[2,256,256]{2,1,0:T(8,128)(2,1)S(1)}, u32[]{:S(2)}, u32[]{:S(2)}) %collective-permute-start.24) | collective-permute-done | bytes 262176 | tf_op jit(solution)/shard_map/ppermute | solution.py:21
  215.4 1.1 collective-permute-start.25
  216.5 3.0 %collective-permute-done.11.refs_2_ = bf16[2,256,256]{2,1,0:T(8,128)(2,1)S(1)} collective-permute-done((bf16[2,256,256]{2,1,0:T(8,128)(2,1)S(1)}, bf16[2,256,256]{2,1,0:T(8,128)(2,1)S(1)}, u32[]{:S(2)}, u32[]{:S(2)}) %collective-permute-start.11) | collective-permute-done | bytes 262176 | tf_op jit(solution)/shard_map/ppermute | solution.py:21
  219.5 1.4 collective-permute-start.12
  220.9 9.4 %collective-permute-done.25.refs_3_ = bf16[4,256,256]{2,1,0:T(8,128)(2,1)S(1)} collective-permute-done((bf16[4,256,256]{2,1,0:T(8,128)(2,1)S(1)}, bf16[4,256,256]{2,1,0:T(8,128)(2,1)S(1)}, u32[]{:S(2)}, u32[]{:S(2)}) %collective-permute-start.25) | collective-permute-done | bytes 524320 | tf_op jit(solution)/shard_map/ppermute | solution.py:21
  231.0 6.7 %collective-permute-done.12.refs_3_ = bf16[4,256,256]{2,1,0:T(8,128)(2,1)S(1)} collective-permute-done((bf16[4,256,256]{2,1,0:T(8,128)(2,1)S(1)}, bf16[4,256,256]{2,1,0:T(8,128)(2,1)S(1)}, u32[]{:S(2)}, u32[]{:S(2)}) %collective-permute-start.12) | collective-permute-done | bytes 524320 | tf_op jit(solution)/shard_map/ppermute | solution.py:21
  238.3 1.6 pad_maximum_fusion
  (75 shorter events, 7.2 us)
Async XLA Ops:
  0.0 5.2 %copy-start = (bf16[4,64,2048]{2,1,0:T(8,128)(2,1)S(1)}, bf16[4,64,2048]{2,1,0:T(8,128)(2,1)}, u32[]{:S(2)}) copy-start(bf16[4,64,2048]{2,1,0:T(8,128)(2,1)} %param.12) | copy-start | bytes 3145732
  18.2 13.1 %all-to-all-start.1 = ((bf16[8,16,512]{2,1,0:T(8,128)(2,1)}), bf16[8,16,512]{2,1,0:T(8,128)(2,1)S(1)}, u32[]{:S(2)}, u32[]{:S(2)}) async-start(bf16[8,16,512]{2,1,0:T(8,128)(2,1)} %broadcast_in_dim.47), calls=%async_computation.1 | async-start | bytes 262144 | tf_op jit(solution)/shard_map/all_to_all | solution.py:300
  24.0 2.0 copy-start.3
  26.0 9.5 %copy-start.2 = (bf16[2,256,2048]{2,1,0:T(8,128)(2,1)S(1)}, bf16[2,256,2048]{2,1,0:T(8,128)(2,1)}, u32[]{:S(2)}) copy-start(bf16[2,256,2048]{2,1,0:T(8,128)(2,1)} %refs_3_.7) | copy-start | bytes 6291460
  31.3 30.0 %all-to-all-start.3 = ((bf16[8,16,3584]{2,1,0:T(8,128)(2,1)}), bf16[8,16,3584]{2,1,0:T(8,128)(2,1)S(1)}, u32[]{:S(2)}, u32[]{:S(2)}) async-start(bf16[8,16,3584]{2,1,0:T(8,128)(2,1)} %pick_pages.3), calls=%async_computation.3 | async-start | bytes 1835008 | tf_op jit(solution)/shard_map/all_to_all | solution.py:287
  45.7 1.2 copy-start.8
  47.0 20.4 %collective-permute-start.13 = (bf16[2,64,3584]{2,1,0:T(8,128)(2,1)}, bf16[2,64,3584]{2,1,0:T(8,128)(2,1)}, u32[]{:S(2)}, u32[]{:S(2)}) collective-permute-start(bf16[2,64,3584]{2,1,0:T(8,128)(2,1)} %get-tuple-element.24), channel_id=1, source_target_pairs={{0,1},{1,0},{2,3},{3,2},{4,5},{5,4},{6,7},{7,6},{8,9},{9,8},{10,11... | collective-permute-start | bytes 2752520 | tf_op jit(solution)/shard_map/ppermute | solution.py:21
  47.0 10.9 %copy-start.4 = (bf16[4,16,28672]{2,1,0:T(8,128)(2,1)S(1)}, bf16[4,16,28672]{2,1,0:T(8,128)(2,1)}, u32[]{:S(2)}) copy-start(bf16[4,16,28672]{2,1,0:T(8,128)(2,1)} %page_ref.3) | copy-start | bytes 11010052
  57.3 3.9 %copy-start.5 = (f32[2,64,3584]{2,1,0:T(8,128)}, f32[2,64,3584]{2,1,0:T(8,128)S(1)}, u32[]{:S(2)}) copy-start(f32[2,64,3584]{2,1,0:T(8,128)S(1)} %get-tuple-element.17) | copy-start | bytes 5505028
  57.3 23.1 %collective-permute-start = (bf16[2,64,3584]{2,1,0:T(8,128)(2,1)}, bf16[2,64,3584]{2,1,0:T(8,128)(2,1)}, u32[]{:S(2)}, u32[]{:S(2)}) collective-permute-start(bf16[2,64,3584]{2,1,0:T(8,128)(2,1)} %get-tuple-element.18), channel_id=1, source_target_pairs={{0,1},{1,0},{2,3},{3,2},{4,5},{5,4},{6,7},{7,6},{8,9},{9,8},{10,11... | collective-permute-start | bytes 2752520 | tf_op jit(solution)/shard_map/ppermute | solution.py:21
  61.4 29.2 %all-to-all-start.2 = ((bf16[8,16,3584]{2,1,0:T(8,128)(2,1)}), bf16[8,16,3584]{2,1,0:T(8,128)(2,1)}, u32[]{:S(2)}, u32[]{:S(2)}) async-start(bf16[8,16,3584]{2,1,0:T(8,128)(2,1)} %pick_pages.2), calls=%async_computation.2 | async-start | bytes 1835008 | tf_op jit(solution)/shard_map/all_to_all | solution.py:287
  69.5 34.6 %collective-permute-start.14 = (bf16[1,64,3584]{2,1,0:T(8,128)(2,1)}, bf16[1,64,3584]{2,1,0:T(8,128)(2,1)}, u32[]{:S(2)}, u32[]{:S(2)}) collective-permute-start(bf16[1,64,3584]{2,1,0:T(8,128)(2,1)} %add_convert_fusion.1), channel_id=1, source_target_pairs={{0,2},{1,3},{2,0},{3,1},{4,6},{5,7},{6,4},{7,5},{8,10},{9,11},{10,... | collective-permute-start | bytes 1376264 | tf_op jit(solution)/shard_map/ppermute | solution.py:21
  69.9 10.6 %copy-start.6 = (f32[2,64,3584]{2,1,0:T(8,128)S(1)}, f32[2,64,3584]{2,1,0:T(8,128)}, u32[]{:S(2)}) copy-start(f32[2,64,3584]{2,1,0:T(8,128)} %copy-done.5) | copy-start | bytes 5505028
  80.5 2.3 copy-start.10
  80.5 20.1 %collective-permute-start.15 = (bf16[2,64,3584]{2,1,0:T(8,128)(2,1)}, bf16[2,64,3584]{2,1,0:T(8,128)(2,1)}, u32[]{:S(2)}, u32[]{:S(2)}) collective-permute-start(bf16[2,64,3584]{2,1,0:T(8,128)(2,1)} %get-tuple-element.26), channel_id=1, source_target_pairs={{0,1},{1,0},{2,3},{3,2},{4,5},{5,4},{6,7},{7,6},{8,9},{9,8},{10,11... | collective-permute-start | bytes 2752520 | tf_op jit(solution)/shard_map/ppermute | solution.py:21
  82.8 34.7 %collective-permute-start.1 = (bf16[1,64,3584]{2,1,0:T(8,128)(2,1)}, bf16[1,64,3584]{2,1,0:T(8,128)(2,1)}, u32[]{:S(2)}, u32[]{:S(2)}) collective-permute-start(bf16[1,64,3584]{2,1,0:T(8,128)(2,1)} %add_convert_fusion.3), channel_id=1, source_target_pairs={{0,2},{1,3},{2,0},{3,1},{4,6},{5,7},{6,4},{7,5},{8,10},{9,11},{10,... | collective-permute-start | bytes 1376264 | tf_op jit(solution)/shard_map/ppermute | solution.py:21
  90.6 10.0 %copy-start.11 = (f32[2,64,3584]{2,1,0:T(8,128)S(1)}, f32[2,64,3584]{2,1,0:T(8,128)}, u32[]{:S(2)}) copy-start(f32[2,64,3584]{2,1,0:T(8,128)} %copy-done.10) | copy-start | bytes 5505028
  100.5 14.8 %copy-start.9 = (f32[2,64,3584]{2,1,0:T(8,128)S(1)}, f32[2,64,3584]{2,1,0:T(8,128)}, u32[]{:S(2)}) copy-start(f32[2,64,3584]{2,1,0:T(8,128)} %copy-done.8) | copy-start | bytes 5505028
  100.5 2.5 %collective-permute-start.2 = (bf16[2,64,3584]{2,1,0:T(8,128)(2,1)S(1)}, bf16[2,64,3584]{2,1,0:T(8,128)(2,1)S(1)}, u32[]{:S(2)}, u32[]{:S(2)}) collective-permute-start(bf16[2,64,3584]{2,1,0:T(8,128)(2,1)S(1)} %get-tuple-element.20), channel_id=1, source_target_pairs={{0,1},{1,0},{2,3},{3,2},{4,5},{5,4},{6,7},{7,6},{8,9},{9,8},{10,11... | collective-permute-start | bytes 2752520 | tf_op jit(solution)/shard_map/ppermute | solution.py:21
  101.8 13.4 %collective-permute-start.16 = (bf16[1,64,3584]{2,1,0:T(8,128)(2,1)S(1)}, bf16[1,64,3584]{2,1,0:T(8,128)(2,1)S(1)}, u32[]{:S(2)}, u32[]{:S(2)}) collective-permute-start(bf16[1,64,3584]{2,1,0:T(8,128)(2,1)S(1)} %add_convert_fusion), channel_id=1, source_target_pairs={{0,2},{1,3},{2,0},{3,1},{4,6},{5,7},{6,4},{7,5},{8,10},{9,11},{10,... | collective-permute-start | bytes 1376264 | tf_op jit(solution)/shard_map/ppermute | solution.py:21
  103.1 22.0 %copy-start.7 = (f32[2,64,3584]{2,1,0:T(8,128)S(1)}, f32[2,64,3584]{2,1,0:T(8,128)}, u32[]{:S(2)}) copy-start(f32[2,64,3584]{2,1,0:T(8,128)} %copy-done.5) | copy-start | bytes 5505028
  103.1 22.0 %collective-permute-start.3 = (bf16[1,64,3584]{2,1,0:T(8,128)(2,1)S(1)}, bf16[1,64,3584]{2,1,0:T(8,128)(2,1)S(1)}, u32[]{:S(2)}, u32[]{:S(2)}) collective-permute-start(bf16[1,64,3584]{2,1,0:T(8,128)(2,1)S(1)} %add_convert_fusion.2), channel_id=1, source_target_pairs={{0,2},{1,3},{2,0},{3,1},{4,6},{5,7},{6,4},{7,5},{8,10},{9,11},{10,... | collective-permute-start | bytes 1376264 | tf_op jit(solution)/shard_map/ppermute | solution.py:21
  117.0 17.9 %collective-permute-start.18 = (bf16[64,3584]{1,0:T(8,128)(2,1)S(1)}, bf16[64,3584]{1,0:T(8,128)(2,1)S(1)}, u32[]{:S(2)}, u32[]{:S(2)}) collective-permute-start(bf16[64,3584]{1,0:T(8,128)(2,1)S(1)} %fusion.6.refs_0_), channel_id=1, source_target_pairs={{0,2},{1,3},{2,0},{3,1},{4,6},{5,7},{6,4},{7,5},{8,10},{9,11},{10,... | collective-permute-start | bytes 1376264 | tf_op jit(solution)/shard_map/ppermute | solution.py:21
  126.7 17.5 %collective-permute-start.5 = (bf16[64,3584]{1,0:T(8,128)(2,1)S(1)}, bf16[64,3584]{1,0:T(8,128)(2,1)S(1)}, u32[]{:S(2)}, u32[]{:S(2)}) collective-permute-start(bf16[64,3584]{1,0:T(8,128)(2,1)S(1)} %fusion.10.refs_0_), channel_id=1, source_target_pairs={{0,2},{1,3},{2,0},{3,1},{4,6},{5,7},{6,4},{7,5},{8,10},{9,11},{10,... | collective-permute-start | bytes 1376264 | tf_op jit(solution)/shard_map/ppermute | solution.py:21
  127.2 17.0 %collective-permute-start.17 = (bf16[64,3584]{1,0:T(8,128)(2,1)S(1)}, bf16[64,3584]{1,0:T(8,128)(2,1)S(1)}, u32[]{:S(2)}, u32[]{:S(2)}) collective-permute-start(bf16[64,3584]{1,0:T(8,128)(2,1)S(1)} %fusion.6.refs_0_), channel_id=1, source_target_pairs={{0,1},{1,0},{2,3},{3,2},{4,5},{5,4},{6,7},{7,6},{8,9},{9,8},{10,11... | collective-permute-start | bytes 1376264 | tf_op jit(solution)/shard_map/ppermute | solution.py:21
  134.9 9.3 %collective-permute-start.19 = (bf16[64,3584]{1,0:T(8,128)(2,1)S(1)}, bf16[64,3584]{1,0:T(8,128)(2,1)S(1)}, u32[]{:S(2)}, u32[]{:S(2)}) collective-permute-start(bf16[64,3584]{1,0:T(8,128)(2,1)S(1)} %collective-permute-done.18.refs_2_), channel_id=1, source_target_pairs={{0,1},{1,0},{2,3},{3,2},{4,5},{5,4},{6,7},{7,6},{8,9},{9,8},{10,11... | collective-permute-start | bytes 1376264 | tf_op jit(solution)/shard_map/ppermute | solution.py:21
  134.9 20.7 %collective-permute-start.4 = (bf16[64,3584]{1,0:T(8,128)(2,1)S(1)}, bf16[64,3584]{1,0:T(8,128)(2,1)S(1)}, u32[]{:S(2)}, u32[]{:S(2)}) collective-permute-start(bf16[64,3584]{1,0:T(8,128)(2,1)S(1)} %fusion.10.refs_0_), channel_id=1, source_target_pairs={{0,1},{1,0},{2,3},{3,2},{4,5},{5,4},{6,7},{7,6},{8,9},{9,8},{10,11... | collective-permute-start | bytes 1376264 | tf_op jit(solution)/shard_map/ppermute | solution.py:21
  144.2 11.4 %collective-permute-start.6 = (bf16[64,3584]{1,0:T(8,128)(2,1)S(1)}, bf16[64,3584]{1,0:T(8,128)(2,1)S(1)}, u32[]{:S(2)}, u32[]{:S(2)}) collective-permute-start(bf16[64,3584]{1,0:T(8,128)(2,1)S(1)} %collective-permute-done.5.refs_2_), channel_id=1, source_target_pairs={{0,1},{1,0},{2,3},{3,2},{4,5},{5,4},{6,7},{7,6},{8,9},{9,8},{10,11... | collective-permute-start | bytes 1376264 | tf_op jit(solution)/shard_map/ppermute | solution.py:21
  154.1 14.5 %collective-permute-start.20 = (bf16[4,256,256]{2,1,0:T(8,128)(2,1)S(1)}, bf16[4,256,256]{2,1,0:T(8,128)(2,1)S(1)}, u32[]{:S(2)}, u32[]{:S(2)}) collective-permute-start(bf16[4,256,256]{2,1,0:T(8,128)(2,1)S(1)} %get-tuple-element.28), channel_id=1, source_target_pairs={{0,4},{4,0},{8,12},{12,8},{16,20},{20,16},{24,28},{28,24},{1,5},{5... | collective-permute-start | bytes 1572872 | tf_op jit(solution)/shard_map/ppermute | solution.py:21
  165.5 14.2 %collective-permute-start.7 = (bf16[4,256,256]{2,1,0:T(8,128)(2,1)S(1)}, bf16[4,256,256]{2,1,0:T(8,128)(2,1)S(1)}, u32[]{:S(2)}, u32[]{:S(2)}) collective-permute-start(bf16[4,256,256]{2,1,0:T(8,128)(2,1)S(1)} %get-tuple-element.22), channel_id=1, source_target_pairs={{0,4},{4,0},{8,12},{12,8},{16,20},{20,16},{24,28},{28,24},{1,5},{5... | collective-permute-start | bytes 1572872 | tf_op jit(solution)/shard_map/ppermute | solution.py:21
  168.7 11.3 %collective-permute-start.21 = (bf16[2,256,256]{2,1,0:T(8,128)(2,1)S(1)}, bf16[2,256,256]{2,1,0:T(8,128)(2,1)S(1)}, u32[]{:S(2)}, u32[]{:S(2)}) collective-permute-start(bf16[2,256,256]{2,1,0:T(8,128)(2,1)S(1)} %get-tuple-element.35), channel_id=1, source_target_pairs={{0,8},{4,12},{8,0},{12,4},{16,24},{20,28},{24,16},{28,20},{1,9},{5... | collective-permute-start | bytes 786440 | tf_op jit(solution)/shard_map/ppermute | solution.py:21
  179.9 10.6 %collective-permute-start.8 = (bf16[2,256,256]{2,1,0:T(8,128)(2,1)S(1)}, bf16[2,256,256]{2,1,0:T(8,128)(2,1)S(1)}, u32[]{:S(2)}, u32[]{:S(2)}) collective-permute-start(bf16[2,256,256]{2,1,0:T(8,128)(2,1)S(1)} %get-tuple-element.33), channel_id=1, source_target_pairs={{0,8},{4,12},{8,0},{12,4},{16,24},{20,28},{24,16},{28,20},{1,9},{5... | collective-permute-start | bytes 786440 | tf_op jit(solution)/shard_map/ppermute | solution.py:21
  180.0 10.6 %collective-permute-start.22 = (bf16[1,256,256]{2,1,0:T(8,128)(2,1)S(1)}, bf16[1,256,256]{2,1,0:T(8,128)(2,1)S(1)}, u32[]{:S(2)}, u32[]{:S(2)}) collective-permute-start(bf16[1,256,256]{2,1,0:T(8,128)(2,1)S(1)} %fusion.14), channel_id=1, source_target_pairs={{0,16},{4,20},{8,24},{12,28},{16,0},{20,4},{24,8},{28,12},{1,17},{... | collective-permute-start | bytes 393224 | tf_op jit(solution)/shard_map/ppermute | solution.py:21
  190.5 10.3 %collective-permute-start.9 = (bf16[1,256,256]{2,1,0:T(8,128)(2,1)S(1)}, bf16[1,256,256]{2,1,0:T(8,128)(2,1)S(1)}, u32[]{:S(2)}, u32[]{:S(2)}) collective-permute-start(bf16[1,256,256]{2,1,0:T(8,128)(2,1)S(1)} %fusion.17), channel_id=1, source_target_pairs={{0,16},{4,20},{8,24},{12,28},{16,0},{20,4},{24,8},{28,12},{1,17},{... | collective-permute-start | bytes 393224 | tf_op jit(solution)/shard_map/ppermute | solution.py:21
  190.6 15.4 %collective-permute-start.23 = (bf16[1,256,256]{2,1,0:T(8,128)(2,1)S(1)}, bf16[1,256,256]{2,1,0:T(8,128)(2,1)S(1)}, u32[]{:S(2)}, u32[]{:S(2)}) collective-permute-start(bf16[1,256,256]{2,1,0:T(8,128)(2,1)S(1)} %fusion.16.refs_0_), channel_id=1, source_target_pairs={{0,16},{4,20},{8,24},{12,28},{16,0},{20,4},{24,8},{28,12},{1,17},{... | collective-permute-start | bytes 393224 | tf_op jit(solution)/shard_map/ppermute | solution.py:21
  200.9 8.1 %collective-permute-start.10 = (bf16[1,256,256]{2,1,0:T(8,128)(2,1)S(1)}, bf16[1,256,256]{2,1,0:T(8,128)(2,1)S(1)}, u32[]{:S(2)}, u32[]{:S(2)}) collective-permute-start(bf16[1,256,256]{2,1,0:T(8,128)(2,1)S(1)} %fusion.19.refs_0_), channel_id=1, source_target_pairs={{0,16},{4,20},{8,24},{12,28},{16,0},{20,4},{24,8},{28,12},{1,17},{... | collective-permute-start | bytes 393224 | tf_op jit(solution)/shard_map/ppermute | solution.py:21
  206.0 9.3 %collective-permute-start.24 = (bf16[2,256,256]{2,1,0:T(8,128)(2,1)S(1)}, bf16[2,256,256]{2,1,0:T(8,128)(2,1)S(1)}, u32[]{:S(2)}, u32[]{:S(2)}) collective-permute-start(bf16[2,256,256]{2,1,0:T(8,128)(2,1)S(1)} %pad_maximum_fusion.4), channel_id=1, source_target_pairs={{0,8},{4,12},{8,0},{12,4},{16,24},{20,28},{24,16},{28,20},{1,9},{5... | collective-permute-start | bytes 786440 | tf_op jit(solution)/shard_map/ppermute | solution.py:21
  209.0 10.5 %collective-permute-start.11 = (bf16[2,256,256]{2,1,0:T(8,128)(2,1)S(1)}, bf16[2,256,256]{2,1,0:T(8,128)(2,1)S(1)}, u32[]{:S(2)}, u32[]{:S(2)}) collective-permute-start(bf16[2,256,256]{2,1,0:T(8,128)(2,1)S(1)} %pad_maximum_fusion.3), channel_id=1, source_target_pairs={{0,8},{4,12},{8,0},{12,4},{16,24},{20,28},{24,16},{28,20},{1,9},{5... | collective-permute-start | bytes 786440 | tf_op jit(solution)/shard_map/ppermute | solution.py:21
  215.4 14.9 %collective-permute-start.25 = (bf16[4,256,256]{2,1,0:T(8,128)(2,1)S(1)}, bf16[4,256,256]{2,1,0:T(8,128)(2,1)S(1)}, u32[]{:S(2)}, u32[]{:S(2)}) collective-permute-start(bf16[4,256,256]{2,1,0:T(8,128)(2,1)S(1)} %pad_maximum_fusion.2), channel_id=1, source_target_pairs={{0,4},{4,0},{8,12},{12,8},{16,20},{20,16},{24,28},{28,24},{1,5},{5... | collective-permute-start | bytes 1572872 | tf_op jit(solution)/shard_map/ppermute | solution.py:21
  219.5 18.1 %collective-permute-start.12 = (bf16[4,256,256]{2,1,0:T(8,128)(2,1)S(1)}, bf16[4,256,256]{2,1,0:T(8,128)(2,1)S(1)}, u32[]{:S(2)}, u32[]{:S(2)}) collective-permute-start(bf16[4,256,256]{2,1,0:T(8,128)(2,1)S(1)} %pad_maximum_fusion.1), channel_id=1, source_target_pairs={{0,4},{4,0},{8,12},{12,8},{16,20},{20,16},{24,28},{28,24},{1,5},{5... | collective-permute-start | bytes 1572872 | tf_op jit(solution)/shard_map/ppermute | solution.py:21
  237.7 2.2 copy-start.1

commit v2 on v1

v2 whole, which is shorter than its diff:
```python
import jax
import jax.numpy as jnp
from jax import lax
from jax.experimental import pallas as pl
from jax.experimental.pallas import tpu as pltpu
from jax.sharding import PartitionSpec as P

ADAPTER_SCALE = 2.0
VMEM_LIMIT = 48 * 1024 * 1024
BF16 = jnp.bfloat16
F32 = jnp.float32


def tile_of(size, choices):
    return next((c for c in choices if size % c == 0), size)


def exchange(x, axis, bit):
    return lax.ppermute(x, axis, [(i, i ^ bit) for i in range(lax.axis_size(axis))])


def params():
    return pltpu.CompilerParams(vmem_limit_bytes=VMEM_LIMIT)


def pick_pages(pool_index, page_table, row_adapter, expand_pages, page_count, pool_count):
    _, ranks, hidden = expand_pages.shape
    width = hidden // pool_count
    batches, row_count = row_adapter.shape

    def body(p_ref, table_ref, rows_ref, pages_ref, chosen_ref, mask_ref, *refs):
        outs, sems = refs[:batches], refs[batches]
        copies = []
        for m in range(batches):
            rows = rows_ref[m : m + 1, :]
            page = jnp.zeros_like(rows)
            for a in range(page_table.shape[0]):
                page = jnp.where(rows == a, table_ref[a], page)
            local = page - p_ref[0] * page_count
            owned = (local >= 0) & (local < page_count)
            mask_ref[m] = jnp.where(owned, 1.0, 0.0)
            chosen = jnp.max(jnp.where(owned, local, 0))
            chosen_ref[m] = chosen
            for q in range(pool_count):
                source = pages_ref.at[chosen, :, pl.ds(q * width, width)]
                copy = pltpu.make_async_copy(source, outs[m].at[q], sems.at[m * pool_count + q])
                copy.start()
                copies.append(copy)
        for copy in copies:
            copy.wait()

    smem = pl.BlockSpec(memory_space=pltpu.SMEM)
    vmem = pl.BlockSpec(memory_space=pltpu.VMEM)
    hbm = pl.BlockSpec(memory_space=pltpu.HBM)
    chosen, mask, *blocks = pl.pallas_call(
        body,
        in_specs=[smem, smem, vmem, hbm],
        out_specs=[smem, vmem] + [hbm] * batches,
        out_shape=[
            jax.ShapeDtypeStruct((batches,), jnp.int32),
            jax.ShapeDtypeStruct((batches, 1, row_count), F32),
        ]
        + [jax.ShapeDtypeStruct((pool_count, ranks, width), BF16)] * batches,
        scratch_shapes=[pltpu.SemaphoreType.DMA((batches * pool_count,))],
        compiler_params=params(),
        name="pick_pages",
    )(pool_index, page_table, row_adapter, expand_pages)
    return chosen, mask, blocks


def shrink(tp_index, chosen, mask, activations, shrink_pages, tp):
    batches, row_count, depth = activations.shape
    ranks = shrink_pages.shape[1]
    local = ranks // tp

    def body(t_ref, chosen_ref, page_ref, x_ref, mask_ref, keep_ref, send_ref):
        part = lax.dot_general(
            page_ref[...], x_ref[...], (((1,), (1,)), ((), ())), preferred_element_type=F32
        )
        part = jnp.where(mask_ref[...] > 0.5, part, 0.0)
        blocks = [part[k * local : (k + 1) * local] for k in range(tp)]
        for bit in range(tp.bit_length() - 1):
            flip = ((t_ref[0] >> bit) & 1) == 1
            blocks = [jnp.where(flip, blocks[k ^ (1 << bit)], blocks[k]) for k in range(tp)]
        for k in range(tp // 2):
            keep_ref[k] = blocks[2 * k]
            send_ref[k] = blocks[2 * k + 1]

    out_spec = pl.BlockSpec((tp // 2, local, row_count), lambda m, t, c: (0, 0, m))
    return pl.pallas_call(
        body,
        grid_spec=pltpu.PrefetchScalarGridSpec(
            num_scalar_prefetch=2,
            grid=(batches,),
            in_specs=[
                pl.BlockSpec((None, ranks, depth), lambda m, t, c: (c[m], 0, 0)),
                pl.BlockSpec((None, row_count, depth), lambda m, t, c: (m, 0, 0)),
                pl.BlockSpec((None, 1, row_count), lambda m, t, c: (m, 0, 0)),
            ],
            out_specs=[out_spec, out_spec],
        ),
        out_shape=[jax.ShapeDtypeStruct((tp // 2, local, batches * row_count), F32)] * 2,
        compiler_params=params(),
        name="shrink",
    )(tp_index, chosen, shrink_pages, activations, mask)


def project(tp_index, activations, group, start, rows, weight, wide=None, factors=None):
    tp = lax.axis_size("tp")
    block = rows // tp
    depth, hidden = weight.shape
    tile = tile_of(hidden, (896, 512, 256, 128))
    half = tp // 2
    order = [(m, r) for first in (0, 1) for m in group for r in range(first, tp, 2)]
    count = len(order)
    pieces = 0 if wide is None else len(factors)

    def body(t_ref, *refs):
        x_refs, refs = refs[:count], refs[count:]
        w_ref, refs = refs[0], refs[1:]
        if wide is not None:
            wide_refs, e_refs = refs[:count], refs[count : count + pieces]
            refs = refs[count + pieces :]
        keep_ref, send_ref, xs = refs[:3]

        @pl.when(pl.program_id(0) == 0)
        def _():
            for k, x_ref in enumerate(x_refs):
                xs[k * block : (k + 1) * block, :] = x_ref[...]
            if wide is not None:
                for k, r_ref in enumerate(wide_refs):
                    refs[3][k * block : (k + 1) * block, :] = r_ref[...]

        acc = jnp.dot(xs[...], w_ref[...], preferred_element_type=F32)
        if wide is not None:
            e_all = jnp.concatenate([e_ref[...] for e_ref in e_refs], axis=0)
            acc += jnp.dot(refs[3][...], e_all, preferred_element_type=F32)
        acc = acc.reshape(2, len(group), half, block, tile)
        keep_ref[...] = acc[0]
        send_ref[...] = acc[1].astype(BF16)

    first = start // block

    def x_spec(m, r, width):
        return pl.BlockSpec((None, block, width), lambda i, t: (m, first + (t[0] ^ r), 0))

    in_specs = [x_spec(m, r, depth) for m, r in order] + [pl.BlockSpec((depth, tile), lambda i, t: (0, i))]
    operands = [activations] * count + [weight]
    scratch = [pltpu.VMEM((count * block, depth), BF16)]
    if wide is not None:
        slots = wide.shape[-1]
        in_specs += [x_spec(m, r, slots) for m, r in order]
        in_specs += [pl.BlockSpec((slots // pieces, tile), lambda i, t: (0, i))] * pieces
        operands += [wide] * count + list(factors)
        scratch += [pltpu.VMEM((count * block, slots), BF16)]
    out_spec = pl.BlockSpec((len(group), half, block, tile), lambda i, t: (0, 0, 0, i))
    return pl.pallas_call(
        body,
        grid_spec=pltpu.PrefetchScalarGridSpec(
            num_scalar_prefetch=1,
            grid=(hidden // tile,),
            in_specs=in_specs,
            out_specs=[out_spec, out_spec],
            scratch_shapes=scratch,
        ),
        out_shape=[
            jax.ShapeDtypeStruct((len(group), half, block, hidden), F32),
            jax.ShapeDtypeStruct((len(group), half, block, hidden), BF16),
        ],
        compiler_params=params(),
        cost_estimate=pl.CostEstimate(
            flops=2 * count * block * depth * hidden, bytes_accessed=2 * depth * hidden, transcendentals=0
        ),
        name="gate" if wide is None else "up",
    )(tp_index, *operands)


def scatter_sum(keep, send, after=()):
    terms, bit = [keep], 1
    while True:
        last = terms[0].shape[1] == 1
        if last and after:
            send, *after = lax.optimization_barrier((send, *after))
        terms.append(exchange(send, "tp", bit))
        if last:
            terms = [x[:, 0] for x in terms]
            return (terms, after) if after else terms
        send = sum(x[:, 1::2].astype(F32) for x in terms).astype(send.dtype)
        terms = [x[:, 0::2] for x in terms]
        bit *= 2


def gather_rows(block):
    tp = lax.axis_size("tp")
    blocks = [block]
    bit = tp // 2
    found = {0: block}
    while bit:
        for r in list(found):
            found[r ^ bit] = exchange(found[r], "tp", bit)
        bit //= 2
    return [found[r] for r in range(tp)]


def down_project(pool_index, blocks, weight, first, columns):
    pool = lax.axis_size("pool")
    tp = len(blocks)
    block, depth = blocks[0].shape
    rows = tp * block
    half = pool // 2
    piece = rows // pool
    per_block = block // piece
    tile = tile_of(columns, (512, 256, 128))

    def body(p_ref, *refs):
        h_refs, w_ref, keep_ref, send_ref, hs = refs[:tp], *refs[tp:]

        @pl.when(pl.program_id(0) == 0)
        def _():
            for k in range(pool):
                q = p_ref[0] ^ k
                at = pl.multiple_of(((q & 1) * half + (q >> 1)) * piece, piece)
                j = k % per_block
                hs[pl.ds(at, piece), :] = h_refs[k // per_block][j * piece : (j + 1) * piece, :]

        acc = jnp.dot(hs[...], w_ref[...], preferred_element_type=F32)
        acc = acc.reshape(2, half, piece, tile)
        keep_ref[...] = acc[0]
        send_ref[...] = acc[1].astype(BF16)

    out_spec = pl.BlockSpec((half, piece, tile), lambda i, p: (0, 0, i))
    return pl.pallas_call(
        body,
        grid_spec=pltpu.PrefetchScalarGridSpec(
            num_scalar_prefetch=1,
            grid=(columns // tile,),
            in_specs=[pl.BlockSpec((block, depth), lambda i, p: (0, 0))] * tp
            + [pl.BlockSpec((depth, tile), lambda i, p: (0, first // tile + i))],
            out_specs=[out_spec, out_spec],
            scratch_shapes=[pltpu.VMEM((rows, depth), BF16)],
        ),
        out_shape=[
            jax.ShapeDtypeStruct((half, piece, columns), F32),
            jax.ShapeDtypeStruct((half, piece, columns), BF16),
        ],
        compiler_params=params(),
        cost_estimate=pl.CostEstimate(
            flops=2 * rows * depth * columns, bytes_accessed=2 * depth * columns, transcendentals=0
        ),
        name="down",
    )(pool_index, *blocks, weight)


def pool_sum(keep, send):
    terms, bit = [keep], 1
    while True:
        terms.append(exchange(send, "pool", bit))
        if terms[0].shape[0] == 1:
            break
        send = sum(x[1::2].astype(F32) for x in terms).astype(BF16)
        terms = [x[0::2] for x in terms]
        bit *= 2
    parts = [(sum(x.astype(F32) for x in terms).astype(BF16), [0])]
    while bit:
        have = jnp.concatenate([x for x, _ in parts]) if len(parts) > 1 else parts[0][0]
        order = [q ^ bit for _, qs in parts for q in qs]
        parts.append((exchange(have, "pool", bit), order))
        bit //= 2
    return parts


def place(tp_index, pool_index, parts, out, shape, batch, start, first):
    pool = sum(len(qs) for _, qs in parts)
    tp = lax.axis_size("tp")
    _, piece, columns = parts[0][0].shape
    per_block = pool // tp

    def body(t_ref, p_ref, *refs):
        out_ref, sems = refs[-2:]
        copies = []
        for part_ref, (_, qs) in zip(refs, parts):
            for j, q in enumerate(qs):
                k = p_ref[0] ^ q
                block = t_ref[0] ^ (k // per_block)
                at = pl.multiple_of(start + (block * per_block + k % per_block) * piece, piece)
                target = out_ref.at[batch, pl.ds(at, piece), pl.ds(first, columns)]
                copies.append(pltpu.make_async_copy(part_ref.at[j], target, sems.at[q]))
        for copy in copies:
            copy.start()
        for copy in copies:
            copy.wait()

    held = [] if out is None else [out]
    return pl.pallas_call(
        body,
        in_specs=[pl.BlockSpec(memory_space=pltpu.SMEM)] * 2
        + [pl.BlockSpec(memory_space=pl.ANY)] * (len(parts) + len(held)),
        out_specs=pl.BlockSpec(memory_space=pl.ANY),
        out_shape=jax.ShapeDtypeStruct(shape, BF16),
        scratch_shapes=[pltpu.SemaphoreType.DMA((pool,))],
        input_output_aliases={2 + len(parts): 0} if held else {},
        compiler_params=params(),
        name="place",
    )(tp_index, pool_index, *[x for x, _ in parts], *held)


def by_index(x, index):
    for bit in range(x.shape[0].bit_length() - 1):
        pairs = x.reshape(-1, 2, 1 << bit, *x.shape[1:])
        x = jnp.where((index >> bit) & 1, pairs[:, ::-1], pairs).reshape(x.shape)
    return x


def on_device(
    activations,
    gate_matrix,
    up_weight,
    down_matrix,
    shrink_pages,
    expand_pages,
    row_adapter,
    page_table,
):
    pool = lax.axis_size("pool")
    tp = lax.axis_size("tp")
    pool_index = lax.axis_index("pool")
    tp_index = lax.axis_index("tp")
    p_scalar = pool_index.astype(jnp.int32).reshape(1)
    t_scalar = tp_index.astype(jnp.int32).reshape(1)
    batches, row_count, _ = activations.shape
    page_count = shrink_pages.shape[0]
    rank_local = expand_pages.shape[1]
    columns = down_matrix.shape[1]
    chunks = [(m, 0, row_count) for m in range(batches)]

    def across(x):
        return lax.all_to_all(x, "pool", split_axis=0, concat_axis=0, tiled=True)

    chosen, mask, picked = pick_pages(
        p_scalar, page_table, row_adapter, expand_pages, page_count, pool
    )
    factors = [across(picked[0])]
    low = shrink(t_scalar, chosen, mask, activations, shrink_pages, tp)
    low = sum(scatter_sum(*(x[None] for x in low)))
    low = ADAPTER_SCALE * low.astype(BF16)
    ready, rows_in = lax.optimization_barrier((low, activations))
    gate = project(t_scalar, rows_in, range(batches), 0, row_count, gate_matrix)
    wide, bit = ready, 1
    while 4 * bit < pool:
        wide = jnp.concatenate([wide, exchange(wide, "pool", bit)])
        bit *= 2
    gate, (wide, *outgoing) = scatter_sum(*gate, (wide, *picked[1:]))
    while bit < pool:
        wide = jnp.concatenate([wide, exchange(wide, "pool", bit)])
        bit *= 2
    wide = wide.reshape(pool, rank_local, -1)
    factors += [across(x) for x in outgoing]
    wide = by_index(wide, pool_index)
    wide = wide.reshape(pool * rank_local, batches * row_count).T
    wide = wide.reshape(batches, row_count, pool * rank_local)
    factors = [x.reshape(pool * rank_local, -1) for x in factors]
    apart = row_count % (16 * pool) == 0 and pool % tp == 0 and columns % 512 == 0
    out = None
    outputs = []
    rows_in = activations
    for m, start, rows in chunks:
        up = project(t_scalar, rows_in, (m,), start, rows, up_weight, wide, [factors[m]])
        held = 0 if apart else len(gate) - 1
        up, gate[held:] = scatter_sum(*up, gate[held:])
        gate_value = sum(x[m].astype(F32) for x in gate)
        up_value = sum(x[0].astype(F32) for x in up)
        hidden = (jax.nn.silu(gate_value) * up_value).astype(BF16)
        hidden, rows_in = lax.optimization_barrier((hidden, rows_in))
        blocks = gather_rows(hidden)
        if apart:
            groups = 2
            width = columns // groups
            for g in range(groups):
                pieces = pool_sum(
                    *down_project(p_scalar, blocks, down_matrix, g * width, width)
                )
                out = place(
                    t_scalar, p_scalar, pieces, out, (batches, row_count, columns), m, start, g * width
                )
        else:
            here = by_index(jnp.stack(blocks), tp_index).reshape(rows, -1)
            partial = jnp.dot(here, down_matrix, preferred_element_type=F32)
            outputs.append(lax.psum(partial, "pool").astype(BF16))
    if out is not None:
        return out
    return jnp.concatenate(outputs, axis=0).reshape(batches, row_count, columns)


def solution(mesh):
    in_specs = (
        P(None, None, "tp"),
        P("tp", "pool"),
        P("tp", "pool"),
        P("pool", "tp"),
        P("pool", None, "tp"),
        P("pool", "tp", None),
        P(),
        P(),
    )
    return jax.shard_map(
        on_device, mesh=mesh, in_specs=in_specs, out_specs=P(None, None, "tp"), check_vma=False
    )
```

time: 241 us -> 204 us (0.85)
  waiting for transfers between devices: 106 us -> 68.3 us
  starting transfers between devices: 31.6 us -> 64.7 us
  Pallas kernels: 69 us -> 55.5 us
  blocking collectives: 8.67 us -> 0 us
  other arithmetic: 12.3 us -> 8.04 us
  matrix products: 3.35 us -> 0 us
  between operations: 3.91 us -> 0.59 us
    ppermute x26 -> x41, starting transfers between devices: 15.6 us -> 55.4 us  [exchange(): lax.ppermute(x, axis, [(i, i ^ bit) for i in range(lax.axis_size(axis))])]
    ppermute x26 -> x41, waiting for transfers between devices: 98.2 us -> 68.3 us  [exchange(): lax.ppermute(x, axis, [(i, i ^ bit) for i in range(lax.axis_size(axis))])]
    pallas_call x4 -> x3, Pallas kernels: 41.2 us -> 29.8 us  [project(): pl.pallas_call(body, grid_spec=pltpu.PrefetchScalarGridSpec(num_scalar_pr...]
    all_to_all x1 -> x0, blocking collectives: 8.67 us -> none  [on_device(): lax.all_to_all(low, 'tp', split_axis=0, concat_axis=0, tiled=True)]
    all_to_all x3 -> x2, waiting for transfers between devices: 8.01 us -> 0.01 us  [across(): return lax.all_to_all(x, 'pool', split_axis=0, concat_axis=0, tiled=True)]
    all_to_all x3 -> x2, starting transfers between devices: 15.9 us -> 9.31 us  [across(): return lax.all_to_all(x, 'pool', split_axis=0, concat_axis=0, tiled=True)]
    convert_element_type x10 -> x14, other arithmetic: 6.1 us -> 0.62 us  [the longest x8 0.29 us: pool_sum(): send = sum((x[1::2].astype(F32) for x in terms)).astype(BF16)]
    squeeze x0 -> x1, other arithmetic: none -> 4.17 us  [scatter_sum(): terms = [x[:, 0] for x in terms]]
  transfers between devices with their start and end apart: 29 -> 43, of which waited for: 17 -> 24; matrix products, arithmetic and copies ran while one was open for 4% -> 5% of each run, Pallas kernels for 28% -> 18%
where the time goes in v2:
time: 204 us; the launch traced here: 203 us
  waiting for transfers between devices  68.3 us (33%)
  starting transfers between devices  64.7 us (32%)
  Pallas kernels  55.5 us (27%)
  other arithmetic  8.04 us (4%)
  local copies, waits for them, and re-layouts  6.3 us (3%)
    ppermute x41, waiting for transfers between devices, exchange(): lax.ppermute(x, axis, [(i, i ^ bit) for i in range(lax.axis_size(axis))])  68.3 us
    ppermute x41, starting transfers between devices, exchange(): lax.ppermute(x, axis, [(i, i ^ bit) for i in range(lax.axis_size(axis))])  55.4 us
    pallas_call x3, Pallas kernels, project(): pl.pallas_call(body, grid_spec=pltpu.PrefetchScalarGridSpec(num_scalar_pr...  29.8 us
    pallas_call x4, Pallas kernels, down_project(): pl.pallas_call(body, grid_spec=pltpu.PrefetchScalarGridSpec(num_scalar_pr...  17.8 us
    all_to_all x2, starting transfers between devices, across(): return lax.all_to_all(x, 'pool', split_axis=0, concat_axis=0, tiled=True)  9.31 us
    squeeze x1, other arithmetic, scatter_sum(): terms = [x[:, 0] for x in terms]  4.17 us
  transfers between devices with their start and end apart: 43, of which 24 were waited for; matrix products, arithmetic and copies ran while one was open for 5% of the time, Pallas kernels for 18%

profile of v2, /device:TPU:0, one launch (start us, length us, event | category | flops | bytes accessed | tf_op | source)
XLA Modules:
  0.0 203.4 jit_solution(1133007787328898197)
XLA Ops:
  0.0 2.0 %copy-done.1 = bf16[4,16,28672]{2,1,0:T(8,128)(2,1)S(1)} copy-done((bf16[4,16,28672]{2,1,0:T(8,128)(2,1)S(1)}, bf16[4,16,28672]{2,1,0:T(8,128)(2,1)}, u32[]{:S(2)}) %copy-start.1) | copy-done | bytes 3670040
  3.4 2.9 %pick_pages.1 = (s32[2]{0:T(128)S(1)}, f32[2,1,256]{2,1,0:T(1,128)S(1)}, bf16[8,16,3584]{2,1,0:T(8,128)(2,1)S(1)}, bf16[8,16,3584]{2,1,0:T(8,128)(2,1)S(1)}) custom-call(s32[1]{0:T(128)} %bitcast.1.p_ref, s32[32]{0:T(128)S(1)} %copy-done.6, s32[2,256]{1,0:T(2,128)S(1)} %copy-done.5, bf16[4,16,28672]{2,1,0:T(8,128)(2,1)S(1)} %copy-done.1), custom_call_target="tpu_custom_call" | custom-call | tf_op jit(solution)/shard_map/pick_pages/pallas_call | solution.py:55
  9.3 2.9 %collective-permute-start.1 = (f32[1,1,16,512]{3,2,1,0:T(8,128)S(1)}, f32[1,1,16,512]{3,2,1,0:T(8,128)S(1)}, u32[]{:S(2)}, u32[]{:S(2)}) collective-permute-start(f32[1,1,16,512]{3,2,1,0:T(8,128)S(1)} %slice_add_fusion.9), channel_id=1, source_target_pairs={{0,2},{1,3},{2,0},{3,1},{4,6},{5,7},{6,4},{7,5},{8,10},{9,11},{10,... | collective-permute-start | bytes 98312 | tf_op jit(solution)/shard_map/ppermute | solution.py:19
  12.2 1.9 collective-permute-done.1
  14.1 12.6 %gate.1 = (f32[2,2,64,3584]{3,2,1,0:T(8,128)}, bf16[2,2,64,3584]{3,2,1,0:T(8,128)(2,1)S(1)}) custom-call(s32[1]{0:T(128)} %bitcast.t_ref, bf16[2,256,2048]{2,1,0:T(8,128)(2,1)S(1)} %copy-done, bf16[2,256,2048]{2,1,0:T(8,128)(2,1)S(1)} %copy-done, bf16[2,256,2048]{2,1,0:T(8,128)(2,1)S(1)} %copy-done, bf16[2,256,2048]{2,1,0:T(8,128)(2,1)S(1)} %copy-done, ...), custom_call_target="tpu_custom_call" | custom-call | flops 7516192768 | bytes 14680064 | tf_op jit(solution)/shard_map/gate/pallas_call | solution.py:157
  28.1 2.0 collective-permute-start.3
  30.1 4.9 %all-to-all-start = ((bf16[8,16,3584]{2,1,0:T(8,128)(2,1)}), bf16[8,16,3584]{2,1,0:T(8,128)(2,1)S(1)}, u32[]{:S(2)}, u32[]{:S(2)}) async-start(bf16[8,16,3584]{2,1,0:T(8,128)(2,1)} %copy-done.4), calls=%async_computation | async-start | bytes 1835008 | tf_op jit(solution)/shard_map/all_to_all | solution.py:337
  35.0 4.2 %slice_bitcast_fusion = (f32[2,64,3584]{2,1,0:T(8,128)}, bf16[2,1,64,3584]{3,2,0,1:T(8,128)(2,1)}) fusion(bf16[2,2,64,3584]{3,2,0,1:T(8,128)(2,1)} %collective-permute-done.2, f32[2,2,64,3584]{3,2,1,0:T(8,128)} %get-tuple-element.46), kind=kLoop, calls=%fused_computation | loop fusion | flops 1376256 | bytes 7340032 | tf_op jit(solution)/shard_map/squeeze | solution.py:186
  39.1 2.0 collective-permute-start.4
  41.2 10.4 %collective-permute-done.4 = bf16[2,16,512]{2,1,0:T(8,128)(2,1)S(1)} collective-permute-done((bf16[2,16,512]{2,1,0:T(8,128)(2,1)S(1)}, bf16[2,16,512]{2,1,0:T(8,128)(2,1)S(1)}, u32[]{:S(2)}, u32[]{:S(2)}) %collective-permute-start.4) | collective-permute-done | bytes 32800 | tf_op jit(solution)/shard_map/ppermute | solution.py:19
  51.5 4.1 %collective-permute-start.5 = (bf16[4,16,512]{2,1,0:T(8,128)(2,1)S(1)}, bf16[4,16,512]{2,1,0:T(8,128)(2,1)S(1)}, u32[]{:S(2)}, u32[]{:S(2)}) collective-permute-start(bf16[4,16,512]{2,1,0:T(8,128)(2,1)S(1)} %pad_maximum_fusion.9), channel_id=1, source_target_pairs={{0,16},{4,20},{8,24},{12,28},{16,0},{20,4},{24,8},{28,12},{1,17},{... | collective-permute-start | bytes 196616 | tf_op jit(solution)/shard_map/ppermute | solution.py:19
  57.2 3.9 %collective-permute-done.5 = bf16[4,16,512]{2,1,0:T(8,128)(2,1)S(1)} collective-permute-done((bf16[4,16,512]{2,1,0:T(8,128)(2,1)S(1)}, bf16[4,16,512]{2,1,0:T(8,128)(2,1)S(1)}, u32[]{:S(2)}, u32[]{:S(2)}) %collective-permute-start.5) | collective-permute-done | bytes 65568 | tf_op jit(solution)/shard_map/ppermute | solution.py:19
  61.4 4.4 %all-to-all-start.1 = ((bf16[8,16,3584]{2,1,0:T(8,128)(2,1)}), bf16[8,16,3584]{2,1,0:T(8,128)(2,1)}, u32[]{:S(2)}, u32[]{:S(2)}) async-start(bf16[8,16,3584]{2,1,0:T(8,128)(2,1)} %copy-done.3), calls=%async_computation.1 | async-start | bytes 1835008 | tf_op jit(solution)/shard_map/all_to_all | solution.py:337
  65.8 8.6 %up.2 = (f32[1,2,64,3584]{3,2,1,0:T(8,128)S(1)}, bf16[1,2,64,3584]{3,2,1,0:T(8,128)(2,1)S(1)}) custom-call(s32[1]{0:T(128)} %bitcast.t_ref, bf16[2,256,2048]{2,1,0:T(8,128)(2,1)S(1)} %copy-done, bf16[2,256,2048]{2,1,0:T(8,128)(2,1)S(1)} %copy-done, bf16[2,256,2048]{2,1,0:T(8,128)(2,1)S(1)} %copy-done, bf16[2,256,2048]{2,1,0:T(8,128)(2,1)S(1)} %copy-done, ...), custom_call_target="tpu_custom_call" | custom-call | flops 3758096384 | bytes 14680064 | tf_op jit(solution)/shard_map/up/pallas_call | solution.py:157
  77.1 1.5 collective-permute-start.8
  78.6 11.0 %collective-permute-done.8 = bf16[1,1,64,3584]{3,2,1,0:T(8,128)(2,1)S(1)} collective-permute-done((bf16[1,1,64,3584]{3,2,1,0:T(8,128)(2,1)S(1)}, bf16[1,1,64,3584]{3,2,1,0:T(8,128)(2,1)S(1)}, u32[]{:S(2)}, u32[]{:S(2)}) %collective-permute-start.8) | collective-permute-done | bytes 458784 | tf_op jit(solution)/shard_map/ppermute | solution.py:19
  91.1 1.6 collective-permute-start.27
  92.7 8.6 %up.3 = (f32[1,2,64,3584]{3,2,1,0:T(8,128)S(1)}, bf16[1,2,64,3584]{3,2,1,0:T(8,128)(2,1)S(1)}) custom-call(s32[1]{0:T(128)} %bitcast.t_ref, bf16[2,256,2048]{2,1,0:T(8,128)(2,1)S(1)} %copy-done, bf16[2,256,2048]{2,1,0:T(8,128)(2,1)S(1)} %copy-done, bf16[2,256,2048]{2,1,0:T(8,128)(2,1)S(1)} %copy-done, bf16[2,256,2048]{2,1,0:T(8,128)(2,1)S(1)} %copy-done, ...), custom_call_target="tpu_custom_call" | custom-call | flops 3758096384 | bytes 14680064 | tf_op jit(solution)/shard_map/up/pallas_call | solution.py:157
  103.0 1.6 collective-permute-done.26.refs_1_
  105.2 4.5 %down.7 = (f32[4,32,1024]{2,1,0:T(8,128)S(1)}, bf16[4,32,1024]{2,1,0:T(8,128)(2,1)S(1)}) custom-call(s32[1]{0:T(128)} %bitcast.1.p_ref, bf16[64,3584]{1,0:T(8,128)(2,1)S(1)} %fusion.5.refs_0_, bf16[64,3584]{1,0:T(8,128)(2,1)S(1)} %collective-permute-done.26.refs_1_, bf16[64,3584]{1,0:T(8,128)(2,1)S(1)} %collective-permute-done.27.refs_2_, ...), custom_call_target="tpu_custom_call" | custom-call | flops 1879048192 | bytes 7340032 | tf_op jit(solution)/shard_map/down/pallas_call | solution.py:232
  109.7 1.8 collective-permute-start.35
  111.5 4.5 %down.6 = (f32[4,32,1024]{2,1,0:T(8,128)S(1)}, bf16[4,32,1024]{2,1,0:T(8,128)(2,1)S(1)}) custom-call(s32[1]{0:T(128)} %bitcast.1.p_ref, bf16[64,3584]{1,0:T(8,128)(2,1)S(1)} %fusion.5.refs_0_, bf16[64,3584]{1,0:T(8,128)(2,1)S(1)} %collective-permute-done.26.refs_1_, bf16[64,3584]{1,0:T(8,128)(2,1)S(1)} %collective-permute-done.27.refs_2_, ...), custom_call_target="tpu_custom_call" | custom-call | flops 1879048192 | bytes 7340032 | tf_op jit(solution)/shard_map/down/pallas_call | solution.py:232
  118.2 1.8 collective-permute-start.36
  119.9 4.1 %collective-permute-done.29 = bf16[4,32,1024]{2,1,0:T(8,128)(2,1)S(1)} collective-permute-done((bf16[4,32,1024]{2,1,0:T(8,128)(2,1)S(1)}, bf16[4,32,1024]{2,1,0:T(8,128)(2,1)S(1)}, u32[]{:S(2)}, u32[]{:S(2)}) %collective-permute-start.29) | collective-permute-done | bytes 262176 | tf_op jit(solution)/shard_map/ppermute | solution.py:19
  124.1 1.5 collective-permute-start.30
  125.7 2.5 %collective-permute-start.37 = (bf16[1,32,1024]{2,1,0:T(8,128)(2,1)S(1)}, bf16[1,32,1024]{2,1,0:T(8,128)(2,1)S(1)}, u32[]{:S(2)}, u32[]{:S(2)}) collective-permute-start(bf16[1,32,1024]{2,1,0:T(8,128)(2,1)S(1)} %fusion.10), channel_id=1, source_target_pairs={{0,16},{4,20},{8,24},{12,28},{16,0},{20,4},{24,8},{28,12},{1,17},{... | collective-permute-start | bytes 196616 | tf_op jit(solution)/shard_map/ppermute | solution.py:19
  131.2 2.7 %collective-permute-start.31 = (bf16[1,32,1024]{2,1,0:T(8,128)(2,1)S(1)}, bf16[1,32,1024]{2,1,0:T(8,128)(2,1)S(1)}, u32[]{:S(2)}, u32[]{:S(2)}) collective-permute-start(bf16[1,32,1024]{2,1,0:T(8,128)(2,1)S(1)} %fusion.15), channel_id=1, source_target_pairs={{0,16},{4,20},{8,24},{12,28},{16,0},{20,4},{24,8},{28,12},{1,17},{... | collective-permute-start | bytes 196616 | tf_op jit(solution)/shard_map/ppermute | solution.py:19
  134.3 6.9 %collective-permute-done.12.refs_2_ = bf16[64,3584]{1,0:T(8,128)(2,1)S(1)} collective-permute-done((bf16[64,3584]{1,0:T(8,128)(2,1)S(1)}, bf16[64,3584]{1,0:T(8,128)(2,1)S(1)}, u32[]{:S(2)}, u32[]{:S(2)}) %collective-permute-start.12) | collective-permute-done | bytes 458784 | tf_op jit(solution)/shard_map/ppermute | solution.py:19
  141.2 2.7 %collective-permute-start.32 = (bf16[1,32,1024]{2,1,0:T(8,128)(2,1)S(1)}, bf16[1,32,1024]{2,1,0:T(8,128)(2,1)S(1)}, u32[]{:S(2)}, u32[]{:S(2)}) collective-permute-start(bf16[1,32,1024]{2,1,0:T(8,128)(2,1)S(1)} %fusion.18.refs_0_), channel_id=1, source_target_pairs={{0,16},{4,20},{8,24},{12,28},{16,0},{20,4},{24,8},{28,12},{1,17},{... | collective-permute-start | bytes 196616 | tf_op jit(solution)/shard_map/ppermute | solution.py:19
  143.9 1.5 collective-permute-start.39
  145.5 2.4 %collective-permute-done.32.refs_1_ = bf16[1,32,1024]{2,1,0:T(8,128)(2,1)S(1)} collective-permute-done((bf16[1,32,1024]{2,1,0:T(8,128)(2,1)S(1)}, bf16[1,32,1024]{2,1,0:T(8,128)(2,1)S(1)}, u32[]{:S(2)}, u32[]{:S(2)}) %collective-permute-start.32) | collective-permute-done | bytes 65568 | tf_op jit(solution)/shard_map/ppermute | solution.py:19
  149.0 4.5 %down.5 = (f32[4,32,1024]{2,1,0:T(8,128)S(1)}, bf16[4,32,1024]{2,1,0:T(8,128)(2,1)S(1)}) custom-call(s32[1]{0:T(128)} %bitcast.1.p_ref, bf16[64,3584]{1,0:T(8,128)(2,1)S(1)} %fusion.1.refs_0_, bf16[64,3584]{1,0:T(8,128)(2,1)S(1)} %collective-permute-done.11.refs_1_, bf16[64,3584]{1,0:T(8,128)(2,1)S(1)} %collective-permute-done.12.refs_2_, ...), custom_call_target="tpu_custom_call" | custom-call | flops 1879048192 | bytes 7340032 | tf_op jit(solution)/shard_map/down/pallas_call | solution.py:232
  153.4 1.5 collective-permute-start.20
  155.0 4.5 %down.4 = (f32[4,32,1024]{2,1,0:T(8,128)S(1)}, bf16[4,32,1024]{2,1,0:T(8,128)(2,1)S(1)}) custom-call(s32[1]{0:T(128)} %bitcast.1.p_ref, bf16[64,3584]{1,0:T(8,128)(2,1)S(1)} %fusion.1.refs_0_, bf16[64,3584]{1,0:T(8,128)(2,1)S(1)} %collective-permute-done.11.refs_1_, bf16[64,3584]{1,0:T(8,128)(2,1)S(1)} %collective-permute-done.12.refs_2_, ...), custom_call_target="tpu_custom_call" | custom-call | flops 1879048192 | bytes 7340032 | tf_op jit(solution)/shard_map/down/pallas_call | solution.py:232
  160.1 1.5 collective-permute-start.40
  161.7 1.7 collective-permute-start.21
  163.3 5.4 %collective-permute-done.14 = bf16[4,32,1024]{2,1,0:T(8,128)(2,1)S(1)} collective-permute-done((bf16[4,32,1024]{2,1,0:T(8,128)(2,1)S(1)}, bf16[4,32,1024]{2,1,0:T(8,128)(2,1)S(1)}, u32[]{:S(2)}, u32[]{:S(2)}) %collective-permute-start.14) | collective-permute-done | bytes 262176 | tf_op jit(solution)/shard_map/ppermute | solution.py:19
  168.8 1.7 collective-permute-start.15
  170.5 1.9 collective-permute-start.22
  173.8 3.5 %collective-permute-start.16 = (bf16[1,32,1024]{2,1,0:T(8,128)(2,1)S(1)}, bf16[1,32,1024]{2,1,0:T(8,128)(2,1)S(1)}, u32[]{:S(2)}, u32[]{:S(2)}) collective-permute-start(bf16[1,32,1024]{2,1,0:T(8,128)(2,1)S(1)} %fusion.25), channel_id=1, source_target_pairs={{0,16},{4,20},{8,24},{12,28},{16,0},{20,4},{24,8},{28,12},{1,17},{... | collective-permute-start | bytes 196616 | tf_op jit(solution)/shard_map/ppermute | solution.py:19
  178.4 3.1 %collective-permute-done.16 = bf16[1,32,1024]{2,1,0:T(8,128)(2,1)S(1)} collective-permute-done((bf16[1,32,1024]{2,1,0:T(8,128)(2,1)S(1)}, bf16[1,32,1024]{2,1,0:T(8,128)(2,1)S(1)}, u32[]{:S(2)}, u32[]{:S(2)}) %collective-permute-start.16) | collective-permute-done | bytes 65568 | tf_op jit(solution)/shard_map/ppermute | solution.py:19
  183.1 1.7 collective-permute-start.24
  184.9 2.7 %collective-permute-done.17.refs_1_ = bf16[1,32,1024]{2,1,0:T(8,128)(2,1)S(1)} collective-permute-done((bf16[1,32,1024]{2,1,0:T(8,128)(2,1)S(1)}, bf16[1,32,1024]{2,1,0:T(8,128)(2,1)S(1)}, u32[]{:S(2)}, u32[]{:S(2)}) %collective-permute-start.17) | collective-permute-done | bytes 65568 | tf_op jit(solution)/shard_map/ppermute | solution.py:19
  188.6 1.9 collective-permute-start.25
  190.5 2.1 %collective-permute-done.18.refs_2_ = bf16[2,32,1024]{2,1,0:T(8,128)(2,1)S(1)} collective-permute-done((bf16[2,32,1024]{2,1,0:T(8,128)(2,1)S(1)}, bf16[2,32,1024]{2,1,0:T(8,128)(2,1)S(1)}, u32[]{:S(2)}, u32[]{:S(2)}) %collective-permute-start.18) | collective-permute-done | bytes 131104 | tf_op jit(solution)/shard_map/ppermute | solution.py:19
  194.2 2.5 %collective-permute-done.34.refs_3_ = bf16[4,32,1024]{2,1,0:T(8,128)(2,1)S(1)} collective-permute-done((bf16[4,32,1024]{2,1,0:T(8,128)(2,1)S(1)}, bf16[4,32,1024]{2,1,0:T(8,128)(2,1)S(1)}, u32[]{:S(2)}, u32[]{:S(2)}) %collective-permute-start.34) | collective-permute-done | bytes 262176 | tf_op jit(solution)/shard_map/ppermute | solution.py:19
  197.6 2.0 collective-permute-done.25.refs_3_
  200.4 2.0 collective-permute-done.19.refs_3_
  (113 shorter events, 30.6 us)
Async XLA Ops:
  6.3 20.4 %copy-start.3 = (bf16[8,16,3584]{2,1,0:T(8,128)(2,1)}, bf16[8,16,3584]{2,1,0:T(8,128)(2,1)S(1)}, u32[]{:S(2)}) copy-start(bf16[8,16,3584]{2,1,0:T(8,128)(2,1)S(1)} %get-tuple-element.60) | copy-start | bytes 2752516
  6.3 20.4 %copy-start.4 = (bf16[8,16,3584]{2,1,0:T(8,128)(2,1)}, bf16[8,16,3584]{2,1,0:T(8,128)(2,1)S(1)}, u32[]{:S(2)}) copy-start(bf16[8,16,3584]{2,1,0:T(8,128)(2,1)S(1)} %get-tuple-element.51) | copy-start | bytes 2752516
  7.9 1.4 collective-permute-start
  9.3 4.8 %collective-permute-start.1 = (f32[1,1,16,512]{3,2,1,0:T(8,128)S(1)}, f32[1,1,16,512]{3,2,1,0:T(8,128)S(1)}, u32[]{:S(2)}, u32[]{:S(2)}) collective-permute-start(f32[1,1,16,512]{3,2,1,0:T(8,128)S(1)} %slice_add_fusion.9), channel_id=1, source_target_pairs={{0,2},{1,3},{2,0},{3,1},{4,6},{5,7},{6,4},{7,5},{8,10},{9,11},{10,... | collective-permute-start | bytes 98312 | tf_op jit(solution)/shard_map/ppermute | solution.py:19
  28.1 6.9 %collective-permute-start.2 = (bf16[2,2,64,3584]{3,2,0,1:T(8,128)(2,1)}, bf16[2,2,64,3584]{3,2,0,1:T(8,128)(2,1)}, u32[]{:S(2)}, u32[]{:S(2)}) collective-permute-start(bf16[2,2,64,3584]{3,2,0,1:T(8,128)(2,1)} %copy.17), channel_id=1, source_target_pairs={{0,1},{1,0},{2,3},{3,2},{4,5},{5,4},{6,7},{7,6},{8,9},{9,8},{10,11... | collective-permute-start | bytes 5505032 | tf_op jit(solution)/shard_map/ppermute | solution.py:19
  28.1 6.9 %collective-permute-start.3 = (bf16[1,16,512]{2,1,0:T(8,128)(2,1)S(1)}, bf16[1,16,512]{2,1,0:T(8,128)(2,1)S(1)}, u32[]{:S(2)}, u32[]{:S(2)}) collective-permute-start(bf16[1,16,512]{2,1,0:T(8,128)(2,1)S(1)} %fusion.32), channel_id=1, source_target_pairs={{0,4},{4,0},{8,12},{12,8},{16,20},{20,16},{24,28},{28,24},{1,5},{5... | collective-permute-start | bytes 49160 | tf_op jit(solution)/shard_map/ppermute | solution.py:19
  30.1 31.3 %all-to-all-start = ((bf16[8,16,3584]{2,1,0:T(8,128)(2,1)}), bf16[8,16,3584]{2,1,0:T(8,128)(2,1)S(1)}, u32[]{:S(2)}, u32[]{:S(2)}) async-start(bf16[8,16,3584]{2,1,0:T(8,128)(2,1)} %copy-done.4), calls=%async_computation | async-start | bytes 1835008 | tf_op jit(solution)/shard_map/all_to_all | solution.py:337
  39.1 12.4 %collective-permute-start.4 = (bf16[2,16,512]{2,1,0:T(8,128)(2,1)S(1)}, bf16[2,16,512]{2,1,0:T(8,128)(2,1)S(1)}, u32[]{:S(2)}, u32[]{:S(2)}) collective-permute-start(bf16[2,16,512]{2,1,0:T(8,128)(2,1)S(1)} %pad_maximum_fusion.10), channel_id=1, source_target_pairs={{0,8},{4,12},{8,0},{12,4},{16,24},{20,28},{24,16},{28,20},{1,9},{5... | collective-permute-start | bytes 98312 | tf_op jit(solution)/shard_map/ppermute | solution.py:19
  51.5 9.5 %collective-permute-start.5 = (bf16[4,16,512]{2,1,0:T(8,128)(2,1)S(1)}, bf16[4,16,512]{2,1,0:T(8,128)(2,1)S(1)}, u32[]{:S(2)}, u32[]{:S(2)}) collective-permute-start(bf16[4,16,512]{2,1,0:T(8,128)(2,1)S(1)} %pad_maximum_fusion.9), channel_id=1, source_target_pairs={{0,16},{4,20},{8,24},{12,28},{16,0},{20,4},{24,8},{28,12},{1,17},{... | collective-permute-start | bytes 196616 | tf_op jit(solution)/shard_map/ppermute | solution.py:19
  55.7 21.4 %collective-permute-start.7 = (bf16[2,1,64,3584]{3,2,0,1:T(8,128)(2,1)}, bf16[2,1,64,3584]{3,2,0,1:T(8,128)(2,1)}, u32[]{:S(2)}, u32[]{:S(2)}) collective-permute-start(bf16[2,1,64,3584]{3,2,0,1:T(8,128)(2,1)} %get-tuple-element.54), channel_id=1, source_target_pairs={{0,2},{1,3},{2,0},{3,1},{4,6},{5,7},{6,4},{7,5},{8,10},{9,11},{10,... | collective-permute-start | bytes 2752520 | tf_op jit(solution)/shard_map/ppermute | solution.py:19
  61.4 31.4 %all-to-all-start.1 = ((bf16[8,16,3584]{2,1,0:T(8,128)(2,1)}), bf16[8,16,3584]{2,1,0:T(8,128)(2,1)}, u32[]{:S(2)}, u32[]{:S(2)}) async-start(bf16[8,16,3584]{2,1,0:T(8,128)(2,1)} %copy-done.3), calls=%async_computation.1 | async-start | bytes 1835008 | tf_op jit(solution)/shard_map/all_to_all | solution.py:337
  74.4 15.3 %copy-start.7 = (f32[2,64,3584]{2,1,0:T(8,128)S(1)}, f32[2,64,3584]{2,1,0:T(8,128)}, u32[]{:S(2)}) copy-start(f32[2,64,3584]{2,1,0:T(8,128)} %get-tuple-element.63) | copy-start | bytes 5505028
  74.4 2.5 %collective-permute-start.6 = (bf16[1,2,64,3584]{3,2,1,0:T(8,128)(2,1)S(1)}, bf16[1,2,64,3584]{3,2,1,0:T(8,128)(2,1)S(1)}, u32[]{:S(2)}, u32[]{:S(2)}) collective-permute-start(bf16[1,2,64,3584]{3,2,1,0:T(8,128)(2,1)S(1)} %get-tuple-element.53), channel_id=1, source_target_pairs={{0,1},{1,0},{2,3},{3,2},{4,5},{5,4},{6,7},{7,6},{8,9},{9,8},{10,11... | collective-permute-start | bytes 2752520 | tf_op jit(solution)/shard_map/ppermute | solution.py:19
  75.9 15.3 %copy-start.9 = (bf16[2,64,3584]{2,1,0:T(8,128)(2,1)}, bf16[2,64,3584]{2,1,0:T(8,128)(2,1)S(1)}, u32[]{:S(2)}) copy-start(bf16[2,64,3584]{2,1,0:T(8,128)(2,1)S(1)} %slice_bitcast_fusion.1) | copy-start | bytes 2752516
  77.1 12.6 %collective-permute-start.8 = (bf16[1,1,64,3584]{3,2,1,0:T(8,128)(2,1)S(1)}, bf16[1,1,64,3584]{3,2,1,0:T(8,128)(2,1)S(1)}, u32[]{:S(2)}, u32[]{:S(2)}) collective-permute-start(bf16[1,1,64,3584]{3,2,1,0:T(8,128)(2,1)S(1)} %add_convert_fusion.1), channel_id=1, source_target_pairs={{0,2},{1,3},{2,0},{3,1},{4,6},{5,7},{6,4},{7,5},{8,10},{9,11},{10,... | collective-permute-start | bytes 1376264 | tf_op jit(solution)/shard_map/ppermute | solution.py:19
  91.1 11.8 %collective-permute-start.27 = (bf16[64,3584]{1,0:T(8,128)(2,1)S(1)}, bf16[64,3584]{1,0:T(8,128)(2,1)S(1)}, u32[]{:S(2)}, u32[]{:S(2)}) collective-permute-start(bf16[64,3584]{1,0:T(8,128)(2,1)S(1)} %fusion.5.refs_0_), channel_id=1, source_target_pairs={{0,2},{1,3},{2,0},{3,1},{4,6},{5,7},{6,4},{7,5},{8,10},{9,11},{10,... | collective-permute-start | bytes 1376264 | tf_op jit(solution)/shard_map/ppermute | solution.py:19
  101.4 14.9 %collective-permute-start.9 = (bf16[1,2,64,3584]{3,2,1,0:T(8,128)(2,1)S(1)}, bf16[1,2,64,3584]{3,2,1,0:T(8,128)(2,1)S(1)}, u32[]{:S(2)}, u32[]{:S(2)}) collective-permute-start(bf16[1,2,64,3584]{3,2,1,0:T(8,128)(2,1)S(1)} %get-tuple-element.62), channel_id=1, source_target_pairs={{0,1},{1,0},{2,3},{3,2},{4,5},{5,4},{6,7},{7,6},{8,9},{9,8},{10,11... | collective-permute-start | bytes 2752520 | tf_op jit(solution)/shard_map/ppermute | solution.py:19
  101.5 3.1 %collective-permute-start.26 = (bf16[64,3584]{1,0:T(8,128)(2,1)S(1)}, bf16[64,3584]{1,0:T(8,128)(2,1)S(1)}, u32[]{:S(2)}, u32[]{:S(2)}) collective-permute-start(bf16[64,3584]{1,0:T(8,128)(2,1)S(1)} %fusion.5.refs_0_), channel_id=1, source_target_pairs={{0,1},{1,0},{2,3},{3,2},{4,5},{5,4},{6,7},{7,6},{8,9},{9,8},{10,11... | collective-permute-start | bytes 1376264 | tf_op jit(solution)/shard_map/ppermute | solution.py:19
  102.9 2.3 %collective-permute-start.28 = (bf16[64,3584]{1,0:T(8,128)(2,1)S(1)}, bf16[64,3584]{1,0:T(8,128)(2,1)S(1)}, u32[]{:S(2)}, u32[]{:S(2)}) collective-permute-start(bf16[64,3584]{1,0:T(8,128)(2,1)S(1)} %collective-permute-done.27.refs_2_), channel_id=1, source_target_pairs={{0,1},{1,0},{2,3},{3,2},{4,5},{5,4},{6,7},{7,6},{8,9},{9,8},{10,11... | collective-permute-start | bytes 1376264 | tf_op jit(solution)/shard_map/ppermute | solution.py:19
  109.7 8.4 %collective-permute-start.35 = (bf16[4,32,1024]{2,1,0:T(8,128)(2,1)S(1)}, bf16[4,32,1024]{2,1,0:T(8,128)(2,1)S(1)}, u32[]{:S(2)}, u32[]{:S(2)}) collective-permute-start(bf16[4,32,1024]{2,1,0:T(8,128)(2,1)S(1)} %get-tuple-element.76), channel_id=1, source_target_pairs={{0,4},{4,0},{8,12},{12,8},{16,20},{20,16},{24,28},{28,24},{1,5},{5... | collective-permute-start | bytes 786440 | tf_op jit(solution)/shard_map/ppermute | solution.py:19
  115.9 8.1 %collective-permute-start.29 = (bf16[4,32,1024]{2,1,0:T(8,128)(2,1)S(1)}, bf16[4,32,1024]{2,1,0:T(8,128)(2,1)S(1)}, u32[]{:S(2)}, u32[]{:S(2)}) collective-permute-start(bf16[4,32,1024]{2,1,0:T(8,128)(2,1)S(1)} %get-tuple-element.74), channel_id=1, source_target_pairs={{0,4},{4,0},{8,12},{12,8},{16,20},{20,16},{24,28},{28,24},{1,5},{5... | collective-permute-start | bytes 786440 | tf_op jit(solution)/shard_map/ppermute | solution.py:19
  116.4 12.1 %copy-start.8 = (f32[2,64,3584]{2,1,0:T(8,128)S(1)}, f32[2,64,3584]{2,1,0:T(8,128)}, u32[]{:S(2)}) copy-start(f32[2,64,3584]{2,1,0:T(8,128)} %get-tuple-element.63) | copy-start | bytes 5505028
  116.5 12.1 %collective-permute-start.10 = (bf16[1,1,64,3584]{3,2,1,0:T(8,128)(2,1)S(1)}, bf16[1,1,64,3584]{3,2,1,0:T(8,128)(2,1)S(1)}, u32[]{:S(2)}, u32[]{:S(2)}) collective-permute-start(bf16[1,1,64,3584]{3,2,1,0:T(8,128)(2,1)S(1)} %add_convert_fusion), channel_id=1, source_target_pairs={{0,2},{1,3},{2,0},{3,1},{4,6},{5,7},{6,4},{7,5},{8,10},{9,11},{10,... | collective-permute-start | bytes 1376264 | tf_op jit(solution)/shard_map/ppermute | solution.py:19
  118.2 7.5 %collective-permute-start.36 = (bf16[2,32,1024]{2,1,0:T(8,128)(2,1)S(1)}, bf16[2,32,1024]{2,1,0:T(8,128)(2,1)S(1)}, u32[]{:S(2)}, u32[]{:S(2)}) collective-permute-start(bf16[2,32,1024]{2,1,0:T(8,128)(2,1)S(1)} %get-tuple-element.79), channel_id=1, source_target_pairs={{0,8},{4,12},{8,0},{12,4},{16,24},{20,28},{24,16},{28,20},{1,9},{5... | collective-permute-start | bytes 393224 | tf_op jit(solution)/shard_map/ppermute | solution.py:19
  124.1 7.0 %collective-permute-start.30 = (bf16[2,32,1024]{2,1,0:T(8,128)(2,1)S(1)}, bf16[2,32,1024]{2,1,0:T(8,128)(2,1)S(1)}, u32[]{:S(2)}, u32[]{:S(2)}) collective-permute-start(bf16[2,32,1024]{2,1,0:T(8,128)(2,1)S(1)} %get-tuple-element.81), channel_id=1, source_target_pairs={{0,8},{4,12},{8,0},{12,4},{16,24},{20,28},{24,16},{28,20},{1,9},{5... | collective-permute-start | bytes 393224 | tf_op jit(solution)/shard_map/ppermute | solution.py:19
  125.7 8.1 %collective-permute-start.37 = (bf16[1,32,1024]{2,1,0:T(8,128)(2,1)S(1)}, bf16[1,32,1024]{2,1,0:T(8,128)(2,1)S(1)}, u32[]{:S(2)}, u32[]{:S(2)}) collective-permute-start(bf16[1,32,1024]{2,1,0:T(8,128)(2,1)S(1)} %fusion.10), channel_id=1, source_target_pairs={{0,16},{4,20},{8,24},{12,28},{16,0},{20,4},{24,8},{28,12},{1,17},{... | collective-permute-start | bytes 196616 | tf_op jit(solution)/shard_map/ppermute | solution.py:19
  130.0 11.2 %collective-permute-start.12 = (bf16[64,3584]{1,0:T(8,128)(2,1)S(1)}, bf16[64,3584]{1,0:T(8,128)(2,1)S(1)}, u32[]{:S(2)}, u32[]{:S(2)}) collective-permute-start(bf16[64,3584]{1,0:T(8,128)(2,1)S(1)} %fusion.1.refs_0_), channel_id=1, source_target_pairs={{0,2},{1,3},{2,0},{3,1},{4,6},{5,7},{6,4},{7,5},{8,10},{9,11},{10,... | collective-permute-start | bytes 1376264 | tf_op jit(solution)/shard_map/ppermute | solution.py:19
  131.2 10.0 %collective-permute-start.31 = (bf16[1,32,1024]{2,1,0:T(8,128)(2,1)S(1)}, bf16[1,32,1024]{2,1,0:T(8,128)(2,1)S(1)}, u32[]{:S(2)}, u32[]{:S(2)}) collective-permute-start(bf16[1,32,1024]{2,1,0:T(8,128)(2,1)S(1)} %fusion.15), channel_id=1, source_target_pairs={{0,16},{4,20},{8,24},{12,28},{16,0},{20,4},{24,8},{28,12},{1,17},{... | collective-permute-start | bytes 196616 | tf_op jit(solution)/shard_map/ppermute | solution.py:19
  133.9 10.0 %collective-permute-start.38 = (bf16[1,32,1024]{2,1,0:T(8,128)(2,1)S(1)}, bf16[1,32,1024]{2,1,0:T(8,128)(2,1)S(1)}, u32[]{:S(2)}, u32[]{:S(2)}) collective-permute-start(bf16[1,32,1024]{2,1,0:T(8,128)(2,1)S(1)} %fusion.13.refs_0_), channel_id=1, source_target_pairs={{0,16},{4,20},{8,24},{12,28},{16,0},{20,4},{24,8},{28,12},{1,17},{... | collective-permute-start | bytes 196616 | tf_op jit(solution)/shard_map/ppermute | solution.py:19
  134.3 14.7 %collective-permute-start.11 = (bf16[64,3584]{1,0:T(8,128)(2,1)S(1)}, bf16[64,3584]{1,0:T(8,128)(2,1)S(1)}, u32[]{:S(2)}, u32[]{:S(2)}) collective-permute-start(bf16[64,3584]{1,0:T(8,128)(2,1)S(1)} %fusion.1.refs_0_), channel_id=1, source_target_pairs={{0,1},{1,0},{2,3},{3,2},{4,5},{5,4},{6,7},{7,6},{8,9},{9,8},{10,11... | collective-permute-start | bytes 1376264 | tf_op jit(solution)/shard_map/ppermute | solution.py:19
  141.2 7.8 %collective-permute-start.13 = (bf16[64,3584]{1,0:T(8,128)(2,1)S(1)}, bf16[64,3584]{1,0:T(8,128)(2,1)S(1)}, u32[]{:S(2)}, u32[]{:S(2)}) collective-permute-start(bf16[64,3584]{1,0:T(8,128)(2,1)S(1)} %collective-permute-done.12.refs_2_), channel_id=1, source_target_pairs={{0,1},{1,0},{2,3},{3,2},{4,5},{5,4},{6,7},{7,6},{8,9},{9,8},{10,11... | collective-permute-start | bytes 1376264 | tf_op jit(solution)/shard_map/ppermute | solution.py:19
  141.2 6.7 %collective-permute-start.32 = (bf16[1,32,1024]{2,1,0:T(8,128)(2,1)S(1)}, bf16[1,32,1024]{2,1,0:T(8,128)(2,1)S(1)}, u32[]{:S(2)}, u32[]{:S(2)}) collective-permute-start(bf16[1,32,1024]{2,1,0:T(8,128)(2,1)S(1)} %fusion.18.refs_0_), channel_id=1, source_target_pairs={{0,16},{4,20},{8,24},{12,28},{16,0},{20,4},{24,8},{28,12},{1,17},{... | collective-permute-start | bytes 196616 | tf_op jit(solution)/shard_map/ppermute | solution.py:19
  143.9 16.1 %collective-permute-start.39 = (bf16[2,32,1024]{2,1,0:T(8,128)(2,1)S(1)}, bf16[2,32,1024]{2,1,0:T(8,128)(2,1)S(1)}, u32[]{:S(2)}, u32[]{:S(2)}) collective-permute-start(bf16[2,32,1024]{2,1,0:T(8,128)(2,1)S(1)} %pad_maximum_fusion.8), channel_id=1, source_target_pairs={{0,8},{4,12},{8,0},{12,4},{16,24},{20,28},{24,16},{28,20},{1,9},{5... | collective-permute-start | bytes 393224 | tf_op jit(solution)/shard_map/ppermute | solution.py:19
  147.9 40.0 %collective-permute-start.33 = (bf16[2,32,1024]{2,1,0:T(8,128)(2,1)S(1)}, bf16[2,32,1024]{2,1,0:T(8,128)(2,1)S(1)}, u32[]{:S(2)}, u32[]{:S(2)}) collective-permute-start(bf16[2,32,1024]{2,1,0:T(8,128)(2,1)S(1)} %pad_maximum_fusion.7), channel_id=1, source_target_pairs={{0,8},{4,12},{8,0},{12,4},{16,24},{20,28},{24,16},{28,20},{1,9},{5... | collective-permute-start | bytes 393224 | tf_op jit(solution)/shard_map/ppermute | solution.py:19
  153.4 8.2 %collective-permute-start.20 = (bf16[4,32,1024]{2,1,0:T(8,128)(2,1)S(1)}, bf16[4,32,1024]{2,1,0:T(8,128)(2,1)S(1)}, u32[]{:S(2)}, u32[]{:S(2)}) collective-permute-start(bf16[4,32,1024]{2,1,0:T(8,128)(2,1)S(1)} %get-tuple-element.71), channel_id=1, source_target_pairs={{0,4},{4,0},{8,12},{12,8},{16,20},{20,16},{24,28},{28,24},{1,5},{5... | collective-permute-start | bytes 786440 | tf_op jit(solution)/shard_map/ppermute | solution.py:19
  159.4 9.3 %collective-permute-start.14 = (bf16[4,32,1024]{2,1,0:T(8,128)(2,1)S(1)}, bf16[4,32,1024]{2,1,0:T(8,128)(2,1)S(1)}, u32[]{:S(2)}, u32[]{:S(2)}) collective-permute-start(bf16[4,32,1024]{2,1,0:T(8,128)(2,1)S(1)} %get-tuple-element.69), channel_id=1, source_target_pairs={{0,4},{4,0},{8,12},{12,8},{16,20},{20,16},{24,28},{28,24},{1,5},{5... | collective-permute-start | bytes 786440 | tf_op jit(solution)/shard_map/ppermute | solution.py:19
  160.1 33.3 %collective-permute-start.40 = (bf16[4,32,1024]{2,1,0:T(8,128)(2,1)S(1)}, bf16[4,32,1024]{2,1,0:T(8,128)(2,1)S(1)}, u32[]{:S(2)}, u32[]{:S(2)}) collective-permute-start(bf16[4,32,1024]{2,1,0:T(8,128)(2,1)S(1)} %pad_maximum_fusion.3), channel_id=1, source_target_pairs={{0,4},{4,0},{8,12},{12,8},{16,20},{20,16},{24,28},{28,24},{1,5},{5... | collective-permute-start | bytes 786440 | tf_op jit(solution)/shard_map/ppermute | solution.py:19
  161.7 8.8 %collective-permute-start.21 = (bf16[2,32,1024]{2,1,0:T(8,128)(2,1)S(1)}, bf16[2,32,1024]{2,1,0:T(8,128)(2,1)S(1)}, u32[]{:S(2)}, u32[]{:S(2)}) collective-permute-start(bf16[2,32,1024]{2,1,0:T(8,128)(2,1)S(1)} %get-tuple-element.83), channel_id=1, source_target_pairs={{0,8},{4,12},{8,0},{12,4},{16,24},{20,28},{24,16},{28,20},{1,9},{5... | collective-permute-start | bytes 393224 | tf_op jit(solution)/shard_map/ppermute | solution.py:19
  168.8 5.0 %collective-permute-start.15 = (bf16[2,32,1024]{2,1,0:T(8,128)(2,1)S(1)}, bf16[2,32,1024]{2,1,0:T(8,128)(2,1)S(1)}, u32[]{:S(2)}, u32[]{:S(2)}) collective-permute-start(bf16[2,32,1024]{2,1,0:T(8,128)(2,1)S(1)} %get-tuple-element.85), channel_id=1, source_target_pairs={{0,8},{4,12},{8,0},{12,4},{16,24},{20,28},{24,16},{28,20},{1,9},{5... | collective-permute-start | bytes 393224 | tf_op jit(solution)/shard_map/ppermute | solution.py:19
  170.5 6.8 %collective-permute-start.22 = (bf16[1,32,1024]{2,1,0:T(8,128)(2,1)S(1)}, bf16[1,32,1024]{2,1,0:T(8,128)(2,1)S(1)}, u32[]{:S(2)}, u32[]{:S(2)}) collective-permute-start(bf16[1,32,1024]{2,1,0:T(8,128)(2,1)S(1)} %fusion.20), channel_id=1, source_target_pairs={{0,16},{4,20},{8,24},{12,28},{16,0},{20,4},{24,8},{28,12},{1,17},{... | collective-permute-start | bytes 196616 | tf_op jit(solution)/shard_map/ppermute | solution.py:19
  173.8 7.7 %collective-permute-start.16 = (bf16[1,32,1024]{2,1,0:T(8,128)(2,1)S(1)}, bf16[1,32,1024]{2,1,0:T(8,128)(2,1)S(1)}, u32[]{:S(2)}, u32[]{:S(2)}) collective-permute-start(bf16[1,32,1024]{2,1,0:T(8,128)(2,1)S(1)} %fusion.25), channel_id=1, source_target_pairs={{0,16},{4,20},{8,24},{12,28},{16,0},{20,4},{24,8},{28,12},{1,17},{... | collective-permute-start | bytes 196616 | tf_op jit(solution)/shard_map/ppermute | solution.py:19
  177.4 5.8 %collective-permute-start.23 = (bf16[1,32,1024]{2,1,0:T(8,128)(2,1)S(1)}, bf16[1,32,1024]{2,1,0:T(8,128)(2,1)S(1)}, u32[]{:S(2)}, u32[]{:S(2)}) collective-permute-start(bf16[1,32,1024]{2,1,0:T(8,128)(2,1)S(1)} %fusion.23.refs_0_), channel_id=1, source_target_pairs={{0,16},{4,20},{8,24},{12,28},{16,0},{20,4},{24,8},{28,12},{1,17},{... | collective-permute-start | bytes 196616 | tf_op jit(solution)/shard_map/ppermute | solution.py:19
  181.6 5.9 %collective-permute-start.17 = (bf16[1,32,1024]{2,1,0:T(8,128)(2,1)S(1)}, bf16[1,32,1024]{2,1,0:T(8,128)(2,1)S(1)}, u32[]{:S(2)}, u32[]{:S(2)}) collective-permute-start(bf16[1,32,1024]{2,1,0:T(8,128)(2,1)S(1)} %fusion.28.refs_0_), channel_id=1, source_target_pairs={{0,16},{4,20},{8,24},{12,28},{16,0},{20,4},{24,8},{28,12},{1,17},{... | collective-permute-start | bytes 196616 | tf_op jit(solution)/shard_map/ppermute | solution.py:19
  183.1 5.4 %collective-permute-start.24 = (bf16[2,32,1024]{2,1,0:T(8,128)(2,1)S(1)}, bf16[2,32,1024]{2,1,0:T(8,128)(2,1)S(1)}, u32[]{:S(2)}, u32[]{:S(2)}) collective-permute-start(bf16[2,32,1024]{2,1,0:T(8,128)(2,1)S(1)} %pad_maximum_fusion.6), channel_id=1, source_target_pairs={{0,8},{4,12},{8,0},{12,4},{16,24},{20,28},{24,16},{28,20},{1,9},{5... | collective-permute-start | bytes 393224 | tf_op jit(solution)/shard_map/ppermute | solution.py:19
  187.6 5.0 %collective-permute-start.18 = (bf16[2,32,1024]{2,1,0:T(8,128)(2,1)S(1)}, bf16[2,32,1024]{2,1,0:T(8,128)(2,1)S(1)}, u32[]{:S(2)}, u32[]{:S(2)}) collective-permute-start(bf16[2,32,1024]{2,1,0:T(8,128)(2,1)S(1)} %pad_maximum_fusion.5), channel_id=1, source_target_pairs={{0,8},{4,12},{8,0},{12,4},{16,24},{20,28},{24,16},{28,20},{1,9},{5... | collective-permute-start | bytes 393224 | tf_op jit(solution)/shard_map/ppermute | solution.py:19
  188.0 8.8 %collective-permute-start.34 = (bf16[4,32,1024]{2,1,0:T(8,128)(2,1)S(1)}, bf16[4,32,1024]{2,1,0:T(8,128)(2,1)S(1)}, u32[]{:S(2)}, u32[]{:S(2)}) collective-permute-start(bf16[4,32,1024]{2,1,0:T(8,128)(2,1)S(1)} %pad_maximum_fusion.2), channel_id=1, source_target_pairs={{0,4},{4,0},{8,12},{12,8},{16,20},{20,16},{24,28},{28,24},{1,5},{5... | collective-permute-start | bytes 786440 | tf_op jit(solution)/shard_map/ppermute | solution.py:19
  188.6 11.0 %collective-permute-start.25 = (bf16[4,32,1024]{2,1,0:T(8,128)(2,1)S(1)}, bf16[4,32,1024]{2,1,0:T(8,128)(2,1)S(1)}, u32[]{:S(2)}, u32[]{:S(2)}) collective-permute-start(bf16[4,32,1024]{2,1,0:T(8,128)(2,1)S(1)} %pad_maximum_fusion.1), channel_id=1, source_target_pairs={{0,4},{4,0},{8,12},{12,8},{16,20},{20,16},{24,28},{28,24},{1,5},{5... | collective-permute-start | bytes 786440 | tf_op jit(solution)/shard_map/ppermute | solution.py:19
  192.6 9.7 %collective-permute-start.19 = (bf16[4,32,1024]{2,1,0:T(8,128)(2,1)S(1)}, bf16[4,32,1024]{2,1,0:T(8,128)(2,1)S(1)}, u32[]{:S(2)}, u32[]{:S(2)}) collective-permute-start(bf16[4,32,1024]{2,1,0:T(8,128)(2,1)S(1)} %pad_maximum_fusion), channel_id=1, source_target_pairs={{0,4},{4,0},{8,12},{12,8},{16,20},{20,16},{24,28},{28,24},{1,5},{5... | collective-permute-start | bytes 786440 | tf_op jit(solution)/shard_map/ppermute | solution.py:19
  (6 other events, 21.4 us)

commit v3 on v2

--- a/solution.py
+++ b/solution.py
@@ -251,9 +251,11 @@
     )(pool_index, *blocks, weight)
 
 
-def pool_sum(keep, send):
+def pool_sum(keep, send, after=()):
     terms, bit = [keep], 1
     while True:
+        if bit == 2 and after:
+            send, *after = lax.optimization_barrier((send, *after))
         terms.append(exchange(send, "pool", bit))
         if terms[0].shape[0] == 1:
             break
@@ -266,7 +268,7 @@
         order = [q ^ bit for _, qs in parts for q in qs]
         parts.append((exchange(have, "pool", bit), order))
         bit //= 2
-    return parts
+    return parts, after
 
 
 def place(tp_index, pool_index, parts, out, shape, batch, start, first):
@@ -359,36 +361,43 @@
     wide = wide.reshape(pool * rank_local, batches * row_count).T
     wide = wide.reshape(batches, row_count, pool * rank_local)
     factors = [x.reshape(pool * rank_local, -1) for x in factors]
-    apart = row_count % (16 * pool) == 0 and pool % tp == 0 and columns % 512 == 0
-    out = None
-    outputs = []
+    apart = row_count % (16 * pool) == 0 and pool % tp == 0 and columns % 256 == 0
+    out, outputs, waiting = None, [], None
     rows_in = activations
     for m, start, rows in chunks:
         up = project(t_scalar, rows_in, (m,), start, rows, up_weight, wide, [factors[m]])
         held = 0 if apart else len(gate) - 1
         up, gate[held:] = scatter_sum(*up, gate[held:])
+        if waiting:
+            width = columns // 2
+            for first in range(0, columns, width):
+                keep, send = down_project(p_scalar, waiting[1], down_matrix, first, width)
+                if first:
+                    send, up[-1] = lax.optimization_barrier((send, up[-1]))
+                parts, _ = pool_sum(keep, send)
+                out = place(
+                    t_scalar, p_scalar, parts, out, (batches, row_count, columns), *waiting[0], first
+                )
         gate_value = sum(x[m].astype(F32) for x in gate)
         up_value = sum(x[0].astype(F32) for x in up)
         hidden = (jax.nn.silu(gate_value) * up_value).astype(BF16)
         hidden, rows_in = lax.optimization_barrier((hidden, rows_in))
         blocks = gather_rows(hidden)
         if apart:
-            groups = 2
-            width = columns // groups
-            for g in range(groups):
-                pieces = pool_sum(
-                    *down_project(p_scalar, blocks, down_matrix, g * width, width)
-                )
-                out = place(
-                    t_scalar, p_scalar, pieces, out, (batches, row_count, columns), m, start, g * width
-                )
+            waiting = ((m, start), blocks)
         else:
             here = by_index(jnp.stack(blocks), tp_index).reshape(rows, -1)
             partial = jnp.dot(here, down_matrix, preferred_element_type=F32)
             outputs.append(lax.psum(partial, "pool").astype(BF16))
-    if out is not None:
-        return out
-    return jnp.concatenate(outputs, axis=0).reshape(batches, row_count, columns)
+    if not apart:
+        return jnp.concatenate(outputs, axis=0).reshape(batches, row_count, columns)
+    width = columns // 2
+    for first in (0, width):
+        parts, _ = pool_sum(*down_project(p_scalar, waiting[1], down_matrix, first, width))
+        out = place(
+            t_scalar, p_scalar, parts, out, (batches, row_count, columns), *waiting[0], first
+        )
+    return out
 
 
 def solution(mesh):

time: 204 us -> 202 us (level)
  starting transfers between devices: 64.7 us -> 54.2 us
  waiting for transfers between devices: 68.3 us -> 76.4 us
    ppermute x41, starting transfers between devices: 55.4 us -> 44.9 us  [exchange(): lax.ppermute(x, axis, [(i, i ^ bit) for i in range(lax.axis_size(axis))])]
    ppermute x41, waiting for transfers between devices: 68.3 us -> 76.4 us  [exchange(): lax.ppermute(x, axis, [(i, i ^ bit) for i in range(lax.axis_size(axis))])]
  transfers between devices with their start and end apart: 43 -> 43, of which waited for: 24 -> 27; matrix products, arithmetic and copies ran while one was open for 5% -> 5% of each run, Pallas kernels for 18% -> 19%
where the time goes in v3:
time: 202 us; the launch traced here: 201 us
  waiting for transfers between devices  76.4 us (38%)
  Pallas kernels  55.5 us (27%)
  starting transfers between devices  54.2 us (27%)
  other arithmetic  7.96 us (4%)
  local copies, waits for them, and re-layouts  6.3 us (3%)
    ppermute x41, waiting for transfers between devices, exchange(): lax.ppermute(x, axis, [(i, i ^ bit) for i in range(lax.axis_size(axis))])  76.4 us
    ppermute x41, starting transfers between devices, exchange(): lax.ppermute(x, axis, [(i, i ^ bit) for i in range(lax.axis_size(axis))])  44.9 us
    pallas_call x3, Pallas kernels, project(): pl.pallas_call(body, grid_spec=pltpu.PrefetchScalarGridSpec(num_scalar_pr...  29.8 us
    pallas_call x4, Pallas kernels, down_project(): pl.pallas_call(body, grid_spec=pltpu.PrefetchScalarGridSpec(num_scalar_pr...  17.8 us
    all_to_all x2, starting transfers between devices, across(): return lax.all_to_all(x, 'pool', split_axis=0, concat_axis=0, tiled=True)  9.31 us
    squeeze x1, other arithmetic, scatter_sum(): terms = [x[:, 0] for x in terms]  4.17 us
  transfers between devices with their start and end apart: 43, of which 27 were waited for; matrix products, arithmetic and copies ran while one was open for 5% of the time, Pallas kernels for 19%

profile of v3, /device:TPU:0, one launch (start us, length us, event | category | flops | bytes accessed | tf_op | source)
XLA Modules:
  0.0 201.1 jit_solution(18395605746847949887)
XLA Ops:
  0.0 2.0 %copy-done.1 = bf16[4,16,28672]{2,1,0:T(8,128)(2,1)S(1)} copy-done((bf16[4,16,28672]{2,1,0:T(8,128)(2,1)S(1)}, bf16[4,16,28672]{2,1,0:T(8,128)(2,1)}, u32[]{:S(2)}) %copy-start.1) | copy-done | bytes 3670040
  3.4 2.9 %pick_pages.1 = (s32[2]{0:T(128)S(1)}, f32[2,1,256]{2,1,0:T(1,128)S(1)}, bf16[8,16,3584]{2,1,0:T(8,128)(2,1)S(1)}, bf16[8,16,3584]{2,1,0:T(8,128)(2,1)S(1)}) custom-call(s32[1]{0:T(128)} %bitcast.1.p_ref, s32[32]{0:T(128)S(1)} %copy-done.6, s32[2,256]{1,0:T(2,128)S(1)} %copy-done.5, bf16[4,16,28672]{2,1,0:T(8,128)(2,1)S(1)} %copy-done.1), custom_call_target="tpu_custom_call" | custom-call | tf_op jit(solution)/shard_map/pick_pages/pallas_call | solution.py:55
  6.4 1.5 shrink.1
  9.3 2.9 %collective-permute-start.1 = (f32[1,1,16,512]{3,2,1,0:T(8,128)S(1)}, f32[1,1,16,512]{3,2,1,0:T(8,128)S(1)}, u32[]{:S(2)}, u32[]{:S(2)}) collective-permute-start(f32[1,1,16,512]{3,2,1,0:T(8,128)S(1)} %slice_add_fusion.9), channel_id=1, source_target_pairs={{0,2},{1,3},{2,0},{3,1},{4,6},{5,7},{6,4},{7,5},{8,10},{9,11},{10,... | collective-permute-start | bytes 98312 | tf_op jit(solution)/shard_map/ppermute | solution.py:19
  12.2 1.9 collective-permute-done.1
  14.1 12.6 %gate.1 = (f32[2,2,64,3584]{3,2,1,0:T(8,128)}, bf16[2,2,64,3584]{3,2,1,0:T(8,128)(2,1)S(1)}) custom-call(s32[1]{0:T(128)} %bitcast.t_ref, bf16[2,256,2048]{2,1,0:T(8,128)(2,1)S(1)} %copy-done, bf16[2,256,2048]{2,1,0:T(8,128)(2,1)S(1)} %copy-done, bf16[2,256,2048]{2,1,0:T(8,128)(2,1)S(1)} %copy-done, bf16[2,256,2048]{2,1,0:T(8,128)(2,1)S(1)} %copy-done, ...), custom_call_target="tpu_custom_call" | custom-call | flops 7516192768 | bytes 14680064 | tf_op jit(solution)/shard_map/gate/pallas_call | solution.py:157
  28.1 2.0 collective-permute-start.3
  30.1 4.9 %all-to-all-start = ((bf16[8,16,3584]{2,1,0:T(8,128)(2,1)}), bf16[8,16,3584]{2,1,0:T(8,128)(2,1)S(1)}, u32[]{:S(2)}, u32[]{:S(2)}) async-start(bf16[8,16,3584]{2,1,0:T(8,128)(2,1)} %copy-done.4), calls=%async_computation | async-start | bytes 1835008 | tf_op jit(solution)/shard_map/all_to_all | solution.py:339
  35.0 4.2 %slice_bitcast_fusion = (f32[2,64,3584]{2,1,0:T(8,128)}, bf16[2,1,64,3584]{3,2,0,1:T(8,128)(2,1)}) fusion(bf16[2,2,64,3584]{3,2,0,1:T(8,128)(2,1)} %collective-permute-done.2, f32[2,2,64,3584]{3,2,1,0:T(8,128)} %get-tuple-element.48), kind=kLoop, calls=%fused_computation | loop fusion | flops 1376256 | bytes 7340032 | tf_op jit(solution)/shard_map/squeeze | solution.py:186
  39.1 2.0 %collective-permute-start.4 = (bf16[2,16,512]{2,1,0:T(8,128)(2,1)S(1)}, bf16[2,16,512]{2,1,0:T(8,128)(2,1)S(1)}, u32[]{:S(2)}, u32[]{:S(2)}) collective-permute-start(bf16[2,16,512]{2,1,0:T(8,128)(2,1)S(1)} %pad_maximum_fusion.10), channel_id=1, source_target_pairs={{0,8},{4,12},{8,0},{12,4},{16,24},{20,28},{24,16},{28,20},{1,9},{5... | collective-permute-start | bytes 98312 | tf_op jit(solution)/shard_map/ppermute | solution.py:19
  41.2 10.4 %collective-permute-done.4 = bf16[2,16,512]{2,1,0:T(8,128)(2,1)S(1)} collective-permute-done((bf16[2,16,512]{2,1,0:T(8,128)(2,1)S(1)}, bf16[2,16,512]{2,1,0:T(8,128)(2,1)S(1)}, u32[]{:S(2)}, u32[]{:S(2)}) %collective-permute-start.4) | collective-permute-done | bytes 32800 | tf_op jit(solution)/shard_map/ppermute | solution.py:19
  51.5 4.1 %collective-permute-start.5 = (bf16[4,16,512]{2,1,0:T(8,128)(2,1)S(1)}, bf16[4,16,512]{2,1,0:T(8,128)(2,1)S(1)}, u32[]{:S(2)}, u32[]{:S(2)}) collective-permute-start(bf16[4,16,512]{2,1,0:T(8,128)(2,1)S(1)} %pad_maximum_fusion.9), channel_id=1, source_target_pairs={{0,16},{4,20},{8,24},{12,28},{16,0},{20,4},{24,8},{28,12},{1,17},{... | collective-permute-start | bytes 196616 | tf_op jit(solution)/shard_map/ppermute | solution.py:19
  55.7 1.5 collective-permute-start.7
  57.2 3.9 %collective-permute-done.5 = bf16[4,16,512]{2,1,0:T(8,128)(2,1)S(1)} collective-permute-done((bf16[4,16,512]{2,1,0:T(8,128)(2,1)S(1)}, bf16[4,16,512]{2,1,0:T(8,128)(2,1)S(1)}, u32[]{:S(2)}, u32[]{:S(2)}) %collective-permute-start.5) | collective-permute-done | bytes 65568 | tf_op jit(solution)/shard_map/ppermute | solution.py:19
  61.4 4.4 %all-to-all-start.1 = ((bf16[8,16,3584]{2,1,0:T(8,128)(2,1)}), bf16[8,16,3584]{2,1,0:T(8,128)(2,1)}, u32[]{:S(2)}, u32[]{:S(2)}) async-start(bf16[8,16,3584]{2,1,0:T(8,128)(2,1)} %copy-done.3), calls=%async_computation.1 | async-start | bytes 1835008 | tf_op jit(solution)/shard_map/all_to_all | solution.py:339
  65.8 8.6 %up.2 = (f32[1,2,64,3584]{3,2,1,0:T(8,128)S(1)}, bf16[1,2,64,3584]{3,2,1,0:T(8,128)(2,1)S(1)}) custom-call(s32[1]{0:T(128)} %bitcast.t_ref, bf16[2,256,2048]{2,1,0:T(8,128)(2,1)S(1)} %copy-done, bf16[2,256,2048]{2,1,0:T(8,128)(2,1)S(1)} %copy-done, bf16[2,256,2048]{2,1,0:T(8,128)(2,1)S(1)} %copy-done, bf16[2,256,2048]{2,1,0:T(8,128)(2,1)S(1)} %copy-done, ...), custom_call_target="tpu_custom_call" | custom-call | flops 3758096384 | bytes 14680064 | tf_op jit(solution)/shard_map/up/pallas_call | solution.py:157
  77.1 1.5 collective-permute-start.8
  78.6 11.0 %collective-permute-done.8 = bf16[1,1,64,3584]{3,2,1,0:T(8,128)(2,1)S(1)} collective-permute-done((bf16[1,1,64,3584]{3,2,1,0:T(8,128)(2,1)S(1)}, bf16[1,1,64,3584]{3,2,1,0:T(8,128)(2,1)S(1)}, u32[]{:S(2)}, u32[]{:S(2)}) %collective-permute-start.8) | collective-permute-done | bytes 458784 | tf_op jit(solution)/shard_map/ppermute | solution.py:19
  89.7 1.5 fusion.6.refs_0_
  91.1 1.6 collective-permute-start.11
  92.7 8.6 %up.3 = (f32[1,2,64,3584]{3,2,1,0:T(8,128)S(1)}, bf16[1,2,64,3584]{3,2,1,0:T(8,128)(2,1)S(1)}) custom-call(s32[1]{0:T(128)} %bitcast.t_ref, bf16[2,256,2048]{2,1,0:T(8,128)(2,1)S(1)} %copy-done, bf16[2,256,2048]{2,1,0:T(8,128)(2,1)S(1)} %copy-done, bf16[2,256,2048]{2,1,0:T(8,128)(2,1)S(1)} %copy-done, bf16[2,256,2048]{2,1,0:T(8,128)(2,1)S(1)} %copy-done, ...), custom_call_target="tpu_custom_call" | custom-call | flops 3758096384 | bytes 14680064 | tf_op jit(solution)/shard_map/up/pallas_call | solution.py:157
  103.0 1.6 collective-permute-done.10.refs_1_
  105.2 4.5 %down.7 = (f32[4,32,1024]{2,1,0:T(8,128)S(1)}, bf16[4,32,1024]{2,1,0:T(8,128)(2,1)S(1)}) custom-call(s32[1]{0:T(128)} %bitcast.1.p_ref, bf16[64,3584]{1,0:T(8,128)(2,1)S(1)} %fusion.6.refs_0_, bf16[64,3584]{1,0:T(8,128)(2,1)S(1)} %collective-permute-done.10.refs_1_, bf16[64,3584]{1,0:T(8,128)(2,1)S(1)} %collective-permute-done.11.refs_2_, ...), custom_call_target="tpu_custom_call" | custom-call | flops 1879048192 | bytes 7340032 | tf_op jit(solution)/shard_map/down/pallas_call | solution.py:232
  109.7 1.8 collective-permute-start.35
  112.7 5.4 %collective-permute-done.35 = bf16[4,32,1024]{2,1,0:T(8,128)(2,1)S(1)} collective-permute-done((bf16[4,32,1024]{2,1,0:T(8,128)(2,1)S(1)}, bf16[4,32,1024]{2,1,0:T(8,128)(2,1)S(1)}, u32[]{:S(2)}, u32[]{:S(2)}) %collective-permute-start.35) | collective-permute-done | bytes 262176 | tf_op jit(solution)/shard_map/ppermute | solution.py:19
  118.2 1.8 collective-permute-start.36
  119.9 4.5 %down.4 = (f32[4,32,1024]{2,1,0:T(8,128)S(1)}, bf16[4,32,1024]{2,1,0:T(8,128)(2,1)S(1)}) custom-call(s32[1]{0:T(128)} %bitcast.1.p_ref, bf16[64,3584]{1,0:T(8,128)(2,1)S(1)} %fusion.6.refs_0_, bf16[64,3584]{1,0:T(8,128)(2,1)S(1)} %collective-permute-done.10.refs_1_, bf16[64,3584]{1,0:T(8,128)(2,1)S(1)} %collective-permute-done.11.refs_2_, ...), custom_call_target="tpu_custom_call" | custom-call | flops 1879048192 | bytes 7340032 | tf_op jit(solution)/shard_map/down/pallas_call | solution.py:232
  124.5 2.5 %collective-permute-start.37 = (bf16[1,32,1024]{2,1,0:T(8,128)(2,1)S(1)}, bf16[1,32,1024]{2,1,0:T(8,128)(2,1)S(1)}, u32[]{:S(2)}, u32[]{:S(2)}) collective-permute-start(bf16[1,32,1024]{2,1,0:T(8,128)(2,1)S(1)} %fusion.11), channel_id=1, source_target_pairs={{0,16},{4,20},{8,24},{12,28},{16,0},{20,4},{24,8},{28,12},{1,17},{... | collective-permute-start | bytes 196616 | tf_op jit(solution)/shard_map/ppermute | solution.py:19
  126.9 1.5 collective-permute-start.29
  128.4 1.5 fusion.2.refs_0_
  132.2 1.7 collective-permute-done.29
  134.7 2.2 %collective-permute-done.38.refs_1_ = bf16[1,32,1024]{2,1,0:T(8,128)(2,1)S(1)} collective-permute-done((bf16[1,32,1024]{2,1,0:T(8,128)(2,1)S(1)}, bf16[1,32,1024]{2,1,0:T(8,128)(2,1)S(1)}, u32[]{:S(2)}, u32[]{:S(2)}) %collective-permute-start.38) | collective-permute-done | bytes 65568 | tf_op jit(solution)/shard_map/ppermute | solution.py:19
  137.5 3.3 %collective-permute-done.15.refs_2_ = bf16[64,3584]{1,0:T(8,128)(2,1)S(1)} collective-permute-done((bf16[64,3584]{1,0:T(8,128)(2,1)S(1)}, bf16[64,3584]{1,0:T(8,128)(2,1)S(1)}, u32[]{:S(2)}, u32[]{:S(2)}) %collective-permute-start.15) | collective-permute-done | bytes 458784 | tf_op jit(solution)/shard_map/ppermute | solution.py:19
  143.0 4.8 %collective-permute-done.31 = bf16[1,32,1024]{2,1,0:T(8,128)(2,1)S(1)} collective-permute-done((bf16[1,32,1024]{2,1,0:T(8,128)(2,1)S(1)}, bf16[1,32,1024]{2,1,0:T(8,128)(2,1)S(1)}, u32[]{:S(2)}, u32[]{:S(2)}) %collective-permute-start.31) | collective-permute-done | bytes 65568 | tf_op jit(solution)/shard_map/ppermute | solution.py:19
  147.9 4.5 %down.6 = (f32[4,32,1024]{2,1,0:T(8,128)S(1)}, bf16[4,32,1024]{2,1,0:T(8,128)(2,1)S(1)}) custom-call(s32[1]{0:T(128)} %bitcast.1.p_ref, bf16[64,3584]{1,0:T(8,128)(2,1)S(1)} %fusion.2.refs_0_, bf16[64,3584]{1,0:T(8,128)(2,1)S(1)} %collective-permute-done.14.refs_1_, bf16[64,3584]{1,0:T(8,128)(2,1)S(1)} %collective-permute-done.15.refs_2_, ...), custom_call_target="tpu_custom_call" | custom-call | flops 1879048192 | bytes 7340032 | tf_op jit(solution)/shard_map/down/pallas_call | solution.py:232
  153.0 4.5 %down.5 = (f32[4,32,1024]{2,1,0:T(8,128)S(1)}, bf16[4,32,1024]{2,1,0:T(8,128)(2,1)S(1)}) custom-call(s32[1]{0:T(128)} %bitcast.1.p_ref, bf16[64,3584]{1,0:T(8,128)(2,1)S(1)} %fusion.2.refs_0_, bf16[64,3584]{1,0:T(8,128)(2,1)S(1)} %collective-permute-done.14.refs_1_, bf16[64,3584]{1,0:T(8,128)(2,1)S(1)} %collective-permute-done.15.refs_2_, ...), custom_call_target="tpu_custom_call" | custom-call | flops 1879048192 | bytes 7340032 | tf_op jit(solution)/shard_map/down/pallas_call | solution.py:232
  157.4 1.5 collective-permute-start.17
  162.4 3.7 %collective-permute-done.17 = bf16[4,32,1024]{2,1,0:T(8,128)(2,1)S(1)} collective-permute-done((bf16[4,32,1024]{2,1,0:T(8,128)(2,1)S(1)}, bf16[4,32,1024]{2,1,0:T(8,128)(2,1)S(1)}, u32[]{:S(2)}, u32[]{:S(2)}) %collective-permute-start.17) | collective-permute-done | bytes 262176 | tf_op jit(solution)/shard_map/ppermute | solution.py:19
  167.1 2.2 %collective-permute-start.25 = (bf16[1,32,1024]{2,1,0:T(8,128)(2,1)S(1)}, bf16[1,32,1024]{2,1,0:T(8,128)(2,1)S(1)}, u32[]{:S(2)}, u32[]{:S(2)}) collective-permute-start(bf16[1,32,1024]{2,1,0:T(8,128)(2,1)S(1)} %fusion.21), channel_id=1, source_target_pairs={{0,16},{4,20},{8,24},{12,28},{16,0},{20,4},{24,8},{28,12},{1,17},{... | collective-permute-start | bytes 196616 | tf_op jit(solution)/shard_map/ppermute | solution.py:19
  169.3 2.4 %collective-permute-done.18 = bf16[2,32,1024]{2,1,0:T(8,128)(2,1)S(1)} collective-permute-done((bf16[2,32,1024]{2,1,0:T(8,128)(2,1)S(1)}, bf16[2,32,1024]{2,1,0:T(8,128)(2,1)S(1)}, u32[]{:S(2)}, u32[]{:S(2)}) %collective-permute-start.18) | collective-permute-done | bytes 131104 | tf_op jit(solution)/shard_map/ppermute | solution.py:19
  171.7 3.0 %collective-permute-start.19 = (bf16[1,32,1024]{2,1,0:T(8,128)(2,1)S(1)}, bf16[1,32,1024]{2,1,0:T(8,128)(2,1)S(1)}, u32[]{:S(2)}, u32[]{:S(2)}) collective-permute-start(bf16[1,32,1024]{2,1,0:T(8,128)(2,1)S(1)} %fusion.26), channel_id=1, source_target_pairs={{0,16},{4,20},{8,24},{12,28},{16,0},{20,4},{24,8},{28,12},{1,17},{... | collective-permute-start | bytes 196616 | tf_op jit(solution)/shard_map/ppermute | solution.py:19
  174.9 3.2 %collective-permute-done.19 = bf16[1,32,1024]{2,1,0:T(8,128)(2,1)S(1)} collective-permute-done((bf16[1,32,1024]{2,1,0:T(8,128)(2,1)S(1)}, bf16[1,32,1024]{2,1,0:T(8,128)(2,1)S(1)}, u32[]{:S(2)}, u32[]{:S(2)}) %collective-permute-start.19) | collective-permute-done | bytes 65568 | tf_op jit(solution)/shard_map/ppermute | solution.py:19
  178.1 2.3 %collective-permute-start.20 = (bf16[1,32,1024]{2,1,0:T(8,128)(2,1)S(1)}, bf16[1,32,1024]{2,1,0:T(8,128)(2,1)S(1)}, u32[]{:S(2)}, u32[]{:S(2)}) collective-permute-start(bf16[1,32,1024]{2,1,0:T(8,128)(2,1)S(1)} %fusion.29.refs_0_), channel_id=1, source_target_pairs={{0,16},{4,20},{8,24},{12,28},{16,0},{20,4},{24,8},{28,12},{1,17},{... | collective-permute-start | bytes 196616 | tf_op jit(solution)/shard_map/ppermute | solution.py:19
  181.5 2.5 %collective-permute-done.20.refs_1_ = bf16[1,32,1024]{2,1,0:T(8,128)(2,1)S(1)} collective-permute-done((bf16[1,32,1024]{2,1,0:T(8,128)(2,1)S(1)}, bf16[1,32,1024]{2,1,0:T(8,128)(2,1)S(1)}, u32[]{:S(2)}, u32[]{:S(2)}) %collective-permute-start.20) | collective-permute-done | bytes 65568 | tf_op jit(solution)/shard_map/ppermute | solution.py:19
  186.6 2.5 %collective-permute-done.21.refs_2_ = bf16[2,32,1024]{2,1,0:T(8,128)(2,1)S(1)} collective-permute-done((bf16[2,32,1024]{2,1,0:T(8,128)(2,1)S(1)}, bf16[2,32,1024]{2,1,0:T(8,128)(2,1)S(1)}, u32[]{:S(2)}, u32[]{:S(2)}) %collective-permute-start.21) | collective-permute-done | bytes 131104 | tf_op jit(solution)/shard_map/ppermute | solution.py:19
  190.1 3.5 %collective-permute-done.34.refs_3_ = bf16[4,32,1024]{2,1,0:T(8,128)(2,1)S(1)} collective-permute-done((bf16[4,32,1024]{2,1,0:T(8,128)(2,1)S(1)}, bf16[4,32,1024]{2,1,0:T(8,128)(2,1)S(1)}, u32[]{:S(2)}, u32[]{:S(2)}) %collective-permute-start.34) | collective-permute-done | bytes 262176 | tf_op jit(solution)/shard_map/ppermute | solution.py:19
  194.4 2.9 %collective-permute-done.28.refs_3_ = bf16[4,32,1024]{2,1,0:T(8,128)(2,1)S(1)} collective-permute-done((bf16[4,32,1024]{2,1,0:T(8,128)(2,1)S(1)}, bf16[4,32,1024]{2,1,0:T(8,128)(2,1)S(1)}, u32[]{:S(2)}, u32[]{:S(2)}) %collective-permute-start.28) | collective-permute-done | bytes 262176 | tf_op jit(solution)/shard_map/ppermute | solution.py:19
  198.2 2.0 collective-permute-done.22.refs_3_
  (113 shorter events, 28.9 us)
Async XLA Ops:
  6.3 20.4 %copy-start.3 = (bf16[8,16,3584]{2,1,0:T(8,128)(2,1)}, bf16[8,16,3584]{2,1,0:T(8,128)(2,1)S(1)}, u32[]{:S(2)}) copy-start(bf16[8,16,3584]{2,1,0:T(8,128)(2,1)S(1)} %get-tuple-element.62) | copy-start | bytes 2752516
  6.3 20.4 %copy-start.4 = (bf16[8,16,3584]{2,1,0:T(8,128)(2,1)}, bf16[8,16,3584]{2,1,0:T(8,128)(2,1)S(1)}, u32[]{:S(2)}) copy-start(bf16[8,16,3584]{2,1,0:T(8,128)(2,1)S(1)} %get-tuple-element.53) | copy-start | bytes 2752516
  7.9 1.4 collective-permute-start
  9.3 4.8 %collective-permute-start.1 = (f32[1,1,16,512]{3,2,1,0:T(8,128)S(1)}, f32[1,1,16,512]{3,2,1,0:T(8,128)S(1)}, u32[]{:S(2)}, u32[]{:S(2)}) collective-permute-start(f32[1,1,16,512]{3,2,1,0:T(8,128)S(1)} %slice_add_fusion.9), channel_id=1, source_target_pairs={{0,2},{1,3},{2,0},{3,1},{4,6},{5,7},{6,4},{7,5},{8,10},{9,11},{10,... | collective-permute-start | bytes 98312 | tf_op jit(solution)/shard_map/ppermute | solution.py:19
  28.1 6.9 %collective-permute-start.2 = (bf16[2,2,64,3584]{3,2,0,1:T(8,128)(2,1)}, bf16[2,2,64,3584]{3,2,0,1:T(8,128)(2,1)}, u32[]{:S(2)}, u32[]{:S(2)}) collective-permute-start(bf16[2,2,64,3584]{3,2,0,1:T(8,128)(2,1)} %copy.17), channel_id=1, source_target_pairs={{0,1},{1,0},{2,3},{3,2},{4,5},{5,4},{6,7},{7,6},{8,9},{9,8},{10,11... | collective-permute-start | bytes 5505032 | tf_op jit(solution)/shard_map/ppermute | solution.py:19
  28.1 6.9 %collective-permute-start.3 = (bf16[1,16,512]{2,1,0:T(8,128)(2,1)S(1)}, bf16[1,16,512]{2,1,0:T(8,128)(2,1)S(1)}, u32[]{:S(2)}, u32[]{:S(2)}) collective-permute-start(bf16[1,16,512]{2,1,0:T(8,128)(2,1)S(1)} %fusion.33), channel_id=1, source_target_pairs={{0,4},{4,0},{8,12},{12,8},{16,20},{20,16},{24,28},{28,24},{1,5},{5... | collective-permute-start | bytes 49160 | tf_op jit(solution)/shard_map/ppermute | solution.py:19
  30.1 31.3 %all-to-all-start = ((bf16[8,16,3584]{2,1,0:T(8,128)(2,1)}), bf16[8,16,3584]{2,1,0:T(8,128)(2,1)S(1)}, u32[]{:S(2)}, u32[]{:S(2)}) async-start(bf16[8,16,3584]{2,1,0:T(8,128)(2,1)} %copy-done.4), calls=%async_computation | async-start | bytes 1835008 | tf_op jit(solution)/shard_map/all_to_all | solution.py:339
  39.1 12.4 %collective-permute-start.4 = (bf16[2,16,512]{2,1,0:T(8,128)(2,1)S(1)}, bf16[2,16,512]{2,1,0:T(8,128)(2,1)S(1)}, u32[]{:S(2)}, u32[]{:S(2)}) collective-permute-start(bf16[2,16,512]{2,1,0:T(8,128)(2,1)S(1)} %pad_maximum_fusion.10), channel_id=1, source_target_pairs={{0,8},{4,12},{8,0},{12,4},{16,24},{20,28},{24,16},{28,20},{1,9},{5... | collective-permute-start | bytes 98312 | tf_op jit(solution)/shard_map/ppermute | solution.py:19
  51.5 9.5 %collective-permute-start.5 = (bf16[4,16,512]{2,1,0:T(8,128)(2,1)S(1)}, bf16[4,16,512]{2,1,0:T(8,128)(2,1)S(1)}, u32[]{:S(2)}, u32[]{:S(2)}) collective-permute-start(bf16[4,16,512]{2,1,0:T(8,128)(2,1)S(1)} %pad_maximum_fusion.9), channel_id=1, source_target_pairs={{0,16},{4,20},{8,24},{12,28},{16,0},{20,4},{24,8},{28,12},{1,17},{... | collective-permute-start | bytes 196616 | tf_op jit(solution)/shard_map/ppermute | solution.py:19
  55.7 21.4 %collective-permute-start.7 = (bf16[2,1,64,3584]{3,2,0,1:T(8,128)(2,1)}, bf16[2,1,64,3584]{3,2,0,1:T(8,128)(2,1)}, u32[]{:S(2)}, u32[]{:S(2)}) collective-permute-start(bf16[2,1,64,3584]{3,2,0,1:T(8,128)(2,1)} %get-tuple-element.56), channel_id=1, source_target_pairs={{0,2},{1,3},{2,0},{3,1},{4,6},{5,7},{6,4},{7,5},{8,10},{9,11},{10,... | collective-permute-start | bytes 2752520 | tf_op jit(solution)/shard_map/ppermute | solution.py:19
  61.4 31.4 %all-to-all-start.1 = ((bf16[8,16,3584]{2,1,0:T(8,128)(2,1)}), bf16[8,16,3584]{2,1,0:T(8,128)(2,1)}, u32[]{:S(2)}, u32[]{:S(2)}) async-start(bf16[8,16,3584]{2,1,0:T(8,128)(2,1)} %copy-done.3), calls=%async_computation.1 | async-start | bytes 1835008 | tf_op jit(solution)/shard_map/all_to_all | solution.py:339
  74.4 15.3 %copy-start.7 = (f32[2,64,3584]{2,1,0:T(8,128)S(1)}, f32[2,64,3584]{2,1,0:T(8,128)}, u32[]{:S(2)}) copy-start(f32[2,64,3584]{2,1,0:T(8,128)} %get-tuple-element.65) | copy-start | bytes 5505028
  74.4 2.5 %collective-permute-start.6 = (bf16[1,2,64,3584]{3,2,1,0:T(8,128)(2,1)S(1)}, bf16[1,2,64,3584]{3,2,1,0:T(8,128)(2,1)S(1)}, u32[]{:S(2)}, u32[]{:S(2)}) collective-permute-start(bf16[1,2,64,3584]{3,2,1,0:T(8,128)(2,1)S(1)} %get-tuple-element.55), channel_id=1, source_target_pairs={{0,1},{1,0},{2,3},{3,2},{4,5},{5,4},{6,7},{7,6},{8,9},{9,8},{10,11... | collective-permute-start | bytes 2752520 | tf_op jit(solution)/shard_map/ppermute | solution.py:19
  75.9 15.3 %copy-start.9 = (bf16[2,64,3584]{2,1,0:T(8,128)(2,1)}, bf16[2,64,3584]{2,1,0:T(8,128)(2,1)S(1)}, u32[]{:S(2)}) copy-start(bf16[2,64,3584]{2,1,0:T(8,128)(2,1)S(1)} %slice_bitcast_fusion.1) | copy-start | bytes 2752516
  77.1 12.6 %collective-permute-start.8 = (bf16[1,1,64,3584]{3,2,1,0:T(8,128)(2,1)S(1)}, bf16[1,1,64,3584]{3,2,1,0:T(8,128)(2,1)S(1)}, u32[]{:S(2)}, u32[]{:S(2)}) collective-permute-start(bf16[1,1,64,3584]{3,2,1,0:T(8,128)(2,1)S(1)} %add_convert_fusion.1), channel_id=1, source_target_pairs={{0,2},{1,3},{2,0},{3,1},{4,6},{5,7},{6,4},{7,5},{8,10},{9,11},{10,... | collective-permute-start | bytes 1376264 | tf_op jit(solution)/shard_map/ppermute | solution.py:19
  91.1 11.8 %collective-permute-start.11 = (bf16[64,3584]{1,0:T(8,128)(2,1)S(1)}, bf16[64,3584]{1,0:T(8,128)(2,1)S(1)}, u32[]{:S(2)}, u32[]{:S(2)}) collective-permute-start(bf16[64,3584]{1,0:T(8,128)(2,1)S(1)} %fusion.6.refs_0_), channel_id=1, source_target_pairs={{0,2},{1,3},{2,0},{3,1},{4,6},{5,7},{6,4},{7,5},{8,10},{9,11},{10,... | collective-permute-start | bytes 1376264 | tf_op jit(solution)/shard_map/ppermute | solution.py:19
  101.4 10.1 %collective-permute-start.9 = (bf16[1,2,64,3584]{3,2,1,0:T(8,128)(2,1)S(1)}, bf16[1,2,64,3584]{3,2,1,0:T(8,128)(2,1)S(1)}, u32[]{:S(2)}, u32[]{:S(2)}) collective-permute-start(bf16[1,2,64,3584]{3,2,1,0:T(8,128)(2,1)S(1)} %get-tuple-element.64), channel_id=1, source_target_pairs={{0,1},{1,0},{2,3},{3,2},{4,5},{5,4},{6,7},{7,6},{8,9},{9,8},{10,11... | collective-permute-start | bytes 2752520 | tf_op jit(solution)/shard_map/ppermute | solution.py:19
  101.5 3.1 %collective-permute-start.10 = (bf16[64,3584]{1,0:T(8,128)(2,1)S(1)}, bf16[64,3584]{1,0:T(8,128)(2,1)S(1)}, u32[]{:S(2)}, u32[]{:S(2)}) collective-permute-start(bf16[64,3584]{1,0:T(8,128)(2,1)S(1)} %fusion.6.refs_0_), channel_id=1, source_target_pairs={{0,1},{1,0},{2,3},{3,2},{4,5},{5,4},{6,7},{7,6},{8,9},{9,8},{10,11... | collective-permute-start | bytes 1376264 | tf_op jit(solution)/shard_map/ppermute | solution.py:19
  102.9 2.3 %collective-permute-start.12 = (bf16[64,3584]{1,0:T(8,128)(2,1)S(1)}, bf16[64,3584]{1,0:T(8,128)(2,1)S(1)}, u32[]{:S(2)}, u32[]{:S(2)}) collective-permute-start(bf16[64,3584]{1,0:T(8,128)(2,1)S(1)} %collective-permute-done.11.refs_2_), channel_id=1, source_target_pairs={{0,1},{1,0},{2,3},{3,2},{4,5},{5,4},{6,7},{7,6},{8,9},{9,8},{10,11... | collective-permute-start | bytes 1376264 | tf_op jit(solution)/shard_map/ppermute | solution.py:19
  109.7 8.4 %collective-permute-start.35 = (bf16[4,32,1024]{2,1,0:T(8,128)(2,1)S(1)}, bf16[4,32,1024]{2,1,0:T(8,128)(2,1)S(1)}, u32[]{:S(2)}, u32[]{:S(2)}) collective-permute-start(bf16[4,32,1024]{2,1,0:T(8,128)(2,1)S(1)} %get-tuple-element.80), channel_id=1, source_target_pairs={{0,4},{4,0},{8,12},{12,8},{16,20},{20,16},{24,28},{28,24},{1,5},{5... | collective-permute-start | bytes 786440 | tf_op jit(solution)/shard_map/ppermute | solution.py:19
  111.5 15.4 %collective-permute-start.13 = (bf16[1,1,64,3584]{3,2,1,0:T(8,128)(2,1)S(1)}, bf16[1,1,64,3584]{3,2,1,0:T(8,128)(2,1)S(1)}, u32[]{:S(2)}, u32[]{:S(2)}) collective-permute-start(bf16[1,1,64,3584]{3,2,1,0:T(8,128)(2,1)S(1)} %add_convert_fusion), channel_id=1, source_target_pairs={{0,2},{1,3},{2,0},{3,1},{4,6},{5,7},{6,4},{7,5},{8,10},{9,11},{10,... | collective-permute-start | bytes 1376264 | tf_op jit(solution)/shard_map/ppermute | solution.py:19
  118.2 10.3 %copy-start.8 = (f32[2,64,3584]{2,1,0:T(8,128)S(1)}, f32[2,64,3584]{2,1,0:T(8,128)}, u32[]{:S(2)}) copy-start(f32[2,64,3584]{2,1,0:T(8,128)} %get-tuple-element.65) | copy-start | bytes 5505028
  118.2 6.3 %collective-permute-start.36 = (bf16[2,32,1024]{2,1,0:T(8,128)(2,1)S(1)}, bf16[2,32,1024]{2,1,0:T(8,128)(2,1)S(1)}, u32[]{:S(2)}, u32[]{:S(2)}) collective-permute-start(bf16[2,32,1024]{2,1,0:T(8,128)(2,1)S(1)} %get-tuple-element.83), channel_id=1, source_target_pairs={{0,8},{4,12},{8,0},{12,4},{16,24},{20,28},{24,16},{28,20},{1,9},{5... | collective-permute-start | bytes 393224 | tf_op jit(solution)/shard_map/ppermute | solution.py:19
  124.5 6.5 %collective-permute-start.37 = (bf16[1,32,1024]{2,1,0:T(8,128)(2,1)S(1)}, bf16[1,32,1024]{2,1,0:T(8,128)(2,1)S(1)}, u32[]{:S(2)}, u32[]{:S(2)}) collective-permute-start(bf16[1,32,1024]{2,1,0:T(8,128)(2,1)S(1)} %fusion.11), channel_id=1, source_target_pairs={{0,16},{4,20},{8,24},{12,28},{16,0},{20,4},{24,8},{28,12},{1,17},{... | collective-permute-start | bytes 196616 | tf_op jit(solution)/shard_map/ppermute | solution.py:19
  126.9 7.0 %collective-permute-start.29 = (bf16[4,32,1024]{2,1,0:T(8,128)(2,1)S(1)}, bf16[4,32,1024]{2,1,0:T(8,128)(2,1)S(1)}, u32[]{:S(2)}, u32[]{:S(2)}) collective-permute-start(bf16[4,32,1024]{2,1,0:T(8,128)(2,1)S(1)} %get-tuple-element.78), channel_id=1, source_target_pairs={{0,4},{4,0},{8,12},{12,8},{16,20},{20,16},{24,28},{28,24},{1,5},{5... | collective-permute-start | bytes 786440 | tf_op jit(solution)/shard_map/ppermute | solution.py:19
  129.9 11.0 %collective-permute-start.15 = (bf16[64,3584]{1,0:T(8,128)(2,1)S(1)}, bf16[64,3584]{1,0:T(8,128)(2,1)S(1)}, u32[]{:S(2)}, u32[]{:S(2)}) collective-permute-start(bf16[64,3584]{1,0:T(8,128)(2,1)S(1)} %fusion.2.refs_0_), channel_id=1, source_target_pairs={{0,2},{1,3},{2,0},{3,1},{4,6},{5,7},{6,4},{7,5},{8,10},{9,11},{10,... | collective-permute-start | bytes 1376264 | tf_op jit(solution)/shard_map/ppermute | solution.py:19
  131.0 5.9 %collective-permute-start.38 = (bf16[1,32,1024]{2,1,0:T(8,128)(2,1)S(1)}, bf16[1,32,1024]{2,1,0:T(8,128)(2,1)S(1)}, u32[]{:S(2)}, u32[]{:S(2)}) collective-permute-start(bf16[1,32,1024]{2,1,0:T(8,128)(2,1)S(1)} %fusion.14.refs_0_), channel_id=1, source_target_pairs={{0,16},{4,20},{8,24},{12,28},{16,0},{20,4},{24,8},{28,12},{1,17},{... | collective-permute-start | bytes 196616 | tf_op jit(solution)/shard_map/ppermute | solution.py:19
  133.9 6.9 %collective-permute-start.30 = (bf16[2,32,1024]{2,1,0:T(8,128)(2,1)S(1)}, bf16[2,32,1024]{2,1,0:T(8,128)(2,1)S(1)}, u32[]{:S(2)}, u32[]{:S(2)}) collective-permute-start(bf16[2,32,1024]{2,1,0:T(8,128)(2,1)S(1)} %get-tuple-element.85), channel_id=1, source_target_pairs={{0,8},{4,12},{8,0},{12,4},{16,24},{20,28},{24,16},{28,20},{1,9},{5... | collective-permute-start | bytes 393224 | tf_op jit(solution)/shard_map/ppermute | solution.py:19
  137.0 5.0 %collective-permute-start.39 = (bf16[2,32,1024]{2,1,0:T(8,128)(2,1)S(1)}, bf16[2,32,1024]{2,1,0:T(8,128)(2,1)S(1)}, u32[]{:S(2)}, u32[]{:S(2)}) collective-permute-start(bf16[2,32,1024]{2,1,0:T(8,128)(2,1)S(1)} %pad_maximum_fusion.8), channel_id=1, source_target_pairs={{0,8},{4,12},{8,0},{12,4},{16,24},{20,28},{24,16},{28,20},{1,9},{5... | collective-permute-start | bytes 393224 | tf_op jit(solution)/shard_map/ppermute | solution.py:19
  137.5 10.3 %collective-permute-start.14 = (bf16[64,3584]{1,0:T(8,128)(2,1)S(1)}, bf16[64,3584]{1,0:T(8,128)(2,1)S(1)}, u32[]{:S(2)}, u32[]{:S(2)}) collective-permute-start(bf16[64,3584]{1,0:T(8,128)(2,1)S(1)} %fusion.2.refs_0_), channel_id=1, source_target_pairs={{0,1},{1,0},{2,3},{3,2},{4,5},{5,4},{6,7},{7,6},{8,9},{9,8},{10,11... | collective-permute-start | bytes 1376264 | tf_op jit(solution)/shard_map/ppermute | solution.py:19
  140.8 7.0 %collective-permute-start.16 = (bf16[64,3584]{1,0:T(8,128)(2,1)S(1)}, bf16[64,3584]{1,0:T(8,128)(2,1)S(1)}, u32[]{:S(2)}, u32[]{:S(2)}) collective-permute-start(bf16[64,3584]{1,0:T(8,128)(2,1)S(1)} %collective-permute-done.15.refs_2_), channel_id=1, source_target_pairs={{0,1},{1,0},{2,3},{3,2},{4,5},{5,4},{6,7},{7,6},{8,9},{9,8},{10,11... | collective-permute-start | bytes 1376264 | tf_op jit(solution)/shard_map/ppermute | solution.py:19
  140.9 6.9 %collective-permute-start.31 = (bf16[1,32,1024]{2,1,0:T(8,128)(2,1)S(1)}, bf16[1,32,1024]{2,1,0:T(8,128)(2,1)S(1)}, u32[]{:S(2)}, u32[]{:S(2)}) collective-permute-start(bf16[1,32,1024]{2,1,0:T(8,128)(2,1)S(1)} %fusion.16), channel_id=1, source_target_pairs={{0,16},{4,20},{8,24},{12,28},{16,0},{20,4},{24,8},{28,12},{1,17},{... | collective-permute-start | bytes 196616 | tf_op jit(solution)/shard_map/ppermute | solution.py:19
  142.0 47.1 %collective-permute-start.40 = (bf16[4,32,1024]{2,1,0:T(8,128)(2,1)S(1)}, bf16[4,32,1024]{2,1,0:T(8,128)(2,1)S(1)}, u32[]{:S(2)}, u32[]{:S(2)}) collective-permute-start(bf16[4,32,1024]{2,1,0:T(8,128)(2,1)S(1)} %pad_maximum_fusion.3), channel_id=1, source_target_pairs={{0,4},{4,0},{8,12},{12,8},{16,20},{20,16},{24,28},{28,24},{1,5},{5... | collective-permute-start | bytes 786440 | tf_op jit(solution)/shard_map/ppermute | solution.py:19
  147.8 11.2 %collective-permute-start.32 = (bf16[1,32,1024]{2,1,0:T(8,128)(2,1)S(1)}, bf16[1,32,1024]{2,1,0:T(8,128)(2,1)S(1)}, u32[]{:S(2)}, u32[]{:S(2)}) collective-permute-start(bf16[1,32,1024]{2,1,0:T(8,128)(2,1)S(1)} %fusion.19.refs_0_), channel_id=1, source_target_pairs={{0,16},{4,20},{8,24},{12,28},{16,0},{20,4},{24,8},{28,12},{1,17},{... | collective-permute-start | bytes 196616 | tf_op jit(solution)/shard_map/ppermute | solution.py:19
  152.3 8.9 %collective-permute-start.23 = (bf16[4,32,1024]{2,1,0:T(8,128)(2,1)S(1)}, bf16[4,32,1024]{2,1,0:T(8,128)(2,1)S(1)}, u32[]{:S(2)}, u32[]{:S(2)}) collective-permute-start(bf16[4,32,1024]{2,1,0:T(8,128)(2,1)S(1)} %get-tuple-element.76), channel_id=1, source_target_pairs={{0,4},{4,0},{8,12},{12,8},{16,20},{20,16},{24,28},{28,24},{1,5},{5... | collective-permute-start | bytes 786440 | tf_op jit(solution)/shard_map/ppermute | solution.py:19
  157.4 8.7 %collective-permute-start.17 = (bf16[4,32,1024]{2,1,0:T(8,128)(2,1)S(1)}, bf16[4,32,1024]{2,1,0:T(8,128)(2,1)S(1)}, u32[]{:S(2)}, u32[]{:S(2)}) collective-permute-start(bf16[4,32,1024]{2,1,0:T(8,128)(2,1)S(1)} %get-tuple-element.74), channel_id=1, source_target_pairs={{0,4},{4,0},{8,12},{12,8},{16,20},{20,16},{24,28},{28,24},{1,5},{5... | collective-permute-start | bytes 786440 | tf_op jit(solution)/shard_map/ppermute | solution.py:19
  159.0 25.3 %collective-permute-start.33 = (bf16[2,32,1024]{2,1,0:T(8,128)(2,1)S(1)}, bf16[2,32,1024]{2,1,0:T(8,128)(2,1)S(1)}, u32[]{:S(2)}, u32[]{:S(2)}) collective-permute-start(bf16[2,32,1024]{2,1,0:T(8,128)(2,1)S(1)} %pad_maximum_fusion.7), channel_id=1, source_target_pairs={{0,8},{4,12},{8,0},{12,4},{16,24},{20,28},{24,16},{28,20},{1,9},{5... | collective-permute-start | bytes 393224 | tf_op jit(solution)/shard_map/ppermute | solution.py:19
  161.3 5.8 %collective-permute-start.24 = (bf16[2,32,1024]{2,1,0:T(8,128)(2,1)S(1)}, bf16[2,32,1024]{2,1,0:T(8,128)(2,1)S(1)}, u32[]{:S(2)}, u32[]{:S(2)}) collective-permute-start(bf16[2,32,1024]{2,1,0:T(8,128)(2,1)S(1)} %get-tuple-element.87), channel_id=1, source_target_pairs={{0,8},{4,12},{8,0},{12,4},{16,24},{20,28},{24,16},{28,20},{1,9},{5... | collective-permute-start | bytes 393224 | tf_op jit(solution)/shard_map/ppermute | solution.py:19
  166.1 5.5 %collective-permute-start.18 = (bf16[2,32,1024]{2,1,0:T(8,128)(2,1)S(1)}, bf16[2,32,1024]{2,1,0:T(8,128)(2,1)S(1)}, u32[]{:S(2)}, u32[]{:S(2)}) collective-permute-start(bf16[2,32,1024]{2,1,0:T(8,128)(2,1)S(1)} %get-tuple-element.89), channel_id=1, source_target_pairs={{0,8},{4,12},{8,0},{12,4},{16,24},{20,28},{24,16},{28,20},{1,9},{5... | collective-permute-start | bytes 393224 | tf_op jit(solution)/shard_map/ppermute | solution.py:19
  167.1 7.7 %collective-permute-start.25 = (bf16[1,32,1024]{2,1,0:T(8,128)(2,1)S(1)}, bf16[1,32,1024]{2,1,0:T(8,128)(2,1)S(1)}, u32[]{:S(2)}, u32[]{:S(2)}) collective-permute-start(bf16[1,32,1024]{2,1,0:T(8,128)(2,1)S(1)} %fusion.21), channel_id=1, source_target_pairs={{0,16},{4,20},{8,24},{12,28},{16,0},{20,4},{24,8},{28,12},{1,17},{... | collective-permute-start | bytes 196616 | tf_op jit(solution)/shard_map/ppermute | solution.py:19
  171.7 6.3 %collective-permute-start.19 = (bf16[1,32,1024]{2,1,0:T(8,128)(2,1)S(1)}, bf16[1,32,1024]{2,1,0:T(8,128)(2,1)S(1)}, u32[]{:S(2)}, u32[]{:S(2)}) collective-permute-start(bf16[1,32,1024]{2,1,0:T(8,128)(2,1)S(1)} %fusion.26), channel_id=1, source_target_pairs={{0,16},{4,20},{8,24},{12,28},{16,0},{20,4},{24,8},{28,12},{1,17},{... | collective-permute-start | bytes 196616 | tf_op jit(solution)/shard_map/ppermute | solution.py:19
  174.8 6.6 %collective-permute-start.26 = (bf16[1,32,1024]{2,1,0:T(8,128)(2,1)S(1)}, bf16[1,32,1024]{2,1,0:T(8,128)(2,1)S(1)}, u32[]{:S(2)}, u32[]{:S(2)}) collective-permute-start(bf16[1,32,1024]{2,1,0:T(8,128)(2,1)S(1)} %fusion.24.refs_0_), channel_id=1, source_target_pairs={{0,16},{4,20},{8,24},{12,28},{16,0},{20,4},{24,8},{28,12},{1,17},{... | collective-permute-start | bytes 196616 | tf_op jit(solution)/shard_map/ppermute | solution.py:19
  178.1 5.9 %collective-permute-start.20 = (bf16[1,32,1024]{2,1,0:T(8,128)(2,1)S(1)}, bf16[1,32,1024]{2,1,0:T(8,128)(2,1)S(1)}, u32[]{:S(2)}, u32[]{:S(2)}) collective-permute-start(bf16[1,32,1024]{2,1,0:T(8,128)(2,1)S(1)} %fusion.29.refs_0_), channel_id=1, source_target_pairs={{0,16},{4,20},{8,24},{12,28},{16,0},{20,4},{24,8},{28,12},{1,17},{... | collective-permute-start | bytes 196616 | tf_op jit(solution)/shard_map/ppermute | solution.py:19
  181.5 5.0 %collective-permute-start.27 = (bf16[2,32,1024]{2,1,0:T(8,128)(2,1)S(1)}, bf16[2,32,1024]{2,1,0:T(8,128)(2,1)S(1)}, u32[]{:S(2)}, u32[]{:S(2)}) collective-permute-start(bf16[2,32,1024]{2,1,0:T(8,128)(2,1)S(1)} %pad_maximum_fusion.6), channel_id=1, source_target_pairs={{0,8},{4,12},{8,0},{12,4},{16,24},{20,28},{24,16},{28,20},{1,9},{5... | collective-permute-start | bytes 393224 | tf_op jit(solution)/shard_map/ppermute | solution.py:19
  184.0 5.0 %collective-permute-start.21 = (bf16[2,32,1024]{2,1,0:T(8,128)(2,1)S(1)}, bf16[2,32,1024]{2,1,0:T(8,128)(2,1)S(1)}, u32[]{:S(2)}, u32[]{:S(2)}) collective-permute-start(bf16[2,32,1024]{2,1,0:T(8,128)(2,1)S(1)} %pad_maximum_fusion.5), channel_id=1, source_target_pairs={{0,8},{4,12},{8,0},{12,4},{16,24},{20,28},{24,16},{28,20},{1,9},{5... | collective-permute-start | bytes 393224 | tf_op jit(solution)/shard_map/ppermute | solution.py:19
  184.3 9.3 %collective-permute-start.34 = (bf16[4,32,1024]{2,1,0:T(8,128)(2,1)S(1)}, bf16[4,32,1024]{2,1,0:T(8,128)(2,1)S(1)}, u32[]{:S(2)}, u32[]{:S(2)}) collective-permute-start(bf16[4,32,1024]{2,1,0:T(8,128)(2,1)S(1)} %pad_maximum_fusion.2), channel_id=1, source_target_pairs={{0,4},{4,0},{8,12},{12,8},{16,20},{20,16},{24,28},{28,24},{1,5},{5... | collective-permute-start | bytes 786440 | tf_op jit(solution)/shard_map/ppermute | solution.py:19
  186.5 10.8 %collective-permute-start.28 = (bf16[4,32,1024]{2,1,0:T(8,128)(2,1)S(1)}, bf16[4,32,1024]{2,1,0:T(8,128)(2,1)S(1)}, u32[]{:S(2)}, u32[]{:S(2)}) collective-permute-start(bf16[4,32,1024]{2,1,0:T(8,128)(2,1)S(1)} %pad_maximum_fusion.1), channel_id=1, source_target_pairs={{0,4},{4,0},{8,12},{12,8},{16,20},{20,16},{24,28},{28,24},{1,5},{5... | collective-permute-start | bytes 786440 | tf_op jit(solution)/shard_map/ppermute | solution.py:19
  189.1 11.0 %collective-permute-start.22 = (bf16[4,32,1024]{2,1,0:T(8,128)(2,1)S(1)}, bf16[4,32,1024]{2,1,0:T(8,128)(2,1)S(1)}, u32[]{:S(2)}, u32[]{:S(2)}) collective-permute-start(bf16[4,32,1024]{2,1,0:T(8,128)(2,1)S(1)} %pad_maximum_fusion), channel_id=1, source_target_pairs={{0,4},{4,0},{8,12},{12,8},{16,20},{20,16},{24,28},{28,24},{1,5},{5... | collective-permute-start | bytes 786440 | tf_op jit(solution)/shard_map/ppermute | solution.py:19
  (6 other events, 19.6 us)
